TPU v7x, 128 devices: a whole 4x4x4 slice. The times are simulated.
128 devices in a mesh: table: 8 (over y, core), replica: 16 (over z, x).
Axes of the slice: x: 4, y: 4, z: 4, core: 2. Of those that a mesh axis runs over, the one named last changes fastest.
Arguments:
- hot_ids: int32 [16384, 8], P(('table', 'replica')), may hold values from 0 to 4095
- cold_owner: int32 [16384, 8], P(('table', 'replica')), may hold values from 0 to 127, all different within a row; in each aligned block of 128 rows (0 to 127, 128 to 255, ...) at most 16 rows name the same one
- cold_row: int32 [16384, 8], P(('table', 'replica')), may hold values from 0 to 2047
- cold_exp: int32 [16384, 8], P(('table', 'replica')), may hold values from 0 to 2
- labels: float32 [16384], P(('table', 'replica')), may hold values from 0 to 1
- head_w: float32 [4096], replicated, may hold values from -0.3 to 0.3
- hot_table: float32 [4096, 256], P('table'), may hold values from -2 to 2
- hot_acc: float32 [4096, 256], P('table'), may hold values from 0.01 to 1
- cold_table: float32 [262144, 256], P(('table', 'replica')), may hold values from -2 to 2
- cold_acc: float32 [262144, 256], P(('table', 'replica')), may hold values from 1e-06 to 0.0001
- tower_w: float32 [512, 4096], P(None, 'table'), may hold values from -0.25 to 0.25
- tower_acc: float32 [512, 4096], P(None, 'table'), may hold values from 1 to 100
Outputs:
- new_hot_table: float32 [4096, 256], P('table')
- new_hot_acc: float32 [4096, 256], P('table')
- new_cold_table: float32 [262144, 256], P(('table', 'replica'))
- new_cold_acc: float32 [262144, 256], P(('table', 'replica'))
- new_tower_w: float32 [512, 4096], P(None, 'table')
- new_tower_acc: float32 [512, 4096], P(None, 'table')
Inputs may be any that keep to these rules, and one draw needn't show every extreme that they name: `cold_owner`: the 8 owners of one sample differ; among the samples of one device no owner is named more than 16 times, a bound that some block reaches.
All inputs are finite; a program needn't handle non-finite values.
Results may differ from a plain program's by a relative error of at most 0.0035.
The roundings to bfloat16 on the way count: a program that leaves them out, or rounds other values in their place, can miss the bound.
Values may be sent and summed in bfloat16 or wider, within the bound.
No kernel may reach another device: no remote copies, remote signals or barrier semaphores. Data moves between devices by JAX's collectives and lax.ppermute only.
A program may use at most 128 MiB of HBM per device.

v0:
```python
import jax
import jax.numpy as jnp
from jax import lax
from jax.sharding import PartitionSpec as P

learn_rate = 0.05


def adagrad(param, accum, grad):
    new_accum = accum + grad * grad
    return (param - learn_rate * grad * lax.rsqrt(new_accum), new_accum)


def send_asks(asks):
    return lax.all_to_all(asks, ("table", "replica"), split_axis=0, concat_axis=0, tiled=True)


def send_rows(looked):
    return lax.all_to_all(looked, ("table", "replica"), split_axis=0, concat_axis=0, tiled=True)


def send_grads(outgoing):
    return lax.all_to_all(outgoing, ("table", "replica"), split_axis=0, concat_axis=0, tiled=True)


def on_device(
    hot_ids,
    cold_owner,
    cold_row,
    cold_exp,
    labels,
    head_w,
    hot_table,
    hot_acc,
    cold_table,
    cold_acc,
    tower_w,
    tower_acc,
):
    table_count = lax.axis_size("table")
    replica_count = lax.axis_size("replica")
    devices = table_count * replica_count
    batch, hot_keys = hot_ids.shape
    cold_keys = cold_owner.shape[1]
    width = hot_table.shape[1]
    capacity = max(2, 2 * batch * cold_keys // devices)
    all_hot = lax.all_gather(hot_table.astype(jnp.bfloat16), "table", axis=0, tiled=True)
    hot_pool = jnp.sum(all_hot[hot_ids].astype(jnp.float32), axis=1)
    owner_flat = cold_owner.reshape(-1)
    onehot = (owner_flat[:, None] == jnp.arange(devices, dtype=jnp.int32)[None, :]).astype(
        jnp.int32
    )
    before = jnp.cumsum(onehot, axis=0) - onehot
    slot_ids = jnp.sum(before * onehot, axis=1)
    position = owner_flat * capacity + slot_ids
    asks = jnp.zeros((devices * capacity,), jnp.int32).at[position].set(cold_row.reshape(-1))
    asks = asks.reshape(devices, capacity)
    received = send_asks(asks)
    looked = cold_table.astype(jnp.bfloat16)[received]
    returned = send_rows(looked)
    items = returned.reshape(-1, width)[position].reshape(batch, cold_keys, width)
    scales = jnp.exp2(-cold_exp.astype(jnp.float32))
    cold_pool = jnp.sum(items.astype(jnp.float32) * scales[:, :, None], axis=1)
    features = jnp.concatenate([hot_pool, cold_pool], axis=1).astype(jnp.bfloat16)
    w_half = tower_w.astype(jnp.bfloat16)
    whole_w = lax.all_gather(w_half, "table", axis=1, tiled=True)
    pre = jnp.dot(features, whole_w, preferred_element_type=jnp.float32)
    sig = jax.nn.sigmoid(pre)
    act = pre * sig
    logit = jnp.sum(act * head_w[None, :], axis=1)
    prob = jax.nn.sigmoid(logit)
    dlogit = prob - labels
    dpre = (dlogit[:, None] * head_w[None, :] * sig * (1.0 + pre * (1.0 - sig))).astype(
        jnp.bfloat16
    )
    w_part = lax.dot_general(
        features, dpre, (((0,), (0,)), ((), ())), preferred_element_type=jnp.float32
    )
    dfeat = lax.dot_general(
        dpre, whole_w, (((1,), (1,)), ((), ())), preferred_element_type=jnp.float32
    )
    w_cols = lax.psum_scatter(w_part, "table", scatter_dimension=1, tiled=True)
    dhot = dfeat[:, :width]
    dcold = dfeat[:, width:]
    hot_vals = jnp.broadcast_to(dhot[:, None, :], (batch, hot_keys, width)).reshape(-1, width)
    hot_part = jax.ops.segment_sum(hot_vals, hot_ids.reshape(-1), num_segments=all_hot.shape[0])
    item_grad = (dcold[:, None, :] * scales[:, :, None]).astype(jnp.bfloat16).reshape(-1, width)
    outgoing = jnp.zeros((devices * capacity, width), jnp.bfloat16).at[position].set(item_grad)
    incoming = send_grads(outgoing.reshape(devices, capacity, width))
    cold_grad = jax.ops.segment_sum(
        incoming.reshape(-1, width).astype(jnp.float32),
        received.reshape(-1),
        num_segments=cold_table.shape[0],
    )
    new_cold, new_cold_acc = adagrad(cold_table, cold_acc, cold_grad)
    hot_sum = lax.psum_scatter(hot_part, "table", scatter_dimension=0, tiled=True)
    hot_grad, w_grad = lax.psum((hot_sum, w_cols), "replica")
    new_hot, new_hot_acc = adagrad(hot_table, hot_acc, hot_grad)
    new_w, new_w_acc = adagrad(tower_w, tower_acc, w_grad)
    return (new_hot, new_hot_acc, new_cold, new_cold_acc, new_w, new_w_acc)


def solution(mesh):
    return jax.shard_map(
        on_device,
        mesh=mesh,
        in_specs=(
            P(("table", "replica"), None),
            P(("table", "replica"), None),
            P(("table", "replica"), None),
            P(("table", "replica"), None),
            P(("table", "replica")),
            P(),
            P("table", None),
            P("table", None),
            P(("table", "replica"), None),
            P(("table", "replica"), None),
            P(None, "table"),
            P(None, "table"),
        ),
        out_specs=(
            P("table", None),
            P("table", None),
            P(("table", "replica"), None),
            P(("table", "replica"), None),
            P(None, "table"),
            P(None, "table"),
        ),
        check_vma=False,
    )
```

profile of v0, /device:TPU:2, one launch (start us, length us, event | category | flops | bytes accessed | tf_op | source)
XLA Modules:
  0.0 303.7 jit_solution(12285874707275985331)
XLA Ops:
  7.2 1.8 convert_element_type.42
  9.1 2.1 convert_element_type.50
  12.8 4.3 %scatter_custom_fusion = s32[2048]{0:T(1024)S(1)} fusion(s32[1024]{0:T(1024)S(1)} %bitcast.42, s32[1024]{0:T(1024)S(1)} %reshape.152, s32[]{:T(128)} %constant.11.clone.1), kind=kCustom, calls=%fused_computation.50 | custom fusion | bytes 8196 | tf_op jit(solution)/shard_map/scatter | solution.py:56
  17.8 10.5 %all-to-all-start = ((s32[128,1,16]{2,1,0:T(1,128)}), s32[128,1,16]{2,1,0:T(1,128)S(1)}, u32[]{:S(2)}, u32[]{:S(2)}) async-start(s32[128,1,16]{2,1,0:T(1,128)} %bitcast.6), calls=%async_computation | async-start | bytes 131072 | tf_op jit(solution)/shard_map/all_to_all | solution.py:15
  28.5 8.9 %all-to-all-done = s32[128,1,16]{2,1,0:T(1,128)S(1)} async-done(((s32[128,1,16]{2,1,0:T(1,128)}), s32[128,1,16]{2,1,0:T(1,128)S(1)}, u32[]{:S(2)}, u32[]{:S(2)}) %all-to-all-start) | async-done | bytes 8224 | tf_op jit(solution)/shard_map/all_to_all | solution.py:15
  37.5 9.1 %gather_fusion.1 = bf16[2048,256]{1,0:T(8,128)(2,1)} fusion(bf16[2048,256]{1,0:T(8,128)(2,1)S(1)} %convert_element_type.44, s32[2048]{0:T(1024)S(1)} %broadcast_clamp_fusion), kind=kCustom, calls=%fused_computation.1 | custom fusion | bytes 2105344 | tf_op jit(solution)/shard_map/gather | solution.py:59
  46.6 5.0 %all-to-all-start.1 = ((bf16[128,16,256]{2,1,0:T(8,128)(2,1)}), bf16[128,16,256]{2,1,0:T(8,128)(2,1)S(1)}, u32[]{:S(2)}, u32[]{:S(2)}) async-start(bf16[128,16,256]{2,1,0:T(8,128)(2,1)} %bitcast.37), calls=%async_computation.1 | async-start | bytes 2097152 | tf_op jit(solution)/shard_map/all_to_all | solution.py:19
  52.2 18.9 %all-to-all-done.1 = bf16[128,16,256]{2,1,0:T(8,128)(2,1)S(1)} async-done(((bf16[128,16,256]{2,1,0:T(8,128)(2,1)}), bf16[128,16,256]{2,1,0:T(8,128)(2,1)S(1)}, u32[]{:S(2)}, u32[]{:S(2)}) %all-to-all-start.1) | async-done | bytes 1048608 | tf_op jit(solution)/shard_map/all_to_all | solution.py:19
  71.1 5.0 %gather_fusion.2 = bf16[1024,256]{1,0:T(8,128)(2,1)} fusion(bf16[2048,256]{1,0:T(8,128)(2,1)S(1)} %bitcast.36, s32[1024]{0:T(1024)S(1)} %broadcast_clamp_fusion.1), kind=kCustom, calls=%fused_computation.2 | custom fusion | bytes 1052672 | tf_op jit(solution)/shard_map/gather | solution.py:61
  76.0 1.4 fusion.4
  77.5 5.4 %gather_fusion = bf16[1024,256]{1,0:T(8,128)(2,1)S(1)} fusion(bf16[4096,256]{1,0:T(8,128)(2,1)} %all-gather.3.cloned.1.call-done, s32[1024]{0:T(1024)S(1)} %broadcast_clamp_fusion.2), kind=kCustom, calls=%fused_computation | custom fusion | bytes 1052672 | tf_op jit(solution)/shard_map/gather | solution.py:48
  84.5 3.4 %multiply_reduce_fusion = (f32[128]{0:T(128)S(1)}, f32[128,4096]{1,0:T(8,128)S(1)}) fusion(f32[4096]{0:T(1024)S(1)} %copy-done.10, bf16[512,4096]{1,0:T(8,128)(2,1)} %all-gather.5.cloned.1.call-done, bf16[128,256]{1,0:T(8,128)(2,1)S(1)} %fusion.4, bf16[128,256]{1,0:T(8,128)(2,1)S(1)} %bitcast_reduce_fusion), kind=kOutput, calls=%fused_computation.12 | convolution fusion | flops 540278656 | bytes 6439424 | tf_op jit(solution)/shard_map/dot_general | solution.py:67
  88.0 1.6 fusion.25
  89.6 8.3 %scatter_custom_fusion.1 = f32[4096,256]{1,0:T(8,128)} fusion(s32[1024]{0:T(1024)S(1)} %reshape.158, f32[]{:T(128)} %constant.9.clone.1, f32[128,256]{1,0:T(8,128)S(1)} %get-tuple-element.15), kind=kCustom, calls=%fused_computation.14 | custom fusion | flops 262144 | bytes 4325380 | tf_op jit(solution)/shard_map/scatter-add | solution.py:86
  98.2 6.2 %fusion.19 = f32[512,4096]{1,0:T(8,128)} fusion(bf16[128,256]{1,0:T(8,128)(2,1)S(1)} %fusion.4, bf16[128,256]{1,0:T(8,128)(2,1)S(1)} %bitcast_reduce_fusion, f32[128,4096]{1,0:T(8,128)} %copy-done.12, f32[128]{0:T(128)S(1)} %divide_subtract_fusion, f32[4096]{0:T(1024)S(1)} %copy-done.10), kind=kOutput, calls=%fused_computation.43 | convolution fusion | flops 542375936 | bytes 10633728 | tf_op jit(solution)/shard_map/dot_general | solution.py:76
  104.5 6.5 %scatter_custom_fusion.2 = bf16[2048,256]{1,0:T(8,128)(2,1)} fusion(s32[1024]{0:T(1024)S(1)} %bitcast.44, f32[1024]{0:T(1024)S(1)} %mul.132, f32[128,256]{1,0:T(8,128)S(1)} %get-tuple-element.14, bf16[]{:T(256)} %constant.17.clone.1), kind=kCustom, calls=%fused_computation.24 | custom fusion | flops 524288 | bytes 1183746 | tf_op jit(solution)/shard_map/scatter | solution.py:88
  111.0 8.1 %all-to-all-start.2 = ((bf16[128,16,256]{2,1,0:T(8,128)(2,1)}), bf16[128,16,256]{2,1,0:T(8,128)(2,1)S(1)}, u32[]{:S(2)}, u32[]{:S(2)}) async-start(bf16[128,16,256]{2,1,0:T(8,128)(2,1)} %bitcast.39), calls=%async_computation.3 | async-start | bytes 2097152 | tf_op jit(solution)/shard_map/all_to_all | solution.py:23
  119.1 27.8 %reduce-scatter.3.cloned.1.call-done = f32[512,256]{1,0:T(8,128)} async-done(((f32[4096,256]{1,0:T(8,128)}), f32[512,256]{1,0:T(8,128)}) %reduce-scatter.3.cloned.1.call-update) | async-done | bytes 524304 | tf_op jit(solution)/shard_map/reduce_scatter | solution.py:96
  147.0 53.7 %reduce-scatter.5.cloned.1.call-done = f32[512,512]{1,0:T(8,128)} async-done(((f32[512,4096]{1,0:T(8,128)}), f32[512,512]{1,0:T(8,128)}) %reduce-scatter.5.cloned.1.call-update) | async-done | bytes 1048592 | tf_op jit(solution)/shard_map/reduce_scatter | solution.py:82
  202.1 13.0 %scatter_custom_fusion.3 = f32[2048,256]{1,0:T(8,128)} fusion(s32[2048]{0:T(1024)S(1)} %reshape.174, bf16[2048,256]{1,0:T(8,128)(2,1)S(1)} %bitcast.38, f32[]{:T(128)} %constant.9.clone.1), kind=kCustom, calls=%fused_computation.7 | custom fusion | flops 1048576 | bytes 3145732 | tf_op jit(solution)/shard_map/scatter-add | solution.py:90
  215.1 4.7 %multiply_subtract_fusion = (f32[2048,256]{1,0:T(8,128)}, f32[2048,256]{1,0:T(8,128)}) fusion(f32[2048,256]{1,0:T(8,128)S(1)} %copy-done, f32[2048,256]{1,0:T(8,128)} %scatter_custom_fusion.3, f32[2048,256]{1,0:T(8,128)} %param.21), kind=kLoop, calls=%fused_computation.9 | loop fusion | flops 2621440 | bytes 10485760 | tf_op jit(solution)/shard_map/sub | solution.py:11
  219.9 72.3 %all-reduce.3.cloned.1.call-done = (f32[512,256]{1,0:T(8,128)}, f32[512,512]{1,0:T(8,128)}) async-done(((f32[512,256]{1,0:T(8,128)}, f32[512,512]{1,0:T(8,128)}), (f32[512,256]{1,0:T(8,128)}, f32[512,512]{1,0:T(8,128)})) %all-reduce.3.cloned.1.call-update) | async-done | bytes 1572880 | tf_op jit(solution)/shard_map/psum | solution.py:97
  292.2 2.1 multiply_subtract_fusion.2
  294.3 2.9 multiply_subtract_fusion.1
  (77 shorter events, 6.6 us)
Async XLA Ops:
  7.2 4.0 %copy-start.5 = (s32[128,8]{0,1:T(8,128)S(1)}, s32[128,8]{0,1:T(8,128)}, u32[]{:S(2)}) copy-start(s32[128,8]{0,1:T(8,128)} %param.13) | copy-start | bytes 12292
  7.2 70.3 %all-gather.3.cloned.1.call-start = ((), (), s32[]{:S(2)}) async-start(), calls=%async_computation.5 | async-start | bytes 2359296 | tf_op jit(solution)/shard_map/all_gather | solution.py:47
  9.0 75.5 %all-gather.5.cloned.1.call-start = ((), (), s32[]{:S(2)}) async-start(), calls=%async_computation.6 | async-start | bytes 4718592 | tf_op jit(solution)/shard_map/all_gather | solution.py:66
  11.2 1.1 copy-start.7
  11.2 17.2 %copy-start = (f32[2048,256]{1,0:T(8,128)S(1)}, f32[2048,256]{1,0:T(8,128)}, u32[]{:S(2)}) copy-start(f32[2048,256]{1,0:T(8,128)} %param.20) | copy-start | bytes 6291460
  17.8 19.6 %all-to-all-start = ((s32[128,1,16]{2,1,0:T(1,128)}), s32[128,1,16]{2,1,0:T(1,128)S(1)}, u32[]{:S(2)}, u32[]{:S(2)}) async-start(s32[128,1,16]{2,1,0:T(1,128)} %bitcast.6), calls=%async_computation | async-start | bytes 131072 | tf_op jit(solution)/shard_map/all_to_all | solution.py:15
  46.6 5.1 %copy-start.6 = (s32[128,8]{0,1:T(8,128)S(1)}, s32[128,8]{0,1:T(8,128)}, u32[]{:S(2)}) copy-start(s32[128,8]{0,1:T(8,128)} %param.12) | copy-start | bytes 12292
  46.6 5.3 %copy-start.8 = (s32[128,8]{0,1:T(8,128)S(1)}, s32[128,8]{0,1:T(8,128)}, u32[]{:S(2)}) copy-start(s32[128,8]{0,1:T(8,128)} %param.15) | copy-start | bytes 12292
  46.6 24.5 %all-to-all-start.1 = ((bf16[128,16,256]{2,1,0:T(8,128)(2,1)}), bf16[128,16,256]{2,1,0:T(8,128)(2,1)S(1)}, u32[]{:S(2)}, u32[]{:S(2)}) async-start(bf16[128,16,256]{2,1,0:T(8,128)(2,1)} %bitcast.37), calls=%async_computation.1 | async-start | bytes 2097152 | tf_op jit(solution)/shard_map/all_to_all | solution.py:19
  51.6 95.4 %reduce-scatter.3.cloned.1.call-start = ((), (), s32[]{:S(2)}) async-start(), calls=%async_computation.7 | async-start | bytes 4718592 | tf_op jit(solution)/shard_map/reduce_scatter | solution.py:96
  77.5 7.0 %copy-start.10 = (f32[4096]{0:T(1024)S(1)}, f32[4096]{0:T(1024)}, u32[]{:S(2)}) copy-start(f32[4096]{0:T(1024)} %param.17) | copy-start | bytes 49156
  83.3 4.7 %copy-start.11 = (f32[128]{0:T(128)S(1)}, f32[128]{0:T(128)}, u32[]{:S(2)}) copy-start(f32[128]{0:T(128)} %param.16) | copy-start | bytes 1540
  84.5 3.5 %copy-start.9 = (bf16[512,4096]{1,0:T(8,128)(2,1)S(1)}, bf16[512,4096]{1,0:T(8,128)(2,1)}, u32[]{:S(2)}) copy-start(bf16[512,4096]{1,0:T(8,128)(2,1)} %all-gather.5.cloned.1.call-done) | copy-start | bytes 12582916
  88.0 1.6 copy-start.12
  97.9 102.7 %reduce-scatter.5.cloned.1.call-start = ((), (), s32[]{:S(2)}) async-start(), calls=%async_computation.8 | async-start | bytes 9437184 | tf_op jit(solution)/shard_map/reduce_scatter | solution.py:82
  111.0 91.1 %all-to-all-start.2 = ((bf16[128,16,256]{2,1,0:T(8,128)(2,1)}), bf16[128,16,256]{2,1,0:T(8,128)(2,1)S(1)}, u32[]{:S(2)}, u32[]{:S(2)}) async-start(bf16[128,16,256]{2,1,0:T(8,128)(2,1)} %bitcast.39), calls=%async_computation.3 | async-start | bytes 2097152 | tf_op jit(solution)/shard_map/all_to_all | solution.py:23
  119.1 173.1 %all-reduce.3.cloned.1.call-start = ((), (), s32[]{:S(2)}) async-start(), calls=%async_computation.9 | async-start | bytes 3145728 | tf_op jit(solution)/shard_map/psum | solution.py:97
  215.1 77.1 %copy-start.2 = (f32[512,256]{1,0:T(8,128)S(1)}, f32[512,256]{1,0:T(8,128)}, u32[]{:S(2)}) copy-start(f32[512,256]{1,0:T(8,128)} %param.18) | copy-start | bytes 1572868
  215.1 77.1 %copy-start.4 = (f32[512,256]{1,0:T(8,128)S(1)}, f32[512,256]{1,0:T(8,128)}, u32[]{:S(2)}) copy-start(f32[512,256]{1,0:T(8,128)} %param.19) | copy-start | bytes 1572868
  219.9 74.5 %copy-start.1 = (f32[512,512]{1,0:T(8,128)S(1)}, f32[512,512]{1,0:T(8,128)}, u32[]{:S(2)}) copy-start(f32[512,512]{1,0:T(8,128)} %param.22) | copy-start | bytes 3145732
  219.9 74.5 %copy-start.3 = (f32[512,512]{1,0:T(8,128)S(1)}, f32[512,512]{1,0:T(8,128)}, u32[]{:S(2)}) copy-start(f32[512,512]{1,0:T(8,128)} %param.23) | copy-start | bytes 3145732
Sparse Core Ops, SparseCore 0:
  10.3 28.0 all-gather.2
  40.7 43.7 all-gather.4
  98.0 48.8 reduce-scatter.2
  149.2 51.3 reduce-scatter.4
  203.9 88.2 all-reduce.2
where the time goes:
time: 305 us; the launch traced here: 304 us
  waiting for transfers between devices  183 us (60%)
  other arithmetic  44.8 us (15%)
  local copies, waits for them, and re-layouts  26.7 us (9%)
  starting transfers between devices  24 us (8%)
  between operations  14.1 us (5%)
  matrix products  11.2 us (4%)
    psum x1, waiting for transfers between devices, on_device(): hot_grad, w_grad = lax.psum((hot_sum, w_cols), 'replica')  72.3 us
    reduce_scatter x1, waiting for transfers between devices, on_device(): w_cols = lax.psum_scatter(w_part, 'table', scatter_dimension=1, tiled=True)  53.7 us
    reduce_scatter x1, waiting for transfers between devices, on_device(): lax.psum_scatter(hot_part, 'table', scatter_dimension=0, tiled=True)  27.8 us
    all_to_all x1, waiting for transfers between devices, send_rows(): lax.all_to_all(looked, ('table', 'replica'), split_axis=0, concat_axis=0,...  18.9 us
    scatter-add x1, other arithmetic, on_device(): jax.ops.segment_sum(incoming.reshape(-1, width).astype(jnp.float32), rece...  13 us
    all_to_all x1, starting transfers between devices, send_asks(): lax.all_to_all(asks, ('table', 'replica'), split_axis=0, concat_axis=0, t...  10.5 us
    sub x3, other arithmetic, adagrad(): return (param - learn_rate * grad * lax.rsqrt(new_accum), new_accum)  9.75 us
    gather x1, local copies, waits for them, and re-layouts, on_device(): looked = cold_table.astype(jnp.bfloat16)[received]  9.05 us
  transfers between devices with their start and end apart: 8, of which 6 were waited for; matrix products, arithmetic and copies ran while one was open for 20% of the time, Pallas kernels for 0%

commit v1 on v0

v1 whole, which is shorter than its diff:
```python
import jax
import jax.numpy as jnp
from jax import lax
from jax.experimental import pallas as pl
from jax.experimental.pallas import tpu as pltpu
from jax.sharding import PartitionSpec as P

learn_rate = 0.05
bf16 = jnp.bfloat16
f32 = jnp.float32
i32 = jnp.int32
ALL = ("table", "replica")
VM = pl.BlockSpec(memory_space=pltpu.VMEM)
PARAMS = pltpu.CompilerParams(vmem_limit_bytes=48 * 1024 * 1024)


def adagrad(param, accum, grad):
    new_accum = accum + grad * grad
    return (param - learn_rate * grad * lax.rsqrt(new_accum), new_accum)


def iota(shape, axis):
    return lax.broadcasted_iota(i32, shape, axis)


def route_kernel(own_ref, row_ref, exp_ref, asks_ref, place_ref, scale_ref):
    keys, batch = own_ref.shape
    devices, capacity = asks_ref.shape
    owners = iota((devices, batch), 0)
    named = jnp.zeros((devices, batch), f32)
    rows = jnp.zeros((devices, batch), f32)
    scales = jnp.zeros((devices, batch), f32)
    expo = exp_ref[...]
    scale = jnp.where(expo == 0, 1.0, jnp.where(expo == 1, 0.5, 0.25))
    row = row_ref[...].astype(f32)
    own = own_ref[...]
    for k in range(keys):
        hit = own[k : k + 1, :] == owners
        named = jnp.where(hit, 1.0, named)
        rows = jnp.where(hit, row[k : k + 1, :], rows)
        scales = jnp.where(hit, scale[k : k + 1, :], scales)
    earlier = (iota((batch, batch), 0) < iota((batch, batch), 1)).astype(bf16)
    before = jnp.dot(named.astype(bf16), earlier, preferred_element_type=f32)
    place = jnp.where(named > 0, before + 1.0, 0.0)
    place_ref[...] = place
    scale_ref[...] = scales
    lanes = iota((devices, capacity), 1)
    asks = jnp.zeros((devices, capacity), f32)
    for s in range(capacity):
        col = jnp.sum(jnp.where(place == s + 1.0, rows, 0.0), axis=1, keepdims=True)
        asks = jnp.where(lanes == s, col, asks)
    asks_ref[...] = asks.astype(i32)


def route(own, row, expo, devices, capacity):
    batch = own.shape[1]
    return pl.pallas_call(
        route_kernel,
        out_shape=(
            jax.ShapeDtypeStruct((devices, capacity), i32),
            jax.ShapeDtypeStruct((devices, batch), f32),
            jax.ShapeDtypeStruct((devices, batch), f32),
        ),
        in_specs=[VM] * 3,
        out_specs=(VM,) * 3,
        compiler_params=PARAMS,
        name="route",
    )(own, row, expo)


def spread_kernel(place_ref, scale_ref, out_ref):
    devices, batch = place_ref.shape
    capacity = out_ref.shape[0] // devices
    full = (devices, capacity, batch)
    slots = (iota(full, 1) + 1).astype(f32)
    place = jnp.broadcast_to(place_ref[...][:, None, :], full)
    scale = jnp.broadcast_to(scale_ref[...][:, None, :], full)
    out = jnp.where(place == slots, scale, 0.0)
    out_ref[...] = out.reshape(devices * capacity, batch).astype(bf16)


def spread(place, scale, capacity):
    devices, batch = place.shape
    return pl.pallas_call(
        spread_kernel,
        out_shape=jax.ShapeDtypeStruct((devices * capacity, batch), bf16),
        in_specs=[VM] * 2,
        out_specs=VM,
        compiler_params=PARAMS,
        name="spread",
    )(place, scale)


def lookup_kernel(asked_ref, table_ref, out_ref):
    devices, capacity = asked_ref.shape
    slots, width = out_ref.shape
    rows = table_ref.shape[0]
    full = (devices, capacity, capacity)
    wide = jnp.broadcast_to(asked_ref[...].astype(f32)[:, None, :], full)
    kept = jnp.where(iota(full, 1) == iota(full, 2), wide, 0.0).reshape(slots, capacity)
    col = jnp.sum(kept, axis=1, keepdims=True).astype(i32)
    step = 256
    for at in range(0, slots, step):
        hit = col[at : at + step] == iota((step, rows), 1)
        onehot = jnp.where(hit, 1.0, 0.0).astype(bf16)
        got = jnp.dot(onehot, table_ref[...], preferred_element_type=f32)
        out_ref[at : at + step, :] = got.astype(bf16)


def lookup(asked, table):
    devices, capacity = asked.shape
    return pl.pallas_call(
        lookup_kernel,
        out_shape=jax.ShapeDtypeStruct((devices * capacity, table.shape[1]), bf16),
        in_specs=[VM] * 2,
        out_specs=VM,
        compiler_params=PARAMS,
        name="lookup",
    )(asked, table)


def contract_rows(a, b):
    return lax.dot_general(a, b, (((0,), (0,)), ((), ())), preferred_element_type=f32)


def tower_kernel(
    feat_ref, w_ref, head_ref, label_ref, ids_ref, spread_ref, out_ref, load_ref, pre_ref, sig_ref
):
    batch, din = feat_ref.shape
    parts, _, part = w_ref.shape
    width = din // 2
    keys = ids_ref.shape[1]
    feat = feat_ref[...]
    logit = jnp.zeros((batch, 1), f32)
    for t in range(parts):
        cols = slice(t * part, (t + 1) * part)
        pre = jnp.dot(feat, w_ref[t], preferred_element_type=f32)
        sig = jax.nn.sigmoid(pre)
        pre_ref[:, cols] = pre
        sig_ref[:, cols] = sig
        logit += jnp.sum(pre * sig * head_ref[:, cols], axis=1, keepdims=True)
    dlogit = jax.nn.sigmoid(logit) - label_ref[...]
    dfeat = jnp.zeros((batch, din), f32)
    for t in range(parts):
        cols = slice(t * part, (t + 1) * part)
        pre = pre_ref[:, cols]
        sig = sig_ref[:, cols]
        dpre = (dlogit * head_ref[:, cols] * sig * (1.0 + pre * (1.0 - sig))).astype(bf16)
        dfeat += lax.dot_general(
            dpre, w_ref[t], (((1,), (1,)), ((), ())), preferred_element_type=f32
        )
    dhot = dfeat[:, :width]
    dcold = dfeat[:, width:].astype(bf16)
    out_ref[...] = jnp.dot(spread_ref[...], dcold, preferred_element_type=f32).astype(bf16)
    hot_hi = dhot.astype(bf16)
    hot_lo = (dhot - hot_hi.astype(f32)).astype(bf16)
    load_ref[:, :din] = feat
    load_ref[:, din : din + width] = hot_hi
    load_ref[:, din + width : din + 2 * width] = hot_lo
    first = dlogit.astype(bf16).astype(f32)
    second = (dlogit - first).astype(bf16).astype(f32)
    third = dlogit - first - second
    lanes = iota((batch, 128), 1)
    extra = jnp.where(lanes == 0, first, 0.0)
    extra = jnp.where(lanes == 1, second, extra)
    extra = jnp.where(lanes == 2, third, extra)
    ids = ids_ref[...]
    high = lax.shift_right_logical(ids, 6)
    low = ids - high * 64
    high = high.astype(f32)
    low = low.astype(f32)
    for k in range(keys):
        extra = jnp.where(lanes == 8 + k, high[:, k : k + 1], extra)
        extra = jnp.where(lanes == 8 + keys + k, low[:, k : k + 1], extra)
    load_ref[:, din + 2 * width :] = extra.astype(bf16)


def tower(feat, w_parts, head, label, ids, spread_mat):
    batch, din = feat.shape
    hidden = w_parts.shape[0] * w_parts.shape[2]
    return pl.pallas_call(
        tower_kernel,
        out_shape=(
            jax.ShapeDtypeStruct((spread_mat.shape[0], din // 2), bf16),
            jax.ShapeDtypeStruct((batch, 2 * din + 128), bf16),
        ),
        in_specs=[VM] * 6,
        out_specs=(VM,) * 2,
        scratch_shapes=[pltpu.VMEM((batch, hidden), f32), pltpu.VMEM((batch, hidden), f32)],
        compiler_params=PARAMS,
        name="tower",
    )(feat, w_parts, head, label, ids, spread_mat)


def columns_kernel(keys, base_ref, load_ref, w_ref, head_ref, out_ref):
    samples = load_ref.shape[0]
    din, part = w_ref.shape
    width = din // 2
    rows = out_ref.shape[0]
    feat = load_ref[:, :din]
    extra = load_ref[:, 2 * din :].astype(f32)
    dlogit = extra[:, 0:1] + extra[:, 1:2] + extra[:, 2:3]
    pre = jnp.dot(feat, w_ref[...], preferred_element_type=f32)
    sig = jax.nn.sigmoid(pre)
    dpre = (dlogit * head_ref[...] * sig * (1.0 + pre * (1.0 - sig))).astype(bf16)
    out_ref[:, :part] = contract_rows(feat, dpre).astype(bf16)
    lanes = (iota((samples, rows), 1) + base_ref[0]).astype(f32)
    counts = jnp.zeros((samples, rows), f32)
    for k in range(keys):
        ids = extra[:, 8 + k : 9 + k] * 64.0 + extra[:, 8 + keys + k : 9 + keys + k]
        counts += jnp.where(ids == lanes, 1.0, 0.0)
    counts = counts.astype(bf16)
    hot = contract_rows(counts, load_ref[:, din : din + width])
    hot += contract_rows(counts, load_ref[:, din + width : 2 * din])
    out_ref[:, part:] = hot.astype(bf16)


def columns(load, w_half, head, base, keys, rows):
    din, part = w_half.shape
    return pl.pallas_call(
        lambda *refs: columns_kernel(keys, *refs),
        out_shape=jax.ShapeDtypeStruct((rows, part + din // 2), bf16),
        in_specs=[pl.BlockSpec(memory_space=pltpu.SMEM)] + [VM] * 3,
        out_specs=VM,
        compiler_params=PARAMS,
        name="columns",
    )(base, load, w_half, head)


def cold_kernel(asked_ref, grads_ref, table_ref, acc_ref, new_ref, new_acc_ref):
    step, width = table_ref.shape
    slots = grads_ref.shape[0]
    rows = iota((step, slots), 0) + pl.program_id(0) * step
    onehot = jnp.where(asked_ref[...] == rows, 1.0, 0.0).astype(bf16)
    grad = jnp.dot(onehot, grads_ref[...], preferred_element_type=f32)
    param, acc = adagrad(table_ref[...], acc_ref[...], grad)
    new_ref[...] = param
    new_acc_ref[...] = acc


def cold_update(asked, grads, table, acc):
    rows, width = table.shape
    slots = grads.shape[0]
    step = 256
    block = pl.BlockSpec((step, width), lambda i: (i, 0))
    return pl.pallas_call(
        cold_kernel,
        grid=(rows // step,),
        out_shape=(jax.ShapeDtypeStruct(table.shape, f32),) * 2,
        in_specs=[
            pl.BlockSpec((1, slots), lambda i: (0, 0)),
            pl.BlockSpec((slots, width), lambda i: (0, 0)),
            block,
            block,
        ],
        out_specs=(block, block),
        compiler_params=PARAMS,
        name="cold_update",
    )(asked, grads, table, acc)


def on_device(
    hot_ids,
    cold_owner,
    cold_row,
    cold_exp,
    labels,
    head_w,
    hot_table,
    hot_acc,
    cold_table,
    cold_acc,
    tower_w,
    tower_acc,
):
    devices = lax.axis_size("table") * lax.axis_size("replica")
    replicas = lax.axis_size("replica")
    me = lax.axis_index("table")
    batch, keys = hot_ids.shape
    hot_rows, width = hot_table.shape
    part = tower_w.shape[1]
    capacity = max(2, 2 * batch * cold_owner.shape[1] // devices)
    w_half = tower_w.astype(bf16)
    w_parts = lax.all_gather(w_half, "table", axis=0)
    all_hot = lax.all_gather(hot_table.astype(bf16), "table", axis=0, tiled=True)

    asks, place, scale = route(cold_owner.T, cold_row.T, cold_exp.T, devices, capacity)
    asked = lax.all_to_all(asks, ALL, split_axis=0, concat_axis=0, tiled=True)
    spread_mat = spread(place, scale, capacity)
    looked = lookup(asked, cold_table.astype(bf16))
    returned = lax.all_to_all(
        looked.reshape(devices, capacity, width), ALL, split_axis=0, concat_axis=0, tiled=True
    ).reshape(-1, width)

    counts = jnp.sum(
        (hot_ids[:, :, None] == jnp.arange(all_hot.shape[0], dtype=i32)[None, None, :]).astype(f32),
        axis=1,
    ).astype(bf16)
    hot_pool = jnp.dot(counts, all_hot, preferred_element_type=f32)
    cold_pool = contract_rows(spread_mat, returned)
    feat = jnp.concatenate([hot_pool, cold_pool], axis=1).astype(bf16)
    outgoing, load = tower(
        feat, w_parts, head_w[None, :], labels[:, None], hot_ids, spread_mat
    )
    loads = lax.all_gather(load, "table", axis=0, tiled=True)
    incoming = lax.all_to_all(
        outgoing.reshape(devices, capacity, width), ALL, split_axis=0, concat_axis=0, tiled=True
    ).reshape(-1, width)

    head_part = lax.dynamic_slice(head_w, (me * part,), (part,))[None, :]
    base = (me * hot_rows).astype(i32)[None]
    partial = columns(loads, w_half, head_part, base, keys, hot_rows)
    terms = lax.all_to_all(partial, "replica", split_axis=0, concat_axis=0, tiled=True)
    piece = jnp.sum(terms.reshape(replicas, -1, part + width).astype(f32), axis=0)
    copies = jnp.broadcast_to(piece[None], (replicas,) + piece.shape)
    grads = lax.all_to_all(copies, "replica", split_axis=0, concat_axis=0, tiled=True)
    grads = grads.reshape(hot_rows, part + width)

    new_cold, new_cold_acc = cold_update(asked.reshape(1, -1), incoming, cold_table, cold_acc)
    new_hot, new_hot_acc = adagrad(hot_table, hot_acc, grads[:, part:])
    new_w, new_w_acc = adagrad(tower_w, tower_acc, grads[:, :part])
    return (new_hot, new_hot_acc, new_cold, new_cold_acc, new_w, new_w_acc)


def solution(mesh):
    split = P(ALL, None)
    return jax.shard_map(
        on_device,
        mesh=mesh,
        in_specs=(
            split,
            split,
            split,
            split,
            P(ALL),
            P(),
            P("table", None),
            P("table", None),
            split,
            split,
            P(None, "table"),
            P(None, "table"),
        ),
        out_specs=(
            P("table", None),
            P("table", None),
            split,
            split,
            P(None, "table"),
            P(None, "table"),
        ),
        check_vma=False,
    )
```

time: 305 us -> 202 us (0.66)
  waiting for transfers between devices: 183 us -> 84.6 us
  other arithmetic: 44.8 us -> 20.8 us
  blocking collectives: 0 us -> 20.7 us
  Pallas kernels: 0 us -> 18.6 us
  local copies, waits for them, and re-layouts: 26.7 us -> 8.13 us
  matrix products: 11.2 us -> 4.04 us
  starting transfers between devices: 24 us -> 27.9 us
    reduce_scatter x2 -> x0, waiting for transfers between devices: 81.5 us -> none  [the longest x1 53.7 us: on_device(): w_cols = lax.psum_scatter(w_part, 'table', scatter_dimension=1, tiled=True)]
    psum x1 -> x0, waiting for transfers between devices: 72.3 us -> none  [on_device(): hot_grad, w_grad = lax.psum((hot_sum, w_cols), 'replica')]
    all_gather x2 -> x3, waiting for transfers between devices: 1.25 us -> 35.6 us  [the longest x1 25.2 us: on_device(): loads = lax.all_gather(load, 'table', axis=0, tiled=True)]
    scatter-add x2 -> x0, other arithmetic: 21.3 us -> none  [the longest x1 13 us: on_device(): jax.ops.segment_sum(incoming.reshape(-1, width).astype(jnp.float32), rece...]
    all_to_all x3 -> x4, waiting for transfers between devices: 27.8 us -> 48.9 us  [the longest x1 17.6 us: on_device(): lax.all_to_all(outgoing.reshape(devices, capacity, width), ALL, split_axi...]
    all_to_all x0 -> x1, blocking collectives: none -> 20.7 us  [on_device(): lax.all_to_all(partial, 'replica', split_axis=0, concat_axis=0, tiled=True)]
    gather x3 -> x0, local copies, waits for them, and re-layouts: 19.4 us -> none  [the longest x1 9.05 us: on_device(): looked = cold_table.astype(jnp.bfloat16)[received]]
    pallas_call x0 -> x6, Pallas kernels: none -> 18.6 us  [the longest x1 5.39 us: cold_update(): pl.pallas_call(cold_kernel, grid=(rows // step,), out_shape=(jax.ShapeDty...]
  transfers between devices with their start and end apart: 8 -> 7, of which waited for: 6 -> 6; matrix products, arithmetic and copies ran while one was open for 20% -> 9% of each run, Pallas kernels for 0% -> 5%
where the time goes in v1:
time: 202 us; the launch traced here: 199 us
  waiting for transfers between devices  84.6 us (42%)
  starting transfers between devices  27.9 us (14%)
  other arithmetic  20.8 us (10%)
  blocking collectives  20.7 us (10%)
  Pallas kernels  18.6 us (9%)
  between operations  14 us (7%)
  local copies, waits for them, and re-layouts  8.13 us (4%)
  matrix products  4.04 us (2%)
    all_gather x1, waiting for transfers between devices, on_device(): loads = lax.all_gather(load, 'table', axis=0, tiled=True)  25.2 us
    all_to_all x1, blocking collectives, on_device(): lax.all_to_all(partial, 'replica', split_axis=0, concat_axis=0, tiled=True)  20.7 us
    all_to_all x1, waiting for transfers between devices, on_device(): lax.all_to_all(outgoing.reshape(devices, capacity, width), ALL, split_axi...  17.6 us
    all_to_all x1, waiting for transfers between devices, on_device(): lax.all_to_all(copies, 'replica', split_axis=0, concat_axis=0, tiled=True)  13.4 us
    all_to_all x1, starting transfers between devices, on_device(): asked = lax.all_to_all(asks, ALL, split_axis=0, concat_axis=0, tiled=True)  10.5 us
    all_gather x1, waiting for transfers between devices, on_device(): w_parts = lax.all_gather(w_half, 'table', axis=0)  10.4 us
    all_to_all x1, waiting for transfers between devices, on_device(): lax.all_to_all(looked.reshape(devices, capacity, width), ALL, split_axis=...  9.03 us
    reduce_sum x1, other arithmetic, on_device(): jnp.sum((hot_ids[:, :, None] == jnp.arange(all_hot.shape[0], dtype=i32)[N...  8.93 us
  transfers between devices with their start and end apart: 7, of which 6 were waited for; matrix products, arithmetic and copies ran while one was open for 9% of the time, Pallas kernels for 5%

profile of v1, /device:TPU:2, one launch (start us, length us, event | category | flops | bytes accessed | tf_op | source)
XLA Modules:
  0.0 198.7 jit_solution(6646843723365896676)
XLA Ops:
  7.3 1.9 convert_element_type.21
  9.2 2.1 %convert_element_type.23.refs_2_ = bf16[512,512]{1,0:T(8,128)(2,1)} convert(f32[512,512]{1,0:T(8,128)} %param.22) | non-fusion elementwise | flops 262144 | bytes 1572864 | tf_op jit(solution)/shard_map/convert_element_type | solution.py:283
  12.5 10.5 %all-to-all-start = ((s32[128,1,16]{2,1,0:T(1,128)}), s32[128,1,16]{2,1,0:T(1,128)S(1)}, u32[]{:S(2)}, u32[]{:S(2)}) async-start(s32[128,1,16]{2,1,0:T(1,128)} %bitcast.5), calls=%async_computation | async-start | bytes 131072 | tf_op jit(solution)/shard_map/all_to_all | solution.py:288
  23.2 8.9 %all-to-all-done = s32[128,1,16]{2,1,0:T(1,128)S(1)} async-done(((s32[128,1,16]{2,1,0:T(1,128)}), s32[128,1,16]{2,1,0:T(1,128)S(1)}, u32[]{:S(2)}, u32[]{:S(2)}) %all-to-all-start) | async-done | bytes 8224 | tf_op jit(solution)/shard_map/all_to_all | solution.py:288
  32.1 2.4 %lookup.1 = bf16[2048,256]{1,0:T(8,128)(2,1)S(1)} custom-call(s32[128,16]{1,0:T(8,128)S(1)} %bitcast.26, bf16[2048,256]{1,0:T(8,128)(2,1)S(1)} %convert_element_type.22.table_ref), custom_call_target="tpu_custom_call" | custom-call | tf_op jit(solution)/shard_map/lookup/pallas_call | solution.py:112
  35.5 5.9 %all-to-all-start.1 = ((bf16[128,16,256]{2,1,0:T(8,128)(2,1)}), bf16[128,16,256]{2,1,0:T(8,128)(2,1)}, u32[]{:S(2)}, u32[]{:S(2)}) async-start(bf16[128,16,256]{2,1,0:T(8,128)(2,1)} %bitcast.23), calls=%async_computation.1 | async-start | bytes 2097152 | tf_op jit(solution)/shard_map/all_to_all | solution.py:291
  42.0 8.9 %convert_reduce_fusion = bf16[128,4096]{1,0:T(8,128)(2,1)} fusion(s32[128,8]{1,0:T(8,128)S(1)} %copy.28.ids_ref), kind=kLoop, calls=%fused_computation | loop fusion | flops 12058624 | bytes 1052672 | tf_op jit(solution)/shard_map/reduce_sum | solution.py:295
  51.0 9.0 %all-to-all-done.1 = bf16[128,16,256]{2,1,0:T(8,128)(2,1)} async-done(((bf16[128,16,256]{2,1,0:T(8,128)(2,1)}), bf16[128,16,256]{2,1,0:T(8,128)(2,1)}, u32[]{:S(2)}, u32[]{:S(2)}) %all-to-all-start.1) | async-done | bytes 1048608 | tf_op jit(solution)/shard_map/all_to_all | solution.py:291
  60.0 1.6 convolution_convert_fusion.1
  61.6 2.4 %convolution_convert_fusion = bf16[128,256]{1,0:T(8,128)(2,1)S(1)} fusion(bf16[4096,256]{1,0:T(8,128)(2,1)} %all-gather.5.cloned.1.call-done, bf16[128,4096]{1,0:T(8,128)(2,1)} %convert_reduce_fusion), kind=kOutput, calls=%fused_computation.3 | convolution fusion | flops 268468224 | bytes 3211264 | tf_op jit(solution)/shard_map/dot_general | solution.py:299
  64.1 10.4 %all-gather.9.cloned.1.call-done = bf16[4096,512]{1,0:T(8,128)(2,1)} async-done(((bf16[512,512]{1,0:T(8,128)(2,1)}), bf16[4096,512]{1,0:T(8,128)(2,1)}) %all-gather.9.cloned.1.call-update) | async-done | bytes 4194320 | tf_op jit(solution)/shard_map/all_gather | solution.py:284
  74.5 5.2 %tower.1 = (bf16[2048,256]{1,0:T(8,128)(2,1)S(1)}, bf16[128,1152]{1,0:T(8,128)(2,1)S(1)}) custom-call(bf16[128,512]{1,0:T(8,128)(2,1)S(1)} %pad_maximum_fusion.feat_ref, bf16[8,512,512]{2,1,0:T(8,128)(2,1)} %bitcast.32, f32[1,4096]{1,0:T(1,128)S(1)} %bitcast.27, f32[128,1]{1,0:T(8,128)S(1)} %copy.30.label_ref, s32[128,8]{1,0:T(8,128)S(1)} %copy.28.ids_ref, ...), custom_call_target="tpu_custom_call" | custom-call | tf_op jit(solution)/shard_map/tower/pallas_call | solution.py:181
  81.5 25.2 %all-gather.7.cloned.1.call-done.refs_1_ = bf16[1024,1152]{1,0:T(8,128)(2,1)} async-done(((bf16[128,1152]{1,0:T(8,128)(2,1)}), bf16[1024,1152]{1,0:T(8,128)(2,1)}) %all-gather.7.cloned.1.call-update) | async-done | bytes 2359312 | tf_op jit(solution)/shard_map/all_gather | solution.py:305
  106.7 1.7 copy-done.3
  108.3 4.3 %columns.1 = bf16[512,768]{1,0:T(8,128)(2,1)S(1)} custom-call(s32[1]{0:T(128)} %bitcast.refs_0_, bf16[1024,1152]{1,0:T(8,128)(2,1)S(1)} %copy-done.3, bf16[512,512]{1,0:T(8,128)(2,1)S(1)} %copy-done.1, f32[1,512]{1,0:T(1,128)S(1)} %bitcast.28), custom_call_target="tpu_custom_call" | custom-call | tf_op jit(solution)/shard_map/columns/pallas_call | solution.py:220
  112.6 20.7 %all_to_all.35 = bf16[16,32,768]{2,1,0:T(8,128)(2,1)} all-to-all(bf16[16,32,768]{2,1,0:T(8,128)(2,1)S(1)} %bitcast.24), channel_id=1, replica_groups=mesh['table'=8,'replica'=16] {'replica'}, dimensions={0} | all-to-all | bytes 1572864 | tf_op jit(solution)/shard_map/all_to_all | solution.py:313
  133.3 5.7 %all-to-all-start.4 = ((bf16[128,16,256]{2,1,0:T(8,128)(2,1)}), bf16[128,16,256]{2,1,0:T(8,128)(2,1)S(1)}, u32[]{:S(2)}, u32[]{:S(2)}) async-start(bf16[128,16,256]{2,1,0:T(8,128)(2,1)} %bitcast.25), calls=%async_computation.4 | async-start | bytes 2097152 | tf_op jit(solution)/shard_map/all_to_all | solution.py:306
  140.3 17.6 %all-to-all-done.4 = bf16[128,16,256]{2,1,0:T(8,128)(2,1)S(1)} async-done(((bf16[128,16,256]{2,1,0:T(8,128)(2,1)}), bf16[128,16,256]{2,1,0:T(8,128)(2,1)S(1)}, u32[]{:S(2)}, u32[]{:S(2)}) %all-to-all-start.4) | async-done | bytes 1048608 | tf_op jit(solution)/shard_map/all_to_all | solution.py:306
  159.2 5.5 %all-to-all-start.3 = ((f32[16,32,768]{2,1,0:T(8,128)}), f32[16,32,768]{2,1,0:T(8,128)}, u32[]{:S(2)}, u32[]{:S(2)}) async-start(f32[16,32,768]{2,1,0:T(8,128)} %broadcast_in_dim.24), calls=%async_computation.3 | async-start | bytes 3145728 | tf_op jit(solution)/shard_map/all_to_all | solution.py:316
  166.1 1.6 copy-done.4
  167.7 5.4 %cold_update.1 = (f32[2048,256]{1,0:T(8,128)}, f32[2048,256]{1,0:T(8,128)}) custom-call(s32[1,2048]{1,0:T(1,128)S(1)} %reshape.42.asked_ref, bf16[2048,256]{1,0:T(8,128)(2,1)S(1)} %bitcast.22, f32[2048,256]{1,0:T(8,128)S(1)} %copy-done, f32[2048,256]{1,0:T(8,128)S(1)} %copy-done.4), custom_call_target="tpu_custom_call" | custom-call | tf_op jit(solution)/shard_map/cold_update/pallas_call | solution.py:246
  173.0 13.4 %all-to-all-done.3 = f32[16,32,768]{2,1,0:T(8,128)} async-done(((f32[16,32,768]{2,1,0:T(8,128)}), f32[16,32,768]{2,1,0:T(8,128)}, u32[]{:S(2)}, u32[]{:S(2)}) %all-to-all-start.3) | async-done | bytes 1572896 | tf_op jit(solution)/shard_map/all_to_all | solution.py:316
  186.5 3.6 %multiply_subtract_fusion = (f32[512,512]{1,0:T(8,128)}, f32[512,512]{1,0:T(8,128)}) fusion(f32[512,512]{1,0:T(8,128)} %param.22, f32[512,768]{1,0:T(8,128)} %bitcast.14, f32[512,512]{1,0:T(8,128)} %param.23), kind=kLoop, calls=%fused_computation.5 | loop fusion | flops 1310720 | bytes 5242880 | tf_op jit(solution)/shard_map/sub | solution.py:19
  190.1 2.1 %multiply_subtract_fusion.1 = (f32[512,256]{1,0:T(8,128)}, f32[512,256]{1,0:T(8,128)}) fusion(f32[512,256]{1,0:T(8,128)S(1)} %copy-done.11, f32[512,768]{1,0:T(8,128)} %bitcast.14, f32[512,256]{1,0:T(8,128)S(1)} %copy-done.12), kind=kLoop, calls=%fused_computation.8 | loop fusion | flops 655360 | bytes 2621440 | tf_op jit(solution)/shard_map/sub | solution.py:19
  (47 shorter events, 8.7 us)
Async XLA Ops:
  7.2 4.2 %copy-start.8 = (s32[128,8]{0,1:T(8,128)S(1)}, s32[128,8]{0,1:T(8,128)}, u32[]{:S(2)}) copy-start(s32[128,8]{0,1:T(8,128)} %param.13) | copy-start | bytes 12292
  7.2 4.2 %copy-start.9 = (s32[128,8]{0,1:T(8,128)S(1)}, s32[128,8]{0,1:T(8,128)}, u32[]{:S(2)}) copy-start(s32[128,8]{0,1:T(8,128)} %param.14) | copy-start | bytes 12292
  7.2 4.2 %copy-start.10 = (s32[128,8]{0,1:T(8,128)S(1)}, s32[128,8]{0,1:T(8,128)}, u32[]{:S(2)}) copy-start(s32[128,8]{0,1:T(8,128)} %param.15) | copy-start | bytes 12292
  7.2 15.9 %copy-start = (f32[2048,256]{1,0:T(8,128)S(1)}, f32[2048,256]{1,0:T(8,128)}, u32[]{:S(2)}) copy-start(f32[2048,256]{1,0:T(8,128)} %table_ref.1) | copy-start | bytes 6291460
  7.2 54.4 %all-gather.5.cloned.1.call-start = ((), (), s32[]{:S(2)}) async-start(), calls=%async_computation.5 | async-start | bytes 2359296 | tf_op jit(solution)/shard_map/all_gather | solution.py:285
  9.2 65.3 %all-gather.9.cloned.1.call-start = ((), (), s32[]{:S(2)}) async-start(), calls=%async_computation.7 | async-start | bytes 4718592 | tf_op jit(solution)/shard_map/all_gather | solution.py:284
  12.5 19.6 %all-to-all-start = ((s32[128,1,16]{2,1,0:T(1,128)}), s32[128,1,16]{2,1,0:T(1,128)S(1)}, u32[]{:S(2)}, u32[]{:S(2)}) async-start(s32[128,1,16]{2,1,0:T(1,128)} %bitcast.5), calls=%async_computation | async-start | bytes 131072 | tf_op jit(solution)/shard_map/all_to_all | solution.py:288
  32.1 9.5 %copy-start.13 = (s32[128,8]{0,1:T(8,128)S(1)}, s32[128,8]{0,1:T(8,128)}, u32[]{:S(2)}) copy-start(s32[128,8]{0,1:T(8,128)} %param.12) | copy-start | bytes 12292
  32.1 9.6 %copy-start.14 = (f32[128]{0:T(128)S(1)}, f32[128]{0:T(128)}, u32[]{:S(2)}) copy-start(f32[128]{0:T(128)} %param.16) | copy-start | bytes 1540
  34.5 1.0 copy-start.2
  35.5 24.5 %all-to-all-start.1 = ((bf16[128,16,256]{2,1,0:T(8,128)(2,1)}), bf16[128,16,256]{2,1,0:T(8,128)(2,1)}, u32[]{:S(2)}, u32[]{:S(2)}) async-start(bf16[128,16,256]{2,1,0:T(8,128)(2,1)} %bitcast.23), calls=%async_computation.1 | async-start | bytes 2097152 | tf_op jit(solution)/shard_map/all_to_all | solution.py:291
  41.4 65.3 %all-gather.7.cloned.1.call-start = ((), (), s32[]{:S(2)}) async-start(), calls=%async_computation.6 | async-start | bytes 2654208 | tf_op jit(solution)/shard_map/all_gather | solution.py:305
  61.6 12.9 %copy-start.7 = (f32[4096]{0:T(1024)S(1)}, f32[4096]{0:T(1024)}, u32[]{:S(2)}) copy-start(f32[4096]{0:T(1024)} %param.17) | copy-start | bytes 49156
  74.5 32.2 %copy-start.1 = (bf16[512,512]{1,0:T(8,128)(2,1)S(1)}, bf16[512,512]{1,0:T(8,128)(2,1)}, u32[]{:S(2)}) copy-start(bf16[512,512]{1,0:T(8,128)(2,1)} %convert_element_type.23.refs_2_) | copy-start | bytes 1572868
  79.7 1.0 copy-start.5
  80.7 0.7 copy-start.6
  106.7 1.7 copy-start.3
  133.3 24.5 %all-to-all-start.4 = ((bf16[128,16,256]{2,1,0:T(8,128)(2,1)}), bf16[128,16,256]{2,1,0:T(8,128)(2,1)S(1)}, u32[]{:S(2)}, u32[]{:S(2)}) async-start(bf16[128,16,256]{2,1,0:T(8,128)(2,1)} %bitcast.25), calls=%async_computation.4 | async-start | bytes 2097152 | tf_op jit(solution)/shard_map/all_to_all | solution.py:306
  159.2 27.3 %all-to-all-start.3 = ((f32[16,32,768]{2,1,0:T(8,128)}), f32[16,32,768]{2,1,0:T(8,128)}, u32[]{:S(2)}, u32[]{:S(2)}) async-start(f32[16,32,768]{2,1,0:T(8,128)} %broadcast_in_dim.24), calls=%async_computation.3 | async-start | bytes 3145728 | tf_op jit(solution)/shard_map/all_to_all | solution.py:316
  166.1 1.6 copy-start.4
  186.5 3.6 %copy-start.11 = (f32[512,256]{1,0:T(8,128)S(1)}, f32[512,256]{1,0:T(8,128)}, u32[]{:S(2)}) copy-start(f32[512,256]{1,0:T(8,128)} %param.18) | copy-start | bytes 1572868
  186.5 3.6 %copy-start.12 = (f32[512,256]{1,0:T(8,128)S(1)}, f32[512,256]{1,0:T(8,128)}, u32[]{:S(2)}) copy-start(f32[512,256]{1,0:T(8,128)} %param.19) | copy-start | bytes 1572868
Sparse Core Ops, SparseCore 0:
  10.3 28.1 all-gather.4
  40.9 33.5 all-gather.8
  81.5 25.1 all-gather.6

commit v2 on v1

v2 whole, which is shorter than its diff:
```python
import functools
import math

import jax
import jax.numpy as jnp
from jax import lax
from jax.experimental import pallas as pl
from jax.experimental.pallas import tpu as pltpu
from jax.sharding import PartitionSpec as P

learn_rate = 0.05
bf16 = jnp.bfloat16
f32 = jnp.float32
i32 = jnp.int32
ALL = ("y", "core", "z", "x")
TABLE = ("y", "core")
VM = pl.BlockSpec(memory_space=pltpu.VMEM)
HBM = pl.BlockSpec(memory_space=pltpu.HBM)
MIB = 1024 * 1024
PARAMS = pltpu.CompilerParams(vmem_limit_bytes=24 * MIB)
ALONE = pltpu.CompilerParams(vmem_limit_bytes=60 * MIB)


def adagrad(param, accum, grad):
    new_accum = accum + grad * grad
    return (param - learn_rate * grad * lax.rsqrt(new_accum), new_accum)


def cost(us):
    return pl.CostEstimate(flops=int(us * 1e9), bytes_accessed=int(us * 3e6), transcendentals=0)


def iota(shape, axis):
    return lax.broadcasted_iota(i32, shape, axis)


def route_kernel(
    own_hbm,
    row_hbm,
    exp_hbm,
    hot_hbm,
    w_hbm,
    asks_ref,
    place_ref,
    scale_ref,
    half_ref,
    quarter_ref,
    own_ref,
    row_ref,
    exp_ref,
    hot_ref,
    w_ref,
    sems,
):
    pairs = (
        (own_hbm, own_ref),
        (row_hbm, row_ref),
        (exp_hbm, exp_ref),
        (hot_hbm, hot_ref),
        (w_hbm, w_ref),
    )
    copies = [pltpu.make_async_copy(a, b, sems.at[n]) for n, (a, b) in enumerate(pairs)]
    for copy in copies:
        copy.start()
    for copy in copies[:3]:
        copy.wait()
    keys, batch = own_ref.shape
    devices, capacity = asks_ref.shape
    owners = iota((devices, batch), 0)
    named = jnp.zeros((devices, batch), f32)
    rows = jnp.zeros((devices, batch), f32)
    scales = jnp.zeros((devices, batch), f32)
    expo = exp_ref[...]
    scale = jnp.where(expo == 0, 1.0, jnp.where(expo == 1, 0.5, 0.25))
    row = row_ref[...].astype(f32)
    own = own_ref[...]
    for k in range(keys):
        hit = own[k : k + 1, :] == owners
        named = jnp.where(hit, 1.0, named)
        rows = jnp.where(hit, row[k : k + 1, :], rows)
        scales = jnp.where(hit, scale[k : k + 1, :], scales)
    earlier = (iota((batch, batch), 0) < iota((batch, batch), 1)).astype(bf16)
    before = jnp.dot(named.astype(bf16), earlier, preferred_element_type=f32)
    place = jnp.where(named > 0, before + 1.0, 0.0)
    place_ref[...] = place
    scale_ref[...] = scales
    lanes = iota((devices, capacity), 1)
    asks = jnp.zeros((devices, capacity), f32)
    for s in range(capacity):
        col = jnp.sum(jnp.where(place == s + 1.0, rows, 0.0), axis=1, keepdims=True)
        asks = jnp.where(lanes == s, col, asks)
    asks_ref[...] = asks.astype(i32)
    din, rows_hot, width = w_ref.shape[0], hot_ref.shape[0] // 2, hot_ref.shape[1]
    copies[3].wait()
    half_ref[din:, :width] = hot_ref[:rows_hot, :].astype(bf16)
    half_ref[din:, width:] = hot_ref[rows_hot:, :].astype(bf16)
    copies[4].wait()
    half_ref[:din, :] = w_ref[...].astype(bf16)
    for which, axis in ((0, "x"), (1, "z")):
        at = lax.axis_index(axis)
        for first, count, to in ((0, din // 8, 0), (din, rows_hot // 8, din // 8)):
            start = pl.multiple_of(first + which * 4 * count + at * count, count)
            to += which * (din + rows_hot) // 8
            quarter_ref[to : to + count, :] = half_ref[pl.ds(start, count), :]


def route(own, row, expo, hot, w, devices, capacity):
    batch = own.shape[1]
    return pl.pallas_call(
        route_kernel,
        out_shape=(
            jax.ShapeDtypeStruct((devices, capacity), i32),
            jax.ShapeDtypeStruct((devices, batch), f32),
            jax.ShapeDtypeStruct((devices, batch), f32),
            jax.ShapeDtypeStruct((w.shape[0] + hot.shape[0] // 2, w.shape[1]), bf16),
            jax.ShapeDtypeStruct((w.shape[0] // 4 + hot.shape[0] // 8, w.shape[1]), bf16),
        ),
        in_specs=[HBM] * 5,
        out_specs=(VM,) * 5,
        scratch_shapes=[
            pltpu.VMEM(own.shape, i32),
            pltpu.VMEM(row.shape, i32),
            pltpu.VMEM(expo.shape, i32),
            pltpu.VMEM(hot.shape, f32),
            pltpu.VMEM(w.shape, f32),
            pltpu.SemaphoreType.DMA((5,)),
        ],
        compiler_params=ALONE,
        cost_estimate=cost(2),
        name="route",
    )(own, row, expo, hot, w)


def spread_kernel(place_ref, scale_ref, out_hbm, out_ref, sem):
    devices, batch = place_ref.shape
    capacity = out_ref.shape[0] // devices
    full = (devices, capacity, batch)
    slots = (iota(full, 1) + 1).astype(f32)
    place = jnp.broadcast_to(place_ref[...][:, None, :], full)
    scale = jnp.broadcast_to(scale_ref[...][:, None, :], full)
    out = jnp.where(place == slots, scale, 0.0)
    out_ref[...] = out.reshape(devices * capacity, batch).astype(bf16)
    copy = pltpu.make_async_copy(out_ref, out_hbm, sem)
    copy.start()
    copy.wait()


def spread(place, scale, capacity):
    devices, batch = place.shape
    shape = (devices * capacity, batch)
    return pl.pallas_call(
        spread_kernel,
        out_shape=jax.ShapeDtypeStruct(shape, bf16),
        in_specs=[VM] * 2,
        out_specs=HBM,
        scratch_shapes=[pltpu.VMEM(shape, bf16), pltpu.SemaphoreType.DMA],
        compiler_params=ALONE,
        cost_estimate=cost(1),
        name="spread",
    )(place, scale)


def lookup_kernel(asked_ref, table_hbm, out_hbm, table_ref, half_ref, out_ref, in_sems, sems):
    devices, capacity = asked_ref.shape
    slots, width = out_ref.shape
    rows = table_ref.shape[0]
    parts = in_sems.shape[0]
    loads = []
    for n in range(parts):
        at = slice(n * rows // parts, (n + 1) * rows // parts)
        loads.append(pltpu.make_async_copy(table_hbm.at[at], table_ref.at[at], in_sems.at[n]))
        loads[n].start()
    full = (devices, capacity, capacity)
    wide = jnp.broadcast_to(asked_ref[...].astype(f32)[:, None, :], full)
    kept = jnp.where(iota(full, 1) == iota(full, 2), wide, 0.0).reshape(slots, capacity)
    col = jnp.sum(kept, axis=1, keepdims=True).astype(i32)
    for n in range(parts):
        at = slice(n * rows // parts, (n + 1) * rows // parts)
        loads[n].wait()
        half_ref[at, :] = table_ref[at, :].astype(bf16)
    step = 256
    copies = []
    for at in range(0, slots, step):
        hit = col[at : at + step] == iota((step, rows), 1)
        onehot = jnp.where(hit, 1.0, 0.0).astype(bf16)
        got = jnp.dot(onehot, half_ref[...], preferred_element_type=f32)
        out_ref[at : at + step, :] = got.astype(bf16)
        copies.append(
            pltpu.make_async_copy(
                out_ref.at[at : at + step], out_hbm.at[at : at + step], sems.at[at // step]
            )
        )
        copies[-1].start()
    for copy in copies:
        copy.wait()


def lookup(asked, table):
    devices, capacity = asked.shape
    shape = (devices * capacity, table.shape[1])
    return pl.pallas_call(
        lookup_kernel,
        out_shape=jax.ShapeDtypeStruct(shape, bf16),
        in_specs=[VM, HBM],
        out_specs=HBM,
        scratch_shapes=[
            pltpu.VMEM(table.shape, f32),
            pltpu.VMEM(table.shape, bf16),
            pltpu.VMEM(shape, bf16),
            pltpu.SemaphoreType.DMA((4,)),
            pltpu.SemaphoreType.DMA((shape[0] // 256,)),
        ],
        compiler_params=ALONE,
        cost_estimate=cost(3),
        name="lookup",
    )(asked, table)


def contract_rows(a, b):
    return lax.dot_general(a, b, (((0,), (0,)), ((), ())), preferred_element_type=f32)


def gather_copies(refs, first, buf, sems):
    x, z = lax.axis_index("x"), lax.axis_index("z")
    rows = buf.shape[1]
    count = rows // 8
    lists = []
    n = 0
    for side in range(2):
        half, *others = refs[9 * side : 9 * side + 9]
        piece = others[0].shape[0] // 3
        for dy in range(4):
            t = 4 * side + dy
            moves = [] if dy else [(half, first, 0, rows)]
            for which, at in ((0, x), (1, z)) if dy else ():
                for d in range(4):
                    to = lax.rem(at + d, 4) * count + which * 4 * count
                    start = (dy - 1) * piece + first // 8
                    moves.append((others[4 * which + d], start, to, count))
            copies = []
            for src, start, to, size in moves:
                to_rows = pl.ds(pl.multiple_of(to, count), size)
                copies.append(
                    pltpu.make_async_copy(
                        src.at[start : start + size], buf.at[t, to_rows], sems.at[n]
                    )
                )
                n += 1
            lists.append(copies)
    return lists


COPIES = 2 * (1 + 3 * 8)


def hot_pool_kernel(ids_ref, *refs):
    refs, (out_ref, buf, sems) = refs[:-3], refs[-3:]
    batch, keys = ids_ref.shape
    _, rows, wide = buf.shape
    width = out_ref.shape[1]
    lists = gather_copies(refs, refs[0].shape[0] - rows, buf, sems)
    for copies in lists:
        for copy in copies:
            copy.start()
    y, core = lax.axis_index("y"), lax.axis_index("core")
    ids = ids_ref[...]
    pool = jnp.zeros((batch, width), f32)
    for t, copies in enumerate(lists):
        side = core if t < 4 else 1 - core
        first = (2 * lax.rem(y + t, 4) + side) * 2 * rows
        lanes = iota((batch, 2 * rows), 1) + first
        counts = jnp.zeros((batch, 2 * rows), f32)
        for k in range(keys):
            counts += jnp.where(ids[:, k : k + 1] == lanes, 1.0, 0.0)
        counts = counts.astype(bf16)
        for copy in copies:
            copy.wait()
        pool += jnp.dot(counts[:, :rows], buf[t, :, :width], preferred_element_type=f32)
        pool += jnp.dot(counts[:, rows:], buf[t, :, width:], preferred_element_type=f32)
    out_ref[...] = pool.astype(bf16)


def hot_pooled(ids, pieces, width):
    wide = pieces[0].shape[1]
    rows = pieces[0].shape[0] - 2 * width
    return pl.pallas_call(
        hot_pool_kernel,
        out_shape=jax.ShapeDtypeStruct((ids.shape[0], width), bf16),
        in_specs=[VM] + [HBM] * len(pieces),
        out_specs=VM,
        scratch_shapes=[pltpu.VMEM((8, rows, wide), bf16), pltpu.SemaphoreType.DMA((COPIES,))],
        compiler_params=ALONE,
        cost_estimate=cost(0.1),
        name="hot_pool",
    )(ids, *pieces)


def tower_kernel(
    hot_ref,
    head_ref,
    label_ref,
    ids_ref,
    returned_hbm,
    spread_hbm,
    *refs,
):
    pieces, refs = refs[:-9], refs[-9:]
    dcold_ref, load_ref, pre_ref, sig_ref, returned_ref, spread_ref, w_ref, two, sems = refs
    batch, width = hot_ref.shape
    parts, din, part = w_ref.shape
    keys = ids_ref.shape[1]
    firsts = [
        pltpu.make_async_copy(spread_hbm, spread_ref, two.at[0]),
        pltpu.make_async_copy(returned_hbm, returned_ref, two.at[1]),
    ]
    lists = gather_copies(pieces, 0, w_ref, sems)
    for copies in [firsts] + lists:
        for copy in copies:
            copy.start()
    for copy in firsts:
        copy.wait()
    cold = contract_rows(spread_ref[...], returned_ref[...]).astype(bf16)
    feat = jnp.concatenate([hot_ref[...], cold], axis=1)
    logit = jnp.zeros((batch, 1), f32)
    for t in range(parts):
        cols = slice(t * part, (t + 1) * part)
        for copy in lists[t]:
            copy.wait()
        pre = jnp.dot(feat, w_ref[t], preferred_element_type=f32)
        sig = jax.nn.sigmoid(pre)
        pre_ref[:, cols] = pre
        sig_ref[:, cols] = sig
        logit += jnp.sum(pre * sig * head_ref[:, cols], axis=1, keepdims=True)
    dlogit = jax.nn.sigmoid(logit) - label_ref[...]
    dfeat = jnp.zeros((batch, din), f32)
    for t in range(parts):
        cols = slice(t * part, (t + 1) * part)
        pre = pre_ref[:, cols]
        sig = sig_ref[:, cols]
        dpre = (dlogit * head_ref[:, cols] * sig * (1.0 + pre * (1.0 - sig))).astype(bf16)
        dfeat += lax.dot_general(
            dpre, w_ref[t], (((1,), (1,)), ((), ())), preferred_element_type=f32
        )
    dhot = dfeat[:, :width]
    dcold_ref[...] = dfeat[:, width:].astype(bf16)
    hot_hi = dhot.astype(bf16)
    hot_lo = (dhot - hot_hi.astype(f32)).astype(bf16)
    load_ref[:, :din] = feat
    load_ref[:, din : din + width] = hot_hi
    load_ref[:, din + width : 2 * din] = hot_lo
    first = dlogit.astype(bf16).astype(f32)
    second = (dlogit - first).astype(bf16).astype(f32)
    third = dlogit - first - second
    lanes = iota((batch, 128), 1)
    extra = jnp.where(lanes == 0, first, 0.0)
    extra = jnp.where(lanes == 1, second, extra)
    extra = jnp.where(lanes == 2, third, extra)
    ids = ids_ref[...]
    high = lax.shift_right_logical(ids, 6)
    low = ids - high * 64
    high = high.astype(f32)
    low = low.astype(f32)
    for k in range(keys):
        extra = jnp.where(lanes == 8 + k, high[:, k : k + 1], extra)
        extra = jnp.where(lanes == 8 + keys + k, low[:, k : k + 1], extra)
    load_ref[:, 2 * din :] = extra.astype(bf16)


def tower(hot, returned, spread_mat, head, label, ids, pieces):
    batch, width = hot.shape
    hidden = head.shape[1]
    return pl.pallas_call(
        tower_kernel,
        out_shape=(
            jax.ShapeDtypeStruct((batch, width), bf16),
            jax.ShapeDtypeStruct((batch, 4 * width + 128), bf16),
        ),
        in_specs=[VM] * 4 + [HBM] * (2 + len(pieces)),
        out_specs=(VM, VM),
        scratch_shapes=[
            pltpu.VMEM((batch, hidden), f32),
            pltpu.VMEM((batch, hidden), f32),
            pltpu.VMEM(returned.shape, bf16),
            pltpu.VMEM(spread_mat.shape, bf16),
            pltpu.VMEM((8, 2 * width, hidden // 8), bf16),
            pltpu.SemaphoreType.DMA((2,)),
            pltpu.SemaphoreType.DMA((COPIES,)),
        ],
        compiler_params=ALONE,
        cost_estimate=cost(6),
        name="tower",
    )(hot, head, label, ids, returned, spread_mat, *pieces)


def outgoing_kernel(dcold_ref, spread_hbm, out_hbm, spread_ref, out_ref, sems):
    slots = spread_ref.shape[0]
    step = slots // 4
    loads = []
    for n in range(4):
        at = slice(n * step, (n + 1) * step)
        loads.append(pltpu.make_async_copy(spread_hbm.at[at], spread_ref.at[at], sems.at[n]))
        loads[n].start()
    stores = []
    for n in range(4):
        at = slice(n * step, (n + 1) * step)
        loads[n].wait()
        out = jnp.dot(spread_ref[at, :], dcold_ref[...], preferred_element_type=f32)
        out_ref[at, :] = out.astype(bf16)
        stores.append(pltpu.make_async_copy(out_ref.at[at], out_hbm.at[at], sems.at[4 + n]))
        stores[n].start()
    for store in stores:
        store.wait()


def outgoing_of(dcold, spread_mat):
    shape = (spread_mat.shape[0], dcold.shape[1])
    return pl.pallas_call(
        outgoing_kernel,
        out_shape=jax.ShapeDtypeStruct(shape, bf16),
        in_specs=[VM, HBM],
        out_specs=HBM,
        scratch_shapes=[
            pltpu.VMEM(spread_mat.shape, bf16),
            pltpu.VMEM(shape, bf16),
            pltpu.SemaphoreType.DMA((8,)),
        ],
        compiler_params=ALONE,
        cost_estimate=cost(30),
        name="outgoing",
    )(dcold, spread_mat)


def columns_kernel(keys, head_ref, half_hbm, *refs):
    loads, (out_ref, half_ref, load_ref, sems) = refs[:-4], refs[-4:]
    din, part = half_ref.shape
    rows, width = din, din // 2
    batch = loads[0].shape[0]
    first = pltpu.make_async_copy(half_hbm.at[:din], half_ref, sems.at[len(loads)])
    copies = [
        pltpu.make_async_copy(ref, load_ref.at[pl.ds(n * batch, batch)], sems.at[n])
        for n, ref in enumerate(loads)
    ]
    for copy in [first] + copies:
        copy.start()
    first.wait()
    base = (2 * lax.axis_index("y") + lax.axis_index("core")) * rows
    lanes = (iota((2 * batch, rows), 1) + base).astype(f32)
    tower_grad = jnp.zeros((din, part), f32)
    hot_grad = jnp.zeros((rows, width), f32)
    for n in range(0, len(loads), 2):
        copies[n].wait()
        copies[n + 1].wait()
        at = slice(n * batch, (n + 2) * batch)
        feat = load_ref[at, :din]
        extra = load_ref[at, 2 * din :].astype(f32)
        dlogit = extra[:, 0:1] + extra[:, 1:2] + extra[:, 2:3]
        pre = jnp.dot(feat, half_ref[...], preferred_element_type=f32)
        sig = jax.nn.sigmoid(pre)
        dpre = (dlogit * head_ref[...] * sig * (1.0 + pre * (1.0 - sig))).astype(bf16)
        tower_grad += contract_rows(feat, dpre)
        counts = jnp.zeros((2 * batch, rows), f32)
        for k in range(keys):
            ids = extra[:, 8 + k : 9 + k] * 64.0 + extra[:, 8 + keys + k : 9 + keys + k]
            counts += jnp.where(ids == lanes, 1.0, 0.0)
        counts = counts.astype(bf16)
        hot_grad += contract_rows(counts, load_ref[at, din : din + width])
        hot_grad += contract_rows(counts, load_ref[at, din + width : 2 * din])
    out_ref[:, :part] = tower_grad.astype(bf16)
    out_ref[:, part:] = hot_grad.astype(bf16)


def columns(loads, half, head, keys):
    batch, wide = loads[0].shape
    return pl.pallas_call(
        functools.partial(columns_kernel, keys),
        out_shape=jax.ShapeDtypeStruct((half.shape[1], half.shape[0]), bf16),
        in_specs=[VM] + [HBM] * (1 + len(loads)),
        out_specs=VM,
        scratch_shapes=[
            pltpu.VMEM((half.shape[1], half.shape[1]), bf16),
            pltpu.VMEM((batch * len(loads), wide), bf16),
            pltpu.SemaphoreType.DMA((1 + len(loads),)),
        ],
        compiler_params=ALONE,
        cost_estimate=cost(5),
        name="columns",
    )(head, half, *loads)


def total_kernel(terms_ref, left_ref, right_ref):
    total = terms_ref[0].astype(f32)
    for n in range(1, terms_ref.shape[0]):
        total += terms_ref[n].astype(f32)
    half = left_ref.shape[1]
    left_ref[...] = total[:, :half]
    right_ref[...] = total[:, half:]


def total_of(terms):
    _, rows, wide = terms.shape
    return pl.pallas_call(
        total_kernel,
        out_shape=(jax.ShapeDtypeStruct((rows, wide // 2), f32),) * 2,
        in_specs=[VM],
        out_specs=(VM,) * 2,
        compiler_params=PARAMS,
        cost_estimate=cost(1),
        name="total",
    )(terms)


def lay_kernel(*refs):
    out0, out1 = refs[-2:]
    for axis, parts, out in (("z", refs[:4], out0), ("x", refs[4:8], out1)):
        step = parts[0].shape[0]
        for n, ref in enumerate(parts):
            at = lax.rem(lax.axis_index(axis) + n, 4) * step
            out[pl.ds(pl.multiple_of(at, step), step), :] = ref[...]


def lay(left, right):
    rows, wide = left[0].shape
    return pl.pallas_call(
        lay_kernel,
        out_shape=(jax.ShapeDtypeStruct((4 * rows, wide), f32),) * 2,
        in_specs=[VM] * 8,
        out_specs=(VM,) * 2,
        compiler_params=PARAMS,
        cost_estimate=cost(1),
        name="lay",
    )(*left, *right)


def update_kernel(l0, l1, l2, l3, r0, r1, r2, r3, *refs):
    w_ref, w_acc_ref, hot_ref, hot_acc_ref, nw_ref, nwa_ref, nh_ref, nha_ref, grad_ref = refs
    part = w_ref.shape[1]
    step, half = l0.shape
    piece = step // 4
    i = pl.program_id(0)
    for d, left in enumerate((l0, l1, l2, l3)):

        @pl.when(lax.rem(lax.axis_index("x") + d, 4) == i)
        def _():
            grad_ref[:, :half] = left[...]

    start = pl.multiple_of(i * piece, piece)
    for d, right in enumerate((r0, r1, r2, r3)):
        at = lax.rem(lax.axis_index("z") + d, 4) * piece
        grad_ref[pl.ds(pl.multiple_of(at, piece), piece), half:] = right[pl.ds(start, piece), :]
    nw, nwa = adagrad(w_ref[...], w_acc_ref[...], grad_ref[:, :part])
    nw_ref[...] = nw
    nwa_ref[...] = nwa
    nh, nha = adagrad(hot_ref[...], hot_acc_ref[...], grad_ref[:, part:])
    nh_ref[...] = nh
    nha_ref[...] = nha


def update(left, right, w, w_acc, hot, hot_acc):
    step, half = left[0].shape
    w_block = pl.BlockSpec((step, w.shape[1]), lambda i: (i, 0))
    hot_block = pl.BlockSpec((step, hot.shape[1]), lambda i: (i, 0))
    return pl.pallas_call(
        update_kernel,
        grid=(4,),
        in_specs=[VM] * 8
        + [w_block] * 2
        + [hot_block] * 2,
        out_specs=(w_block, w_block, hot_block, hot_block),
        out_shape=(jax.ShapeDtypeStruct(w.shape, f32),) * 2
        + (jax.ShapeDtypeStruct(hot.shape, f32),) * 2,
        scratch_shapes=[pltpu.VMEM((step, 2 * half), f32)],
        compiler_params=ALONE,
        cost_estimate=cost(4),
        name="update",
    )(*left, *right, w, w_acc, hot, hot_acc)


def cold_kernel(asked_ref, grads_ref, table_ref, acc_ref, new_ref, new_acc_ref):
    step, width = table_ref.shape
    slots = grads_ref.shape[0]
    rows = iota((step, slots), 0) + pl.program_id(0) * step
    onehot = jnp.where(asked_ref[...] == rows, 1.0, 0.0).astype(bf16)
    grad = jnp.dot(onehot, grads_ref[...], preferred_element_type=f32)
    param, acc = adagrad(table_ref[...], acc_ref[...], grad)
    new_ref[...] = param
    new_acc_ref[...] = acc


def cold_update(asked, grads, table, acc):
    rows, width = table.shape
    slots = grads.shape[0]
    step = 256
    block = pl.BlockSpec((step, width), lambda i: (i, 0))
    return pl.pallas_call(
        cold_kernel,
        grid=(rows // step,),
        out_shape=(jax.ShapeDtypeStruct(table.shape, f32),) * 2,
        in_specs=[
            pl.BlockSpec((1, slots), lambda i: (0, 0)),
            pl.BlockSpec((slots, width), lambda i: (0, 0)),
            block,
            block,
        ],
        out_specs=(block, block),
        compiler_params=PARAMS,
        cost_estimate=cost(5),
        name="cold_update",
    )(asked, grads, table, acc)


def along(value, axis, by):
    return lax.ppermute(value, axis, [((i + by) % 4, i) for i in range(4)])


def around(value, axis):
    last, one = along(value, axis, 3), along(value, axis, 1)
    return value, one, along(value, axis, 2), last


def swap(value):
    return lax.ppermute(value, "core", [(0, 1), (1, 0)])


def on_device(
    hot_ids,
    cold_owner,
    cold_row,
    cold_exp,
    labels,
    head_w,
    hot_table,
    hot_acc,
    cold_table,
    cold_acc,
    tower_w,
    tower_acc,
):
    devices = math.prod(lax.axis_size(name) for name in ALL)
    y, core = lax.axis_index("y"), lax.axis_index("core")
    me = 2 * y + core
    batch, keys = hot_ids.shape
    hot_rows, width = hot_table.shape
    part = tower_w.shape[1]
    capacity = max(2, 2 * batch * cold_owner.shape[1] // devices)
    asks, place, scale, half, quarter = route(
        cold_owner.T, cold_row.T, cold_exp.T, hot_table, tower_w, devices, capacity
    )
    asked = lax.all_to_all(asks, ALL, split_axis=0, concat_axis=0, tiled=True)
    spread_mat = spread(place, scale, capacity)
    quarters = tuple(along(quarter, "y", by) for by in (1, 2, 3))
    asked, quarters = lax.optimization_barrier((asked, quarters))
    count = quarter.shape[0] // 2
    by_x = jnp.concatenate([value[:count] for value in quarters])
    by_z = jnp.concatenate([value[count:] for value in quarters])
    looked = lookup(asked, cold_table)
    xs = tuple(along(by_x, "x", by) for by in (1, 2, 3))
    zs = tuple(along(by_z, "z", by) for by in (1, 2, 3))
    returned = lax.all_to_all(
        looked.reshape(devices, capacity, width), ALL, split_axis=0, concat_axis=0, tiled=True
    ).reshape(-1, width)
    pieces = lax.optimization_barrier((half, by_x) + xs + (by_z,) + zs)
    pieces += tuple(swap(value) for value in pieces)
    hot_feat = hot_pooled(hot_ids, pieces, width)
    heads = head_w.reshape(4, 2, part)
    turned = jnp.concatenate([heads, heads])
    turned = lax.dynamic_slice_in_dim(turned, y, 4, 0)
    head = jnp.concatenate(
        [lax.dynamic_slice_in_dim(turned, side, 1, 1).reshape(1, -1) for side in (core, 1 - core)],
        axis=1,
    )
    dcold, load = tower(
        hot_feat, returned, spread_mat, head, labels[:, None], hot_ids, pieces
    )
    loads = around(load, "y")
    outgoing = outgoing_of(dcold, spread_mat)
    incoming = lax.all_to_all(
        outgoing.reshape(devices, capacity, width), ALL, split_axis=0, concat_axis=0, tiled=True
    ).reshape(-1, width)
    loads += tuple(swap(part) for part in loads)
    head_part = lax.dynamic_slice(head_w, (me * part,), (part,))[None, :]
    partial = columns(loads, half, head_part, keys)
    partial, incoming = lax.optimization_barrier((partial, incoming))
    terms = lax.all_to_all(partial, ("x", "z"), split_axis=0, concat_axis=0, tiled=True)
    new_cold = cold_update(asked.reshape(1, -1), incoming, cold_table, cold_acc)
    terms, (new_cold, new_cold_acc) = lax.optimization_barrier((terms, new_cold))
    left, right = total_of(terms.reshape(16, -1, part + width))
    left, right = lay(around(left, "z"), around(right, "x"))
    left, right = around(left, "x"), around(right, "z")
    new_w, new_w_acc, new_hot, new_hot_acc = update(
        left, right, tower_w, tower_acc, hot_table, hot_acc
    )
    return (new_hot, new_hot_acc, new_cold, new_cold_acc, new_w, new_w_acc)


def solution(mesh):
    chips = mesh.devices.reshape(4, 2, 4, 4)
    mesh = jax.sharding.Mesh(chips, ALL)
    split = P(ALL, None)
    rows = P(TABLE, None)
    cols = P(None, TABLE)
    return jax.shard_map(
        on_device,
        mesh=mesh,
        in_specs=(split,) * 4 + (P(ALL), P(), rows, rows, split, split, cols, cols),
        out_specs=(rows, rows, split, split, cols, cols),
        check_vma=False,
    )
```

time: 202 us -> 169 us (0.84); the launches traced: 199 us -> 168 us
  waiting for transfers between devices: 84.6 us -> 31 us
  starting transfers between devices: 27.9 us -> 57 us
  Pallas kernels: 18.6 us -> 46.4 us
  other arithmetic: 20.8 us -> 0.65 us
  between operations: 14 us -> 1.23 us
  local copies, waits for them, and re-layouts: 8.13 us -> 12.7 us
  matrix products: 4.04 us -> 0 us
    all_gather x3 -> x0, waiting for transfers between devices: 35.6 us -> none  [the longest x1 25.2 us: on_device(): loads = lax.all_gather(load, 'table', axis=0, tiled=True)]
    ppermute x0 -> x37, starting transfers between devices: none -> 32.8 us  [the longest x24 29.6 us: along(): return lax.ppermute(value, axis, [((i + by) % 4, i) for i in range(4)])]
    pallas_call x4 -> x9, Pallas kernels: 12.1 us -> 38.5 us  [the longest x1 9.66 us: tower(): pl.pallas_call(tower_kernel, out_shape=(jax.ShapeDtypeStruct((batch, widt...]
    ppermute x0 -> x37, waiting for transfers between devices: none -> 19.9 us  [the longest x24 18.4 us: along(): return lax.ppermute(value, axis, [((i + by) % 4, i) for i in range(4)])]
    all_to_all x2 -> x1, waiting for transfers between devices: 22.4 us -> 3.37 us  [on_device(): lax.all_to_all(partial, ('x', 'z'), split_axis=0, concat_axis=0, tiled=True)]
    all_to_all x1, waiting for transfers between devices: 17.6 us -> 6.27 us  [on_device(): lax.all_to_all(outgoing.reshape(devices, capacity, width), ALL, split_axi...]
    all_to_all x2 -> x1, starting transfers between devices: 16 us -> 4.73 us  [on_device(): lax.all_to_all(partial, ('x', 'z'), split_axis=0, concat_axis=0, tiled=True)]
    reduce_sum x2 -> x0, other arithmetic: 10.2 us -> none  [the longest x1 8.93 us: on_device(): jnp.sum((hot_ids[:, :, None] == jnp.arange(all_hot.shape[0], dtype=i32)[N...]
  transfers between devices with their start and end apart: 7 -> 40, of which waited for: 6 -> 15; matrix products, arithmetic and copies ran while one was open for 9% -> 3% of each run, Pallas kernels for 5% -> 17%
where the time goes in v2:
time: 169 us; the launch traced here: 168 us
  starting transfers between devices  57 us (34%)
  Pallas kernels  46.4 us (27%)
  waiting for transfers between devices  31 us (18%)
  blocking collectives  19.2 us (11%)
  local copies, waits for them, and re-layouts  12.7 us (8%)
    ppermute x24, starting transfers between devices, along(): return lax.ppermute(value, axis, [((i + by) % 4, i) for i in range(4)])  29.6 us
    all_to_all x1, blocking collectives, on_device(): asked = lax.all_to_all(asks, ALL, split_axis=0, concat_axis=0, tiled=True)  19.2 us
    ppermute x24, waiting for transfers between devices, along(): return lax.ppermute(value, axis, [((i + by) % 4, i) for i in range(4)])  18.4 us
    all_to_all x1, starting transfers between devices, on_device(): lax.all_to_all(looked.reshape(devices, capacity, width), ALL, split_axis=...  10.4 us
    unnamed x66, local copies, waits for them, and re-layouts  9.76 us
    pallas_call x1, Pallas kernels, tower(): pl.pallas_call(tower_kernel, out_shape=(jax.ShapeDtypeStruct((batch, widt...  9.66 us
    all_to_all x1, starting transfers between devices, on_device(): lax.all_to_all(outgoing.reshape(devices, capacity, width), ALL, split_axi...  9.1 us
    pallas_call x1, Pallas kernels, columns(): pl.pallas_call(functools.partial(columns_kernel, keys), out_shape=jax.Sha...  7.55 us
  transfers between devices with their start and end apart: 40, of which 15 were waited for; matrix products, arithmetic and copies ran while one was open for 3% of the time, Pallas kernels for 17%

profile of v2, /device:TPU:2, one launch (start us, length us, event | category | flops | bytes accessed | tf_op | source)
XLA Modules:
  0.0 168.1 jit_solution(8419946091179421663)
XLA Ops:
  0.6 2.5 %route.1 = (s32[128,16]{1,0:T(8,128)}, f32[128,128]{1,0:T(8,128)}, f32[128,128]{1,0:T(8,128)}, bf16[768,512]{1,0:T(8,128)(2,1)}, bf16[192,512]{1,0:T(8,128)(2,1)}) custom-call(s32[8,128]{1,0:T(8,128)} %bitcast.30, s32[8,128]{1,0:T(8,128)} %bitcast.31, s32[8,128]{1,0:T(8,128)} %bitcast.32, f32[512,256]{1,0:T(8,128)} %refs_2_.1, f32[512,512]{1,0:T(8,128)} %refs_0_.1), custom_call_target="tpu_custom_call" | custom-call | flops 2000000000 | bytes 6000000 | tf_op jit(solution)/shard_map/route/pallas_call | solution.py:109
  3.1 3.1 %collective-permute-start = (bf16[192,512]{1,0:T(8,128)(2,1)}, bf16[192,512]{1,0:T(8,128)(2,1)S(1)}, u32[]{:S(2)}, u32[]{:S(2)}) collective-permute-start(bf16[192,512]{1,0:T(8,128)(2,1)} %get-tuple-element.43), channel_id=1, source_target_pairs={{32,0},{64,32},{96,64},{0,96},{33,1},{65,33},{97,65},{1,97},{34,2}... | collective-permute-start | bytes 589832 | tf_op jit(solution)/shard_map/ppermute | solution.py:612
  7.8 19.2 %all_to_all.34 = s32[128,1,16]{2,1,0:T(1,128)} all-to-all(s32[128,1,16]{2,1,0:T(1,128)} %bitcast.25), channel_id=1, replica_groups=mesh['y'=4,'core'=2,'z'=4,'x'=4] {'y','core','z','x'}, dimensions={0} | all-to-all | bytes 16384 | tf_op jit(solution)/shard_map/all_to_all | solution.py:648
  27.6 2.3 %collective-permute-start.7 = (bf16[288,512]{1,0:T(8,128)(2,1)S(1)}, bf16[288,512]{1,0:T(8,128)(2,1)S(1)}, u32[]{:S(2)}, u32[]{:S(2)}) collective-permute-start(bf16[288,512]{1,0:T(8,128)(2,1)S(1)} %pad_maximum_fusion.1.refs_5_), channel_id=1, source_target_pairs={{8,0},{12,4},{0,8},{4,12},{9,1},{13,5},{1,9},{5,13},{10,2},{14,6},... | collective-permute-start | bytes 884744 | tf_op jit(solution)/shard_map/ppermute | solution.py:612
  31.7 5.3 %collective-permute-done.6.refs_6_ = bf16[288,512]{1,0:T(8,128)(2,1)S(1)} collective-permute-done((bf16[288,512]{1,0:T(8,128)(2,1)S(1)}, bf16[288,512]{1,0:T(8,128)(2,1)S(1)}, u32[]{:S(2)}, u32[]{:S(2)}) %collective-permute-start.6) | collective-permute-done | bytes 294944 | tf_op jit(solution)/shard_map/ppermute | solution.py:612
  37.1 5.6 %lookup.1 = bf16[2048,256]{1,0:T(8,128)(2,1)} custom-call(s32[128,16]{1,0:T(8,128)} %bitcast.23, f32[2048,256]{1,0:T(8,128)} %table_ref.1), custom_call_target="tpu_custom_call" | custom-call | flops 3000000000 | bytes 9000000 | tf_op jit(solution)/shard_map/lookup/pallas_call | solution.py:201
  42.7 10.4 %all-to-all-start.1 = ((bf16[128,16,256]{2,1,0:T(8,128)(2,1)}), bf16[128,16,256]{2,1,0:T(8,128)(2,1)S(1)}, u32[]{:S(2)}, u32[]{:S(2)}) async-start(bf16[128,16,256]{2,1,0:T(8,128)(2,1)} %bitcast.20), calls=%async_computation.1 | async-start | bytes 2097152 | tf_op jit(solution)/shard_map/all_to_all | solution.py:658
  65.1 5.4 %hot_pool.1.hot_ref = bf16[128,256]{1,0:T(8,128)(2,1)} custom-call(s32[128,8]{1,0:T(8,128)} %copy.25.ids_ref, bf16[768,512]{1,0:T(8,128)(2,1)} %get-tuple-element.47.refs_0_.half_hbm, bf16[288,512]{1,0:T(8,128)(2,1)} %copy-done.5, bf16[288,512]{1,0:T(8,128)(2,1)} %copy-done.12, bf16[288,512]{1,0:T(8,128)(2,1)} %collective-permute-done.4.refs_3_, ...), custom_call_target="tpu_custom_call" | custom-call | flops 100000000 | bytes 300000 | tf_op jit(solution)/shard_map/hot_pool/pallas_call | solution.py:286
  72.8 9.7 %tower.1 = (bf16[128,256]{1,0:T(8,128)(2,1)}, bf16[128,1152]{1,0:T(8,128)(2,1)}) custom-call(bf16[128,256]{1,0:T(8,128)(2,1)} %hot_pool.1.hot_ref, f32[1,4096]{1,0:T(1,128)} %pad_maximum_fusion.2.head_ref, f32[128,1]{1,0:T(8,128)} %copy.26.label_ref, s32[128,8]{1,0:T(8,128)} %copy.25.ids_ref, bf16[2048,256]{1,0:T(8,128)(2,1)} %bitcast.19, ...), custom_call_target="tpu_custom_call" | custom-call | flops 6000000000 | bytes 18000000 | tf_op jit(solution)/shard_map/tower/pallas_call | solution.py:372
  85.6 3.6 %outgoing.1 = bf16[2048,256]{1,0:T(8,128)(2,1)} custom-call(bf16[128,256]{1,0:T(8,128)(2,1)} %get-tuple-element.60.dcold_ref, bf16[2048,128]{1,0:T(8,128)(2,1)} %spread.1.spread_hbm), custom_call_target="tpu_custom_call" | custom-call | flops 30000001024 | bytes 90000000 | tf_op jit(solution)/shard_map/outgoing/pallas_call | solution.py:417
  89.2 9.1 %all-to-all-start.2 = ((bf16[128,16,256]{2,1,0:T(8,128)(2,1)}), bf16[128,16,256]{2,1,0:T(8,128)(2,1)S(1)}, u32[]{:S(2)}, u32[]{:S(2)}) async-start(bf16[128,16,256]{2,1,0:T(8,128)(2,1)} %bitcast.21), calls=%async_computation.2 | async-start | bytes 2097152 | tf_op jit(solution)/shard_map/all_to_all | solution.py:676
  99.1 1.9 %collective-permute-done.20.refs_3_ = bf16[128,1152]{1,0:T(8,128)(2,1)S(1)} collective-permute-done((bf16[128,1152]{1,0:T(8,128)(2,1)}, bf16[128,1152]{1,0:T(8,128)(2,1)S(1)}, u32[]{:S(2)}, u32[]{:S(2)}) %collective-permute-start.20) | collective-permute-done | bytes 294944 | tf_op jit(solution)/shard_map/ppermute | solution.py:612
  103.3 7.5 %columns.1 = bf16[512,768]{1,0:T(8,128)(2,1)} custom-call(f32[1,512]{1,0:T(1,128)} %bitcast.28, bf16[768,512]{1,0:T(8,128)(2,1)} %get-tuple-element.47.refs_0_.half_hbm, bf16[128,1152]{1,0:T(8,128)(2,1)} %get-tuple-element.59.refs_0_, bf16[128,1152]{1,0:T(8,128)(2,1)} %copy-done.20, bf16[128,1152]{1,0:T(8,128)(2,1)} %copy-done.21, ...), custom_call_target="tpu_custom_call" | custom-call | flops 5000000000 | bytes 15000000 | tf_op jit(solution)/shard_map/columns/pallas_call | solution.py:474
  110.9 6.3 %all-to-all-done.2 = bf16[128,16,256]{2,1,0:T(8,128)(2,1)S(1)} async-done(((bf16[128,16,256]{2,1,0:T(8,128)(2,1)}), bf16[128,16,256]{2,1,0:T(8,128)(2,1)S(1)}, u32[]{:S(2)}, u32[]{:S(2)}) %all-to-all-start.2) | async-done | bytes 1048608 | tf_op jit(solution)/shard_map/all_to_all | solution.py:676
  117.1 4.7 %all-to-all-start.3 = ((bf16[16,32,768]{2,1,0:T(8,128)(2,1)}), bf16[16,32,768]{2,1,0:T(8,128)(2,1)S(1)}, u32[]{:S(2)}, u32[]{:S(2)}) async-start(bf16[16,32,768]{2,1,0:T(8,128)(2,1)} %bitcast.22), calls=%async_computation.3 | async-start | bytes 1572864 | tf_op jit(solution)/shard_map/all_to_all | solution.py:683
  125.1 5.4 %cold_update.1 = (f32[2048,256]{1,0:T(8,128)}, f32[2048,256]{1,0:T(8,128)}) custom-call(s32[1,2048]{1,0:T(1,128)S(1)} %reshape.50.asked_ref, bf16[2048,256]{1,0:T(8,128)(2,1)S(1)} %bitcast.18, f32[2048,256]{1,0:T(8,128)S(1)} %copy-done, f32[2048,256]{1,0:T(8,128)S(1)} %copy-done.1), custom_call_target="tpu_custom_call" | custom-call | flops 5000000000 | bytes 15000000 | tf_op jit(solution)/shard_map/cold_update/pallas_call | solution.py:594
  130.5 3.4 %all-to-all-done.3 = bf16[16,32,768]{2,1,0:T(8,128)(2,1)S(1)} async-done(((bf16[16,32,768]{2,1,0:T(8,128)(2,1)}), bf16[16,32,768]{2,1,0:T(8,128)(2,1)S(1)}, u32[]{:S(2)}, u32[]{:S(2)}) %all-to-all-start.3) | async-done | bytes 786464 | tf_op jit(solution)/shard_map/all_to_all | solution.py:683
  142.0 3.5 %collective-permute-done.29.refs_6_ = f32[32,384]{1,0:T(8,128)S(1)} collective-permute-done((f32[32,384]{1,0:T(8,128)S(1)}, f32[32,384]{1,0:T(8,128)S(1)}, u32[]{:S(2)}, u32[]{:S(2)}) %collective-permute-start.29) | collective-permute-done | bytes 49184 | tf_op jit(solution)/shard_map/ppermute | solution.py:612
  147.4 2.4 %collective-permute-start.33 = (f32[128,384]{1,0:T(8,128)S(1)}, f32[128,384]{1,0:T(8,128)S(1)}, u32[]{:S(2)}, u32[]{:S(2)}) collective-permute-start(f32[128,384]{1,0:T(8,128)S(1)} %get-tuple-element.68.l0), channel_id=1, source_target_pairs={{3,0},{0,1},{1,2},{2,3},{7,4},{4,5},{5,6},{6,7},{11,8},{8,9},{9,10... | collective-permute-start | bytes 589832 | tf_op jit(solution)/shard_map/ppermute | solution.py:612
  149.8 3.3 %collective-permute-start.34 = (f32[128,384]{1,0:T(8,128)S(1)}, f32[128,384]{1,0:T(8,128)S(1)}, u32[]{:S(2)}, u32[]{:S(2)}) collective-permute-start(f32[128,384]{1,0:T(8,128)S(1)} %get-tuple-element.69.r0), channel_id=1, source_target_pairs={{4,0},{8,4},{12,8},{0,12},{5,1},{9,5},{13,9},{1,13},{6,2},{10,6},{... | collective-permute-start | bytes 589832 | tf_op jit(solution)/shard_map/ppermute | solution.py:612
  155.4 3.0 %collective-permute-done.34.r1 = f32[128,384]{1,0:T(8,128)S(1)} collective-permute-done((f32[128,384]{1,0:T(8,128)S(1)}, f32[128,384]{1,0:T(8,128)S(1)}, u32[]{:S(2)}, u32[]{:S(2)}) %collective-permute-start.34) | collective-permute-done | bytes 196640 | tf_op jit(solution)/shard_map/ppermute | solution.py:612
  158.5 1.9 %collective-permute-done.35.r2 = f32[128,384]{1,0:T(8,128)S(1)} collective-permute-done((f32[128,384]{1,0:T(8,128)S(1)}, f32[128,384]{1,0:T(8,128)S(1)}, u32[]{:S(2)}, u32[]{:S(2)}) %collective-permute-start.35) | collective-permute-done | bytes 196640 | tf_op jit(solution)/shard_map/ppermute | solution.py:612
  160.4 2.0 %collective-permute-done.36.r3 = f32[128,384]{1,0:T(8,128)S(1)} collective-permute-done((f32[128,384]{1,0:T(8,128)S(1)}, f32[128,384]{1,0:T(8,128)S(1)}, u32[]{:S(2)}, u32[]{:S(2)}) %collective-permute-start.36) | collective-permute-done | bytes 196640 | tf_op jit(solution)/shard_map/ppermute | solution.py:612
  163.1 4.8 %update.1 = (f32[512,512]{1,0:T(8,128)}, f32[512,512]{1,0:T(8,128)}, f32[512,256]{1,0:T(8,128)}, f32[512,256]{1,0:T(8,128)}) custom-call(f32[128,384]{1,0:T(8,128)} %copy-done.2, f32[128,384]{1,0:T(8,128)} %copy-done.26, f32[128,384]{1,0:T(8,128)} %copy-done.27, f32[128,384]{1,0:T(8,128)} %copy-done.28, f32[128,384]{1,0:T(8,128)} %copy-done.3, ...), custom_call_target="tpu_custom_call" | custom-call | flops 4000000000 | bytes 12000000 | tf_op jit(solution)/shard_map/update/pallas_call | solution.py:562
  (145 shorter events, 40.7 us)
Async XLA Ops:
  3.1 23.9 %collective-permute-start = (bf16[192,512]{1,0:T(8,128)(2,1)}, bf16[192,512]{1,0:T(8,128)(2,1)S(1)}, u32[]{:S(2)}, u32[]{:S(2)}) collective-permute-start(bf16[192,512]{1,0:T(8,128)(2,1)} %get-tuple-element.43), channel_id=1, source_target_pairs={{32,0},{64,32},{96,64},{0,96},{33,1},{65,33},{97,65},{1,97},{34,2}... | collective-permute-start | bytes 589832 | tf_op jit(solution)/shard_map/ppermute | solution.py:612
  6.2 20.8 %collective-permute-start.1 = (bf16[192,512]{1,0:T(8,128)(2,1)}, bf16[192,512]{1,0:T(8,128)(2,1)S(1)}, u32[]{:S(2)}, u32[]{:S(2)}) collective-permute-start(bf16[192,512]{1,0:T(8,128)(2,1)} %get-tuple-element.43), channel_id=1, source_target_pairs={{64,0},{96,32},{0,64},{32,96},{65,1},{97,33},{1,65},{33,97},{66,2}... | collective-permute-start | bytes 589832 | tf_op jit(solution)/shard_map/ppermute | solution.py:612
  6.8 20.1 %collective-permute-start.2 = (bf16[192,512]{1,0:T(8,128)(2,1)}, bf16[192,512]{1,0:T(8,128)(2,1)S(1)}, u32[]{:S(2)}, u32[]{:S(2)}) collective-permute-start(bf16[192,512]{1,0:T(8,128)(2,1)} %get-tuple-element.43), channel_id=1, source_target_pairs={{96,0},{0,32},{32,64},{64,96},{97,1},{1,33},{33,65},{65,97},{98,2}... | collective-permute-start | bytes 589832 | tf_op jit(solution)/shard_map/ppermute | solution.py:612
  27.1 10.0 %collective-permute-start.6 = (bf16[288,512]{1,0:T(8,128)(2,1)S(1)}, bf16[288,512]{1,0:T(8,128)(2,1)S(1)}, u32[]{:S(2)}, u32[]{:S(2)}) collective-permute-start(bf16[288,512]{1,0:T(8,128)(2,1)S(1)} %pad_maximum_fusion.1.refs_5_), channel_id=1, source_target_pairs={{4,0},{8,4},{12,8},{0,12},{5,1},{9,5},{13,9},{1,13},{6,2},{10,6},{... | collective-permute-start | bytes 884744 | tf_op jit(solution)/shard_map/ppermute | solution.py:612
  27.6 25.5 %collective-permute-start.7 = (bf16[288,512]{1,0:T(8,128)(2,1)S(1)}, bf16[288,512]{1,0:T(8,128)(2,1)S(1)}, u32[]{:S(2)}, u32[]{:S(2)}) collective-permute-start(bf16[288,512]{1,0:T(8,128)(2,1)S(1)} %pad_maximum_fusion.1.refs_5_), channel_id=1, source_target_pairs={{8,0},{12,4},{0,8},{4,12},{9,1},{13,5},{1,9},{5,13},{10,2},{14,6},... | collective-permute-start | bytes 884744 | tf_op jit(solution)/shard_map/ppermute | solution.py:612
  29.9 23.2 %collective-permute-start.8 = (bf16[288,512]{1,0:T(8,128)(2,1)S(1)}, bf16[288,512]{1,0:T(8,128)(2,1)}, u32[]{:S(2)}, u32[]{:S(2)}) collective-permute-start(bf16[288,512]{1,0:T(8,128)(2,1)S(1)} %pad_maximum_fusion.1.refs_5_), channel_id=1, source_target_pairs={{12,0},{0,4},{4,8},{8,12},{13,1},{1,5},{5,9},{9,13},{14,2},{2,6},{... | collective-permute-start | bytes 884744 | tf_op jit(solution)/shard_map/ppermute | solution.py:612
  29.9 23.2 %collective-permute-start.3 = (bf16[288,512]{1,0:T(8,128)(2,1)S(1)}, bf16[288,512]{1,0:T(8,128)(2,1)S(1)}, u32[]{:S(2)}, u32[]{:S(2)}) collective-permute-start(bf16[288,512]{1,0:T(8,128)(2,1)S(1)} %pad_maximum_fusion.refs_1_), channel_id=1, source_target_pairs={{1,0},{2,1},{3,2},{0,3},{5,4},{6,5},{7,6},{4,7},{9,8},{10,9},{11,1... | collective-permute-start | bytes 884744 | tf_op jit(solution)/shard_map/ppermute | solution.py:612
  31.6 21.6 %collective-permute-start.4 = (bf16[288,512]{1,0:T(8,128)(2,1)S(1)}, bf16[288,512]{1,0:T(8,128)(2,1)}, u32[]{:S(2)}, u32[]{:S(2)}) collective-permute-start(bf16[288,512]{1,0:T(8,128)(2,1)S(1)} %pad_maximum_fusion.refs_1_), channel_id=1, source_target_pairs={{2,0},{3,1},{0,2},{1,3},{6,4},{7,5},{4,6},{5,7},{10,8},{11,9},{8,1... | collective-permute-start | bytes 884744 | tf_op jit(solution)/shard_map/ppermute | solution.py:612
  37.1 16.1 %collective-permute-start.5 = (bf16[288,512]{1,0:T(8,128)(2,1)S(1)}, bf16[288,512]{1,0:T(8,128)(2,1)}, u32[]{:S(2)}, u32[]{:S(2)}) collective-permute-start(bf16[288,512]{1,0:T(8,128)(2,1)S(1)} %pad_maximum_fusion.refs_1_), channel_id=1, source_target_pairs={{3,0},{0,1},{1,2},{2,3},{7,4},{4,5},{5,6},{6,7},{11,8},{8,9},{9,10... | collective-permute-start | bytes 884744 | tf_op jit(solution)/shard_map/ppermute | solution.py:612
  42.7 29.2 %all-to-all-start.1 = ((bf16[128,16,256]{2,1,0:T(8,128)(2,1)}), bf16[128,16,256]{2,1,0:T(8,128)(2,1)S(1)}, u32[]{:S(2)}, u32[]{:S(2)}) async-start(bf16[128,16,256]{2,1,0:T(8,128)(2,1)} %bitcast.20), calls=%async_computation.1 | async-start | bytes 2097152 | tf_op jit(solution)/shard_map/all_to_all | solution.py:658
  53.9 10.3 %collective-permute-start.9 = (bf16[768,512]{1,0:T(8,128)(2,1)S(1)}, bf16[768,512]{1,0:T(8,128)(2,1)S(1)}, u32[]{:S(2)}, u32[]{:S(2)}) collective-permute-start(bf16[768,512]{1,0:T(8,128)(2,1)S(1)} %copy-done.7), channel_id=1, source_target_pairs={{0,16},{16,0},{1,17},{17,1},{2,18},{18,2},{3,19},{19,3},{4,20},{20... | collective-permute-start | bytes 2359304 | tf_op jit(solution)/shard_map/ppermute | solution.py:621
  82.5 16.1 %collective-permute-start.18 = (bf16[128,1152]{1,0:T(8,128)(2,1)}, bf16[128,1152]{1,0:T(8,128)(2,1)S(1)}, u32[]{:S(2)}, u32[]{:S(2)}) collective-permute-start(bf16[128,1152]{1,0:T(8,128)(2,1)} %get-tuple-element.59.refs_0_), channel_id=1, source_target_pairs={{32,0},{64,32},{96,64},{0,96},{33,1},{65,33},{97,65},{1,97},{34,2}... | collective-permute-start | bytes 884744 | tf_op jit(solution)/shard_map/ppermute | solution.py:612
  84.0 15.0 %collective-permute-start.19 = (bf16[128,1152]{1,0:T(8,128)(2,1)}, bf16[128,1152]{1,0:T(8,128)(2,1)S(1)}, u32[]{:S(2)}, u32[]{:S(2)}) collective-permute-start(bf16[128,1152]{1,0:T(8,128)(2,1)} %get-tuple-element.59.refs_0_), channel_id=1, source_target_pairs={{64,0},{96,32},{0,64},{32,96},{65,1},{97,33},{1,65},{33,97},{66,2}... | collective-permute-start | bytes 884744 | tf_op jit(solution)/shard_map/ppermute | solution.py:612
  85.2 15.7 %collective-permute-start.20 = (bf16[128,1152]{1,0:T(8,128)(2,1)}, bf16[128,1152]{1,0:T(8,128)(2,1)S(1)}, u32[]{:S(2)}, u32[]{:S(2)}) collective-permute-start(bf16[128,1152]{1,0:T(8,128)(2,1)} %get-tuple-element.59.refs_0_), channel_id=1, source_target_pairs={{96,0},{0,32},{32,64},{64,96},{97,1},{1,33},{33,65},{65,97},{98,2}... | collective-permute-start | bytes 884744 | tf_op jit(solution)/shard_map/ppermute | solution.py:612
  89.2 27.9 %all-to-all-start.2 = ((bf16[128,16,256]{2,1,0:T(8,128)(2,1)}), bf16[128,16,256]{2,1,0:T(8,128)(2,1)S(1)}, u32[]{:S(2)}, u32[]{:S(2)}) async-start(bf16[128,16,256]{2,1,0:T(8,128)(2,1)} %bitcast.21), calls=%async_computation.2 | async-start | bytes 2097152 | tf_op jit(solution)/shard_map/all_to_all | solution.py:676
  117.1 16.8 %all-to-all-start.3 = ((bf16[16,32,768]{2,1,0:T(8,128)(2,1)}), bf16[16,32,768]{2,1,0:T(8,128)(2,1)S(1)}, u32[]{:S(2)}, u32[]{:S(2)}) async-start(bf16[16,32,768]{2,1,0:T(8,128)(2,1)} %bitcast.22), calls=%async_computation.3 | async-start | bytes 1572864 | tf_op jit(solution)/shard_map/all_to_all | solution.py:683
  134.0 6.1 %collective-permute-start.25 = (f32[32,384]{1,0:T(8,128)S(1)}, f32[32,384]{1,0:T(8,128)S(1)}, u32[]{:S(2)}, u32[]{:S(2)}) collective-permute-start(f32[32,384]{1,0:T(8,128)S(1)} %get-tuple-element.66.refs_0_), channel_id=1, source_target_pairs={{4,0},{8,4},{12,8},{0,12},{5,1},{9,5},{13,9},{1,13},{6,2},{10,6},{... | collective-permute-start | bytes 147464 | tf_op jit(solution)/shard_map/ppermute | solution.py:612
  135.5 6.2 %collective-permute-start.26 = (f32[32,384]{1,0:T(8,128)S(1)}, f32[32,384]{1,0:T(8,128)S(1)}, u32[]{:S(2)}, u32[]{:S(2)}) collective-permute-start(f32[32,384]{1,0:T(8,128)S(1)} %get-tuple-element.66.refs_0_), channel_id=1, source_target_pairs={{8,0},{12,4},{0,8},{4,12},{9,1},{13,5},{1,9},{5,13},{10,2},{14,6},... | collective-permute-start | bytes 147464 | tf_op jit(solution)/shard_map/ppermute | solution.py:612
  145.5 8.1 %collective-permute-start.31 = (f32[128,384]{1,0:T(8,128)S(1)}, f32[128,384]{1,0:T(8,128)S(1)}, u32[]{:S(2)}, u32[]{:S(2)}) collective-permute-start(f32[128,384]{1,0:T(8,128)S(1)} %get-tuple-element.68.l0), channel_id=1, source_target_pairs={{1,0},{2,1},{3,2},{0,3},{5,4},{6,5},{7,6},{4,7},{9,8},{10,9},{11,1... | collective-permute-start | bytes 589832 | tf_op jit(solution)/shard_map/ppermute | solution.py:612
  147.1 7.9 %collective-permute-start.32 = (f32[128,384]{1,0:T(8,128)S(1)}, f32[128,384]{1,0:T(8,128)S(1)}, u32[]{:S(2)}, u32[]{:S(2)}) collective-permute-start(f32[128,384]{1,0:T(8,128)S(1)} %get-tuple-element.68.l0), channel_id=1, source_target_pairs={{2,0},{3,1},{0,2},{1,3},{6,4},{7,5},{4,6},{5,7},{10,8},{11,9},{8,1... | collective-permute-start | bytes 589832 | tf_op jit(solution)/shard_map/ppermute | solution.py:612
  147.4 8.0 %collective-permute-start.33 = (f32[128,384]{1,0:T(8,128)S(1)}, f32[128,384]{1,0:T(8,128)S(1)}, u32[]{:S(2)}, u32[]{:S(2)}) collective-permute-start(f32[128,384]{1,0:T(8,128)S(1)} %get-tuple-element.68.l0), channel_id=1, source_target_pairs={{3,0},{0,1},{1,2},{2,3},{7,4},{4,5},{5,6},{6,7},{11,8},{8,9},{9,10... | collective-permute-start | bytes 589832 | tf_op jit(solution)/shard_map/ppermute | solution.py:612
  149.8 8.7 %collective-permute-start.34 = (f32[128,384]{1,0:T(8,128)S(1)}, f32[128,384]{1,0:T(8,128)S(1)}, u32[]{:S(2)}, u32[]{:S(2)}) collective-permute-start(f32[128,384]{1,0:T(8,128)S(1)} %get-tuple-element.69.r0), channel_id=1, source_target_pairs={{4,0},{8,4},{12,8},{0,12},{5,1},{9,5},{13,9},{1,13},{6,2},{10,6},{... | collective-permute-start | bytes 589832 | tf_op jit(solution)/shard_map/ppermute | solution.py:612
  153.1 7.3 %collective-permute-start.35 = (f32[128,384]{1,0:T(8,128)S(1)}, f32[128,384]{1,0:T(8,128)S(1)}, u32[]{:S(2)}, u32[]{:S(2)}) collective-permute-start(f32[128,384]{1,0:T(8,128)S(1)} %get-tuple-element.69.r0), channel_id=1, source_target_pairs={{8,0},{12,4},{0,8},{4,12},{9,1},{13,5},{1,9},{5,13},{10,2},{14,6},... | collective-permute-start | bytes 589832 | tf_op jit(solution)/shard_map/ppermute | solution.py:612
  153.6 8.8 %collective-permute-start.36 = (f32[128,384]{1,0:T(8,128)S(1)}, f32[128,384]{1,0:T(8,128)S(1)}, u32[]{:S(2)}, u32[]{:S(2)}) collective-permute-start(f32[128,384]{1,0:T(8,128)S(1)} %get-tuple-element.69.r0), channel_id=1, source_target_pairs={{12,0},{0,4},{4,8},{8,12},{13,1},{1,5},{5,9},{9,13},{14,2},{2,6},{... | collective-permute-start | bytes 589832 | tf_op jit(solution)/shard_map/ppermute | solution.py:612
  (48 other events, 277.1 us)

commit v3 on v2

--- a/solution.py
+++ b/solution.py
@@ -18,6 +18,7 @@
 HBM = pl.BlockSpec(memory_space=pltpu.HBM)
 MIB = 1024 * 1024
 PARAMS = pltpu.CompilerParams(vmem_limit_bytes=24 * MIB)
+MOST = pltpu.CompilerParams(vmem_limit_bytes=57 * MIB)
 ALONE = pltpu.CompilerParams(vmem_limit_bytes=60 * MIB)
 
 
@@ -160,30 +161,23 @@
     )(place, scale)
 
 
-def lookup_kernel(asked_ref, table_hbm, out_hbm, table_ref, half_ref, out_ref, in_sems, sems):
+def lookup_kernel(asked_ref, table_hbm, out_hbm, table_ref, out_ref, sem, sems):
     devices, capacity = asked_ref.shape
     slots, width = out_ref.shape
     rows = table_ref.shape[0]
-    parts = in_sems.shape[0]
-    loads = []
-    for n in range(parts):
-        at = slice(n * rows // parts, (n + 1) * rows // parts)
-        loads.append(pltpu.make_async_copy(table_hbm.at[at], table_ref.at[at], in_sems.at[n]))
-        loads[n].start()
+    load = pltpu.make_async_copy(table_hbm, table_ref, sem)
+    load.start()
     full = (devices, capacity, capacity)
     wide = jnp.broadcast_to(asked_ref[...].astype(f32)[:, None, :], full)
     kept = jnp.where(iota(full, 1) == iota(full, 2), wide, 0.0).reshape(slots, capacity)
     col = jnp.sum(kept, axis=1, keepdims=True).astype(i32)
-    for n in range(parts):
-        at = slice(n * rows // parts, (n + 1) * rows // parts)
-        loads[n].wait()
-        half_ref[at, :] = table_ref[at, :].astype(bf16)
+    load.wait()
     step = 256
     copies = []
     for at in range(0, slots, step):
         hit = col[at : at + step] == iota((step, rows), 1)
         onehot = jnp.where(hit, 1.0, 0.0).astype(bf16)
-        got = jnp.dot(onehot, half_ref[...], preferred_element_type=f32)
+        got = jnp.dot(onehot, table_ref[...], preferred_element_type=f32)
         out_ref[at : at + step, :] = got.astype(bf16)
         copies.append(
             pltpu.make_async_copy(
@@ -204,10 +198,9 @@
         in_specs=[VM, HBM],
         out_specs=HBM,
         scratch_shapes=[
-            pltpu.VMEM(table.shape, f32),
             pltpu.VMEM(table.shape, bf16),
             pltpu.VMEM(shape, bf16),
-            pltpu.SemaphoreType.DMA((4,)),
+            pltpu.SemaphoreType.DMA,
             pltpu.SemaphoreType.DMA((shape[0] // 256,)),
         ],
         compiler_params=ALONE,
@@ -222,111 +215,130 @@
 
 def gather_copies(refs, first, buf, sems):
     x, z = lax.axis_index("x"), lax.axis_index("z")
-    rows = buf.shape[1]
+    rows = buf.shape[2]
     count = rows // 8
+    start = first // 8
     lists = []
     n = 0
     for side in range(2):
         half, *others = refs[9 * side : 9 * side + 9]
-        piece = others[0].shape[0] // 3
-        for dy in range(4):
-            t = 4 * side + dy
-            moves = [] if dy else [(half, first, 0, rows)]
-            for which, at in ((0, x), (1, z)) if dy else ():
-                for d in range(4):
-                    to = lax.rem(at + d, 4) * count + which * 4 * count
-                    start = (dy - 1) * piece + first // 8
-                    moves.append((others[4 * which + d], start, to, count))
-            copies = []
-            for src, start, to, size in moves:
-                to_rows = pl.ds(pl.multiple_of(to, count), size)
-                copies.append(
-                    pltpu.make_async_copy(
-                        src.at[start : start + size], buf.at[t, to_rows], sems.at[n]
-                    )
-                )
+        copies = [
+            pltpu.make_async_copy(half.at[first : first + rows], buf.at[side, 0], sems.at[n])
+        ]
+        n += 1
+        for which, at in ((0, x), (1, z)):
+            for d in range(4):
+                to = lax.rem(at + d, 4) * count + which * 4 * count
+                to_rows = pl.ds(pl.multiple_of(to, count), count)
+                src = others[4 * which + d].at[:, start : start + count]
+                dst = buf.at[side, 1:4, to_rows]
+                copies.append(pltpu.make_async_copy(src, dst, sems.at[n]))
                 n += 1
-            lists.append(copies)
+        lists.append(copies)
+    for copies in lists:
+        copies[0].start()
+    for copies in lists:
+        for copy in copies[1:]:
+            copy.start()
     return lists
 
 
-COPIES = 2 * (1 + 3 * 8)
-
-
-def hot_pool_kernel(ids_ref, *refs):
-    refs, (out_ref, buf, sems) = refs[:-3], refs[-3:]
+COPIES = 2 * 9
+
+
+def count_kernel(ids_ref, out_hbm, out_ref, sem):
     batch, keys = ids_ref.shape
-    _, rows, wide = buf.shape
-    width = out_ref.shape[1]
-    lists = gather_copies(refs, refs[0].shape[0] - rows, buf, sems)
-    for copies in lists:
-        for copy in copies:
-            copy.start()
+    rows = out_ref.shape[1] // 8
     y, core = lax.axis_index("y"), lax.axis_index("core")
     ids = ids_ref[...]
-    pool = jnp.zeros((batch, width), f32)
-    for t, copies in enumerate(lists):
+    for t in range(8):
         side = core if t < 4 else 1 - core
-        first = (2 * lax.rem(y + t, 4) + side) * 2 * rows
-        lanes = iota((batch, 2 * rows), 1) + first
-        counts = jnp.zeros((batch, 2 * rows), f32)
+        first = (2 * lax.rem(y + t, 4) + side) * rows
+        lanes = iota((batch, rows), 1) + first
+        counts = jnp.zeros((batch, rows), f32)
         for k in range(keys):
             counts += jnp.where(ids[:, k : k + 1] == lanes, 1.0, 0.0)
-        counts = counts.astype(bf16)
+        out_ref[:, t * rows : (t + 1) * rows] = counts.astype(bf16)
+    copy = pltpu.make_async_copy(out_ref, out_hbm, sem)
+    copy.start()
+    copy.wait()
+
+
+def count_of(ids, rows):
+    shape = (ids.shape[0], 8 * rows)
+    return pl.pallas_call(
+        count_kernel,
+        out_shape=jax.ShapeDtypeStruct(shape, bf16),
+        in_specs=[VM],
+        out_specs=HBM,
+        scratch_shapes=[pltpu.VMEM(shape, bf16), pltpu.SemaphoreType.DMA],
+        compiler_params=ALONE,
+        cost_estimate=cost(3),
+        name="count",
+    )(ids)
+
+
+def hot_pool_kernel(counts_hbm, *refs):
+    refs, (out_ref, buf, counts_ref, sem, sems) = refs[:-5], refs[-5:]
+    _, _, rows, wide = buf.shape
+    width = out_ref.shape[1]
+    early = pltpu.make_async_copy(counts_hbm, counts_ref, sem)
+    early.start()
+    lists = gather_copies(refs, refs[0].shape[0] - rows, buf, sems)
+    early.wait()
+    pool = jnp.zeros(out_ref.shape, f32)
+    for side, copies in enumerate(lists):
         for copy in copies:
             copy.wait()
-        pool += jnp.dot(counts[:, :rows], buf[t, :, :width], preferred_element_type=f32)
-        pool += jnp.dot(counts[:, rows:], buf[t, :, width:], preferred_element_type=f32)
+        for y in range(4):
+            at = (4 * side + y) * 2 * rows
+            counts = counts_ref[:, at : at + 2 * rows]
+            part = buf[side, y]
+            pool += jnp.dot(counts[:, :rows], part[:, :width], preferred_element_type=f32)
+            pool += jnp.dot(counts[:, rows:], part[:, width:], preferred_element_type=f32)
     out_ref[...] = pool.astype(bf16)
 
 
-def hot_pooled(ids, pieces, width):
+def hot_pooled(counts, pieces, width):
     wide = pieces[0].shape[1]
     rows = pieces[0].shape[0] - 2 * width
     return pl.pallas_call(
         hot_pool_kernel,
-        out_shape=jax.ShapeDtypeStruct((ids.shape[0], width), bf16),
-        in_specs=[VM] + [HBM] * len(pieces),
+        out_shape=jax.ShapeDtypeStruct((counts.shape[0], width), bf16),
+        in_specs=[HBM] * (1 + len(pieces)),
         out_specs=VM,
-        scratch_shapes=[pltpu.VMEM((8, rows, wide), bf16), pltpu.SemaphoreType.DMA((COPIES,))],
+        scratch_shapes=[
+            pltpu.VMEM((2, 4, rows, wide), bf16),
+            pltpu.VMEM(counts.shape, bf16),
+            pltpu.SemaphoreType.DMA,
+            pltpu.SemaphoreType.DMA((COPIES,)),
+        ],
         compiler_params=ALONE,
         cost_estimate=cost(0.1),
         name="hot_pool",
-    )(ids, *pieces)
-
-
-def tower_kernel(
-    hot_ref,
-    head_ref,
-    label_ref,
-    ids_ref,
-    returned_hbm,
-    spread_hbm,
-    *refs,
-):
+    )(counts, *pieces)
+
+
+def tower_kernel(hot_ref, head_ref, label_ref, ids_ref, returned_ref, spread_hbm, *refs):
     pieces, refs = refs[:-9], refs[-9:]
-    dcold_ref, load_ref, pre_ref, sig_ref, returned_ref, spread_ref, w_ref, two, sems = refs
+    out_hbm, load_ref, pre_ref, sig_ref, spread_ref, w_ref, out_ref, two, sems = refs
     batch, width = hot_ref.shape
-    parts, din, part = w_ref.shape
+    _, _, din, part = w_ref.shape
+    parts = 8
     keys = ids_ref.shape[1]
-    firsts = [
-        pltpu.make_async_copy(spread_hbm, spread_ref, two.at[0]),
-        pltpu.make_async_copy(returned_hbm, returned_ref, two.at[1]),
-    ]
+    early = pltpu.make_async_copy(spread_hbm, spread_ref, two.at[0])
+    early.start()
     lists = gather_copies(pieces, 0, w_ref, sems)
-    for copies in [firsts] + lists:
-        for copy in copies:
-            copy.start()
-    for copy in firsts:
-        copy.wait()
+    early.wait()
     cold = contract_rows(spread_ref[...], returned_ref[...]).astype(bf16)
     feat = jnp.concatenate([hot_ref[...], cold], axis=1)
     logit = jnp.zeros((batch, 1), f32)
-    for t in range(parts):
+    waits = {0: lists[0][:1], 4: lists[1][:1], 1: lists[0][1:], 5: lists[1][1:]}
+    for t in (0, 4, 1, 2, 3, 5, 6, 7):
         cols = slice(t * part, (t + 1) * part)
-        for copy in lists[t]:
+        for copy in waits.get(t, ()):
             copy.wait()
-        pre = jnp.dot(feat, w_ref[t], preferred_element_type=f32)
+        pre = jnp.dot(feat, w_ref[t // 4, t % 4], preferred_element_type=f32)
         sig = jax.nn.sigmoid(pre)
         pre_ref[:, cols] = pre
         sig_ref[:, cols] = sig
@@ -339,15 +351,15 @@
         sig = sig_ref[:, cols]
         dpre = (dlogit * head_ref[:, cols] * sig * (1.0 + pre * (1.0 - sig))).astype(bf16)
         dfeat += lax.dot_general(
-            dpre, w_ref[t], (((1,), (1,)), ((), ())), preferred_element_type=f32
+            dpre, w_ref[t // 4, t % 4], (((1,), (1,)), ((), ())), preferred_element_type=f32
         )
     dhot = dfeat[:, :width]
-    dcold_ref[...] = dfeat[:, width:].astype(bf16)
-    hot_hi = dhot.astype(bf16)
-    hot_lo = (dhot - hot_hi.astype(f32)).astype(bf16)
+    dcold = dfeat[:, width:].astype(bf16)
+    out_ref[...] = jnp.dot(spread_ref[...], dcold, preferred_element_type=f32).astype(bf16)
+    last = pltpu.make_async_copy(out_ref, out_hbm, two.at[1])
+    last.start()
     load_ref[:, :din] = feat
-    load_ref[:, din : din + width] = hot_hi
-    load_ref[:, din + width : 2 * din] = hot_lo
+    load_ref[:, din : din + width] = dhot.astype(bf16)
     first = dlogit.astype(bf16).astype(f32)
     second = (dlogit - first).astype(bf16).astype(f32)
     third = dlogit - first - second
@@ -363,7 +375,8 @@
     for k in range(keys):
         extra = jnp.where(lanes == 8 + k, high[:, k : k + 1], extra)
         extra = jnp.where(lanes == 8 + keys + k, low[:, k : k + 1], extra)
-    load_ref[:, 2 * din :] = extra.astype(bf16)
+    load_ref[:, din + width :] = extra.astype(bf16)
+    last.wait()
 
 
 def tower(hot, returned, spread_mat, head, label, ids, pieces):
@@ -372,87 +385,75 @@
     return pl.pallas_call(
         tower_kernel,
         out_shape=(
-            jax.ShapeDtypeStruct((batch, width), bf16),
-            jax.ShapeDtypeStruct((batch, 4 * width + 128), bf16),
+            jax.ShapeDtypeStruct(returned.shape, bf16),
+            jax.ShapeDtypeStruct((batch, 3 * width + 128), bf16),
         ),
-        in_specs=[VM] * 4 + [HBM] * (2 + len(pieces)),
-        out_specs=(VM, VM),
+        in_specs=[VM] * 5 + [HBM] * (1 + len(pieces)),
+        out_specs=(HBM, VM),
         scratch_shapes=[
             pltpu.VMEM((batch, hidden), f32),
             pltpu.VMEM((batch, hidden), f32),
+            pltpu.VMEM(spread_mat.shape, bf16),
+            pltpu.VMEM((2, 4, 2 * width, hidden // 8), bf16),
             pltpu.VMEM(returned.shape, bf16),
-            pltpu.VMEM(spread_mat.shape, bf16),
-            pltpu.VMEM((8, 2 * width, hidden // 8), bf16),
             pltpu.SemaphoreType.DMA((2,)),
             pltpu.SemaphoreType.DMA((COPIES,)),
         ],
-        compiler_params=ALONE,
+        compiler_params=MOST,
         cost_estimate=cost(6),
         name="tower",
     )(hot, head, label, ids, returned, spread_mat, *pieces)
 
 
-def outgoing_kernel(dcold_ref, spread_hbm, out_hbm, spread_ref, out_ref, sems):
-    slots = spread_ref.shape[0]
-    step = slots // 4
-    loads = []
-    for n in range(4):
-        at = slice(n * step, (n + 1) * step)
-        loads.append(pltpu.make_async_copy(spread_hbm.at[at], spread_ref.at[at], sems.at[n]))
-        loads[n].start()
-    stores = []
-    for n in range(4):
-        at = slice(n * step, (n + 1) * step)
-        loads[n].wait()
-        out = jnp.dot(spread_ref[at, :], dcold_ref[...], preferred_element_type=f32)
-        out_ref[at, :] = out.astype(bf16)
-        stores.append(pltpu.make_async_copy(out_ref.at[at], out_hbm.at[at], sems.at[4 + n]))
-        stores[n].start()
-    for store in stores:
-        store.wait()
-
-
-def outgoing_of(dcold, spread_mat):
-    shape = (spread_mat.shape[0], dcold.shape[1])
-    return pl.pallas_call(
-        outgoing_kernel,
-        out_shape=jax.ShapeDtypeStruct(shape, bf16),
-        in_specs=[VM, HBM],
+def hold_kernel(in_ref, out_ref):
+    pass
+
+
+def hold(value):
+    return pl.pallas_call(
+        hold_kernel,
+        out_shape=jax.ShapeDtypeStruct(value.shape, value.dtype),
+        in_specs=[HBM],
         out_specs=HBM,
-        scratch_shapes=[
-            pltpu.VMEM(spread_mat.shape, bf16),
-            pltpu.VMEM(shape, bf16),
-            pltpu.SemaphoreType.DMA((8,)),
-        ],
+        input_output_aliases={0: 0},
         compiler_params=ALONE,
         cost_estimate=cost(30),
-        name="outgoing",
-    )(dcold, spread_mat)
-
-
-def columns_kernel(keys, head_ref, half_hbm, *refs):
-    loads, (out_ref, half_ref, load_ref, sems) = refs[:-4], refs[-4:]
+        name="hold",
+    )(value)
+
+
+def columns_kernel(keys, last, head_ref, half_hbm, *refs):
+    if last:
+        before_hbm, *refs = refs
+        *loads, out_ref, half_ref, load_ref, sems, before_ref = refs
+    else:
+        *loads, out_ref, half_ref, load_ref, sems = refs
     din, part = half_ref.shape
     rows, width = din, din // 2
     batch = loads[0].shape[0]
-    first = pltpu.make_async_copy(half_hbm.at[:din], half_ref, sems.at[len(loads)])
+    count = len(loads)
+    first = pltpu.make_async_copy(half_hbm.at[:din], half_ref, sems.at[count])
+    first.start()
     copies = [
         pltpu.make_async_copy(ref, load_ref.at[pl.ds(n * batch, batch)], sems.at[n])
         for n, ref in enumerate(loads)
     ]
-    for copy in [first] + copies:
+    for copy in copies:
         copy.start()
+    if last:
+        before = pltpu.make_async_copy(before_hbm, before_ref, sems.at[count + 1])
+        before.start()
     first.wait()
     base = (2 * lax.axis_index("y") + lax.axis_index("core")) * rows
     lanes = (iota((2 * batch, rows), 1) + base).astype(f32)
     tower_grad = jnp.zeros((din, part), f32)
     hot_grad = jnp.zeros((rows, width), f32)
-    for n in range(0, len(loads), 2):
+    for n in range(0, count, 2):
         copies[n].wait()
         copies[n + 1].wait()
         at = slice(n * batch, (n + 2) * batch)
         feat = load_ref[at, :din]
-        extra = load_ref[at, 2 * din :].astype(f32)
+        extra = load_ref[at, din + width :].astype(f32)
         dlogit = extra[:, 0:1] + extra[:, 1:2] + extra[:, 2:3]
         pre = jnp.dot(feat, half_ref[...], preferred_element_type=f32)
         sig = jax.nn.sigmoid(pre)
@@ -462,29 +463,36 @@
         for k in range(keys):
             ids = extra[:, 8 + k : 9 + k] * 64.0 + extra[:, 8 + keys + k : 9 + keys + k]
             counts += jnp.where(ids == lanes, 1.0, 0.0)
-        counts = counts.astype(bf16)
-        hot_grad += contract_rows(counts, load_ref[at, din : din + width])
-        hot_grad += contract_rows(counts, load_ref[at, din + width : 2 * din])
-    out_ref[:, :part] = tower_grad.astype(bf16)
-    out_ref[:, part:] = hot_grad.astype(bf16)
-
-
-def columns(loads, half, head, keys):
+        hot_grad += contract_rows(counts.astype(bf16), load_ref[at, din : din + width])
+    if last:
+        before.wait()
+        out_ref[:, :part] = (tower_grad + before_ref[:, :part]).astype(bf16)
+        out_ref[:, part:] = (hot_grad + before_ref[:, part:]).astype(bf16)
+    else:
+        out_ref[:, :part] = tower_grad
+        out_ref[:, part:] = hot_grad
+
+
+def columns(loads, half, head, keys, before=()):
     batch, wide = loads[0].shape
-    return pl.pallas_call(
-        functools.partial(columns_kernel, keys),
-        out_shape=jax.ShapeDtypeStruct((half.shape[1], half.shape[0]), bf16),
-        in_specs=[VM] + [HBM] * (1 + len(loads)),
+    rows, part = half.shape[1], head.shape[1]
+    shape = (rows, half.shape[0])
+    last = len(before) > 0
+    return pl.pallas_call(
+        functools.partial(columns_kernel, keys, last),
+        out_shape=jax.ShapeDtypeStruct(shape, bf16 if last else f32),
+        in_specs=[VM] + [HBM] * (1 + len(before) + len(loads)),
         out_specs=VM,
         scratch_shapes=[
-            pltpu.VMEM((half.shape[1], half.shape[1]), bf16),
+            pltpu.VMEM((rows, part), bf16),
             pltpu.VMEM((batch * len(loads), wide), bf16),
-            pltpu.SemaphoreType.DMA((1 + len(loads),)),
-        ],
+            pltpu.SemaphoreType.DMA((2 + len(loads),)),
+        ]
+        + [pltpu.VMEM(shape, f32)] * len(before),
         compiler_params=ALONE,
-        cost_estimate=cost(5),
+        cost_estimate=cost(0.2),
         name="columns",
-    )(head, half, *loads)
+    )(head, half, *before, *loads)
 
 
 def total_kernel(terms_ref, left_ref, right_ref):
@@ -569,10 +577,35 @@
         out_shape=(jax.ShapeDtypeStruct(w.shape, f32),) * 2
         + (jax.ShapeDtypeStruct(hot.shape, f32),) * 2,
         scratch_shapes=[pltpu.VMEM((step, 2 * half), f32)],
-        compiler_params=ALONE,
+        compiler_params=PARAMS,
         cost_estimate=cost(4),
         name="update",
     )(*left, *right, w, w_acc, hot, hot_acc)
+
+
+def stage_kernel(*refs):
+    count = len(refs) // 2
+    sems = refs[-1]
+    copies = [
+        pltpu.make_async_copy(refs[n], refs[count + n], sems.at[n]) for n in range(count)
+    ]
+    for copy in copies:
+        copy.start()
+    for copy in copies:
+        copy.wait()
+
+
+def stage(values):
+    return pl.pallas_call(
+        stage_kernel,
+        out_shape=tuple(jax.ShapeDtypeStruct(value.shape, value.dtype) for value in values),
+        in_specs=[HBM] * len(values),
+        out_specs=(VM,) * len(values),
+        scratch_shapes=[pltpu.SemaphoreType.DMA((len(values),))],
+        compiler_params=PARAMS,
+        cost_estimate=cost(4),
+        name="stage",
+    )(*values)
 
 
 def cold_kernel(asked_ref, grads_ref, table_ref, acc_ref, new_ref, new_acc_ref):
@@ -648,11 +681,15 @@
     asked = lax.all_to_all(asks, ALL, split_axis=0, concat_axis=0, tiled=True)
     spread_mat = spread(place, scale, capacity)
     quarters = tuple(along(quarter, "y", by) for by in (1, 2, 3))
-    asked, quarters = lax.optimization_barrier((asked, quarters))
+    counts = count_of(hot_ids, hot_rows)
+    cold_half = cold_table.astype(bf16)
+    asked, counts, cold_half, spread_mat = lax.optimization_barrier(
+        (asked, counts, cold_half, spread_mat)
+    )
     count = quarter.shape[0] // 2
-    by_x = jnp.concatenate([value[:count] for value in quarters])
-    by_z = jnp.concatenate([value[count:] for value in quarters])
-    looked = lookup(asked, cold_table)
+    by_x = jnp.stack([value[:count] for value in quarters])
+    by_z = jnp.stack([value[count:] for value in quarters])
+    looked = lookup(asked, cold_half)
     xs = tuple(along(by_x, "x", by) for by in (1, 2, 3))
     zs = tuple(along(by_z, "z", by) for by in (1, 2, 3))
     returned = lax.all_to_all(
@@ -660,7 +697,7 @@
     ).reshape(-1, width)
     pieces = lax.optimization_barrier((half, by_x) + xs + (by_z,) + zs)
     pieces += tuple(swap(value) for value in pieces)
-    hot_feat = hot_pooled(hot_ids, pieces, width)
+    hot_feat = hot_pooled(counts, pieces, width)
     heads = head_w.reshape(4, 2, part)
     turned = jnp.concatenate([heads, heads])
     turned = lax.dynamic_slice_in_dim(turned, y, 4, 0)
@@ -668,26 +705,31 @@
         [lax.dynamic_slice_in_dim(turned, side, 1, 1).reshape(1, -1) for side in (core, 1 - core)],
         axis=1,
     )
-    dcold, load = tower(
+    outgoing, load = tower(
         hot_feat, returned, spread_mat, head, labels[:, None], hot_ids, pieces
     )
     loads = around(load, "y")
-    outgoing = outgoing_of(dcold, spread_mat)
+    outgoing, loads = lax.optimization_barrier((outgoing, loads))
     incoming = lax.all_to_all(
         outgoing.reshape(devices, capacity, width), ALL, split_axis=0, concat_axis=0, tiled=True
     ).reshape(-1, width)
     loads += tuple(swap(part) for part in loads)
     head_part = lax.dynamic_slice(head_w, (me * part,), (part,))[None, :]
-    partial = columns(loads, half, head_part, keys)
+    own, one, two, last = loads[:4]
+    early = columns((own, loads[4], one, last), half, head_part, keys)
+    partial = columns((two,) + loads[5:], half, head_part, keys, (early,))
     partial, incoming = lax.optimization_barrier((partial, incoming))
     terms = lax.all_to_all(partial, ("x", "z"), split_axis=0, concat_axis=0, tiled=True)
     new_cold = cold_update(asked.reshape(1, -1), incoming, cold_table, cold_acc)
     terms, (new_cold, new_cold_acc) = lax.optimization_barrier((terms, new_cold))
     left, right = total_of(terms.reshape(16, -1, part + width))
     left, right = lay(around(left, "z"), around(right, "x"))
+    params = (tower_w, tower_acc, hot_table, hot_acc)
+    left, right, params = lax.optimization_barrier((left, right, params))
+    params = stage(params)
     left, right = around(left, "x"), around(right, "z")
     new_w, new_w_acc, new_hot, new_hot_acc = update(
-        left, right, tower_w, tower_acc, hot_table, hot_acc
+        left, right, *params
     )
     return (new_hot, new_hot_acc, new_cold, new_cold_acc, new_w, new_w_acc)
 

time: 169 us -> 162 us (0.959)
  blocking collectives: 19.2 us -> 0 us
  waiting for transfers between devices: 31 us -> 41.7 us
  starting transfers between devices: 57 us -> 67 us
  local copies, waits for them, and re-layouts: 12.7 us -> 4.99 us
    all_to_all x1 -> x0, blocking collectives: 19.2 us -> none  [on_device(): asked = lax.all_to_all(asks, ALL, split_axis=0, concat_axis=0, tiled=True)]
    ppermute x24, starting transfers between devices: 29.6 us -> 38.9 us  [along(): return lax.ppermute(value, axis, [((i + by) % 4, i) for i in range(4)])]
    all_to_all x0 -> x1, starting transfers between devices: none -> 8.01 us  [on_device(): asked = lax.all_to_all(asks, ALL, split_axis=0, concat_axis=0, tiled=True)]
    unnamed x66 -> x50, local copies, waits for them, and re-layouts: 9.76 us -> 3.43 us
    all_to_all x1, waiting for transfers between devices: 1.4 us -> 7.22 us  [on_device(): lax.all_to_all(looked.reshape(devices, capacity, width), ALL, split_axis=...]
    all_to_all x1, starting transfers between devices: 10.4 us -> 6.16 us  [on_device(): lax.all_to_all(looked.reshape(devices, capacity, width), ALL, split_axis=...]
    all_to_all x1, starting transfers between devices: 9.1 us -> 5.68 us  [on_device(): lax.all_to_all(outgoing.reshape(devices, capacity, width), ALL, split_axi...]
    pallas_call x1, Pallas kernels: 4.78 us -> 2.19 us  [update(): pl.pallas_call(update_kernel, grid=(4,), in_specs=[VM] * 8 + [w_block] *...]
  transfers between devices with their start and end apart: 40 -> 41, of which waited for: 15 -> 17; matrix products, arithmetic and copies ran while one was open for 3% -> 2% of each run, Pallas kernels for 17% -> 19%
where the time goes in v3:
time: 162 us; the launch traced here: 161 us
  starting transfers between devices  67 us (41%)
  Pallas kernels  44.8 us (28%)
  waiting for transfers between devices  41.7 us (26%)
  local copies, waits for them, and re-layouts  4.99 us (3%)
  other arithmetic  1.76 us (1%)
    ppermute x24, starting transfers between devices, along(): return lax.ppermute(value, axis, [((i + by) % 4, i) for i in range(4)])  38.9 us
    ppermute x24, waiting for transfers between devices, along(): return lax.ppermute(value, axis, [((i + by) % 4, i) for i in range(4)])  19.2 us
    pallas_call x2, Pallas kernels, columns(): pl.pallas_call(functools.partial(columns_kernel, keys, last), out_shape=j...  10.2 us
    pallas_call x1, Pallas kernels, tower(): pl.pallas_call(tower_kernel, out_shape=(jax.ShapeDtypeStruct(returned.sha...  8.8 us
    all_to_all x1, starting transfers between devices, on_device(): asked = lax.all_to_all(asks, ALL, split_axis=0, concat_axis=0, tiled=True)  8.01 us
    all_to_all x1, waiting for transfers between devices, on_device(): lax.all_to_all(looked.reshape(devices, capacity, width), ALL, split_axis=...  7.22 us
    all_to_all x1, waiting for transfers between devices, on_device(): lax.all_to_all(outgoing.reshape(devices, capacity, width), ALL, split_axi...  6.76 us
    all_to_all x1, starting transfers between devices, on_device(): lax.all_to_all(looked.reshape(devices, capacity, width), ALL, split_axis=...  6.16 us
  transfers between devices with their start and end apart: 41, of which 17 were waited for; matrix products, arithmetic and copies ran while one was open for 2% of the time, Pallas kernels for 19%

profile of v3, /device:TPU:2, one launch (start us, length us, event | category | flops | bytes accessed | tf_op | source)
XLA Modules:
  0.0 161.3 jit_solution(9168124741488034816)
XLA Ops:
  0.6 2.5 %route.1 = (s32[128,16]{1,0:T(8,128)}, f32[128,128]{1,0:T(8,128)}, f32[128,128]{1,0:T(8,128)}, bf16[768,512]{1,0:T(8,128)(2,1)}, bf16[192,512]{1,0:T(8,128)(2,1)}) custom-call(s32[8,128]{1,0:T(8,128)} %bitcast.42, s32[8,128]{1,0:T(8,128)} %bitcast.43, s32[8,128]{1,0:T(8,128)} %bitcast.44, f32[512,256]{1,0:T(8,128)} %refs_2_, f32[512,512]{1,0:T(8,128)} %refs_0_), custom_call_target="tpu_custom_call" | custom-call | flops 2000000000 | bytes 6000000 | tf_op jit(solution)/shard_map/route/pallas_call | solution.py:110
  4.8 2.9 %collective-permute-start.1 = (bf16[192,512]{1,0:T(8,128)(2,1)}, bf16[192,512]{1,0:T(8,128)(2,1)S(1)}, u32[]{:S(2)}, u32[]{:S(2)}) collective-permute-start(bf16[192,512]{1,0:T(8,128)(2,1)} %get-tuple-element.61), channel_id=1, source_target_pairs={{64,0},{96,32},{0,64},{32,96},{65,1},{97,33},{1,65},{33,97},{66,2}... | collective-permute-start | bytes 589832 | tf_op jit(solution)/shard_map/ppermute | solution.py:645
  9.0 8.0 %all-to-all-start = ((s32[128,1,16]{2,1,0:T(1,128)}), s32[128,1,16]{2,1,0:T(1,128)S(1)}, u32[]{:S(2)}, u32[]{:S(2)}) async-start(s32[128,1,16]{2,1,0:T(1,128)} %bitcast.36), calls=%async_computation | async-start | bytes 131072 | tf_op jit(solution)/shard_map/all_to_all | solution.py:681
  19.4 3.5 %count.1.counts_hbm = bf16[128,4096]{1,0:T(8,128)(2,1)} custom-call(s32[128,8]{1,0:T(8,128)} %copy.25.ids_ref), custom_call_target="tpu_custom_call" | custom-call | flops 3000000000 | bytes 9000000 | tf_op jit(solution)/shard_map/count/pallas_call | solution.py:269
  31.0 3.2 %collective-permute-start.7 = (bf16[3,96,512]{2,1,0:T(8,128)(2,1)S(1)}, bf16[3,96,512]{2,1,0:T(8,128)(2,1)}, u32[]{:S(2)}, u32[]{:S(2)}) collective-permute-start(bf16[3,96,512]{2,1,0:T(8,128)(2,1)S(1)} %pad_maximum_fusion.1.refs_5_), channel_id=1, source_target_pairs={{8,0},{12,4},{0,8},{4,12},{9,1},{13,5},{1,9},{5,13},{10,2},{14,6},... | collective-permute-start | bytes 884744 | tf_op jit(solution)/shard_map/ppermute | solution.py:645
  35.5 5.2 %lookup.1 = bf16[2048,256]{1,0:T(8,128)(2,1)} custom-call(s32[128,16]{1,0:T(8,128)} %bitcast.34, bf16[2048,256]{1,0:T(8,128)(2,1)} %convert_element_type.3.table_hbm), custom_call_target="tpu_custom_call" | custom-call | flops 3000000000 | bytes 9000000 | tf_op jit(solution)/shard_map/lookup/pallas_call | solution.py:195
  40.7 6.2 %all-to-all-start.1 = ((bf16[128,16,256]{2,1,0:T(8,128)(2,1)}), bf16[128,16,256]{2,1,0:T(8,128)(2,1)}, u32[]{:S(2)}, u32[]{:S(2)}) async-start(bf16[128,16,256]{2,1,0:T(8,128)(2,1)} %bitcast.32), calls=%async_computation.1 | async-start | bytes 2097152 | tf_op jit(solution)/shard_map/all_to_all | solution.py:695
  54.7 3.5 %hot_pool.1.hot_ref = bf16[128,256]{1,0:T(8,128)(2,1)} custom-call(bf16[128,4096]{1,0:T(8,128)(2,1)} %count.1.counts_hbm, bf16[768,512]{1,0:T(8,128)(2,1)} %get-tuple-element.62.refs_0_.half_hbm, bf16[3,96,512]{2,1,0:T(8,128)(2,1)} %copy-done.7, bf16[3,96,512]{2,1,0:T(8,128)(2,1)} %collective-permute-done.3.refs_2_, ...), custom_call_target="tpu_custom_call" | custom-call | flops 100000000 | bytes 300000 | tf_op jit(solution)/shard_map/hot_pool/pallas_call | solution.py:305
  58.2 7.2 %all-to-all-done.1 = bf16[128,16,256]{2,1,0:T(8,128)(2,1)} async-done(((bf16[128,16,256]{2,1,0:T(8,128)(2,1)}), bf16[128,16,256]{2,1,0:T(8,128)(2,1)}, u32[]{:S(2)}, u32[]{:S(2)}) %all-to-all-start.1) | async-done | bytes 1048608 | tf_op jit(solution)/shard_map/all_to_all | solution.py:695
  65.4 8.8 %tower.1 = (bf16[2048,256]{1,0:T(8,128)(2,1)}, bf16[128,896]{1,0:T(8,128)(2,1)}) custom-call(bf16[128,256]{1,0:T(8,128)(2,1)} %hot_pool.1.hot_ref, f32[1,4096]{1,0:T(1,128)} %pad_maximum_fusion.2.head_ref, f32[128,1]{1,0:T(8,128)} %copy.26.label_ref, s32[128,8]{1,0:T(8,128)} %copy.25.ids_ref, bf16[2048,256]{1,0:T(8,128)(2,1)} %bitcast.17.returned_ref, ...), custom_call_target="tpu_custom_call" | custom-call | flops 6000000000 | bytes 18000000 | tf_op jit(solution)/shard_map/tower/pallas_call | solution.py:385
  77.6 10.3 %collective-permute-done.20.refs_3_ = bf16[128,896]{1,0:T(8,128)(2,1)} collective-permute-done((bf16[128,896]{1,0:T(8,128)(2,1)}, bf16[128,896]{1,0:T(8,128)(2,1)}, u32[]{:S(2)}, u32[]{:S(2)}) %collective-permute-start.20) | collective-permute-done | bytes 229408 | tf_op jit(solution)/shard_map/ppermute | solution.py:645
  88.6 5.7 %all-to-all-start.2 = ((bf16[128,16,256]{2,1,0:T(8,128)(2,1)}), bf16[128,16,256]{2,1,0:T(8,128)(2,1)S(1)}, u32[]{:S(2)}, u32[]{:S(2)}) async-start(bf16[128,16,256]{2,1,0:T(8,128)(2,1)} %bitcast.33), calls=%async_computation.2 | async-start | bytes 2097152 | tf_op jit(solution)/shard_map/all_to_all | solution.py:713
  96.0 5.2 %columns.2.refs_0_ = f32[512,768]{1,0:T(8,128)} custom-call(f32[1,512]{1,0:T(1,128)} %bitcast.39, bf16[768,512]{1,0:T(8,128)(2,1)} %get-tuple-element.62.refs_0_.half_hbm, bf16[128,896]{1,0:T(8,128)(2,1)} %get-tuple-element.76.refs_0_, bf16[128,896]{1,0:T(8,128)(2,1)} %collective-permute-done.21.refs_1_, bf16[128,896]{1,0:T(8,128)(2,1)} %collective-permute-done.18.refs_2_, ...), custom_call_target="tpu_custom_call" | custom-call | flops 200000000 | bytes 600000 | tf_op jit(solution)/shard_map/columns/pallas_call | solution.py:481
  101.2 5.1 %columns.3 = bf16[512,768]{1,0:T(8,128)(2,1)} custom-call(f32[1,512]{1,0:T(1,128)} %bitcast.40, bf16[768,512]{1,0:T(8,128)(2,1)} %get-tuple-element.62.refs_0_.half_hbm, f32[512,768]{1,0:T(8,128)} %columns.2.refs_0_, bf16[128,896]{1,0:T(8,128)(2,1)} %collective-permute-done.19.refs_1_, bf16[128,896]{1,0:T(8,128)(2,1)} %collective-permute-done.22.refs_2_, ...), custom_call_target="tpu_custom_call" | custom-call | flops 200000000 | bytes 600000 | tf_op jit(solution)/shard_map/columns/pallas_call | solution.py:481
  106.3 6.8 %all-to-all-done.2 = bf16[128,16,256]{2,1,0:T(8,128)(2,1)S(1)} async-done(((bf16[128,16,256]{2,1,0:T(8,128)(2,1)}), bf16[128,16,256]{2,1,0:T(8,128)(2,1)S(1)}, u32[]{:S(2)}, u32[]{:S(2)}) %all-to-all-start.2) | async-done | bytes 1048608 | tf_op jit(solution)/shard_map/all_to_all | solution.py:713
  113.1 5.3 %all-to-all-start.3 = ((bf16[16,32,768]{2,1,0:T(8,128)(2,1)}), bf16[16,32,768]{2,1,0:T(8,128)(2,1)}, u32[]{:S(2)}, u32[]{:S(2)}) async-start(bf16[16,32,768]{2,1,0:T(8,128)(2,1)} %bitcast.31), calls=%async_computation.3 | async-start | bytes 1572864 | tf_op jit(solution)/shard_map/all_to_all | solution.py:722
  120.1 5.4 %cold_update.1 = (f32[2048,256]{1,0:T(8,128)}, f32[2048,256]{1,0:T(8,128)}) custom-call(s32[1,2048]{1,0:T(1,128)S(1)} %reshape.50.asked_ref, bf16[2048,256]{1,0:T(8,128)(2,1)S(1)} %bitcast.30, f32[2048,256]{1,0:T(8,128)S(1)} %copy-done, f32[2048,256]{1,0:T(8,128)S(1)} %copy-done.1), custom_call_target="tpu_custom_call" | custom-call | flops 5000000000 | bytes 15000000 | tf_op jit(solution)/shard_map/cold_update/pallas_call | solution.py:627
  125.5 5.1 %all-to-all-done.3 = bf16[16,32,768]{2,1,0:T(8,128)(2,1)} async-done(((bf16[16,32,768]{2,1,0:T(8,128)(2,1)}), bf16[16,32,768]{2,1,0:T(8,128)(2,1)}, u32[]{:S(2)}, u32[]{:S(2)}) %all-to-all-start.3) | async-done | bytes 786464 | tf_op jit(solution)/shard_map/all_to_all | solution.py:722
  132.4 2.4 %collective-permute-start.26 = (f32[32,384]{1,0:T(8,128)S(1)}, f32[32,384]{1,0:T(8,128)S(1)}, u32[]{:S(2)}, u32[]{:S(2)}) collective-permute-start(f32[32,384]{1,0:T(8,128)S(1)} %get-tuple-element.86.refs_0_), channel_id=1, source_target_pairs={{8,0},{12,4},{0,8},{4,12},{9,1},{13,5},{1,9},{5,13},{10,2},{14,6},... | collective-permute-start | bytes 147464 | tf_op jit(solution)/shard_map/ppermute | solution.py:645
  137.7 2.5 %collective-permute-start.29 = (f32[32,384]{1,0:T(8,128)S(1)}, f32[32,384]{1,0:T(8,128)S(1)}, u32[]{:S(2)}, u32[]{:S(2)}) collective-permute-start(f32[32,384]{1,0:T(8,128)S(1)} %get-tuple-element.87.refs_4_), channel_id=1, source_target_pairs={{2,0},{3,1},{0,2},{1,3},{6,4},{7,5},{4,6},{5,7},{10,8},{11,9},{8,1... | collective-permute-start | bytes 147464 | tf_op jit(solution)/shard_map/ppermute | solution.py:645
  140.7 2.6 %collective-permute-done.29.refs_6_ = f32[32,384]{1,0:T(8,128)S(1)} collective-permute-done((f32[32,384]{1,0:T(8,128)S(1)}, f32[32,384]{1,0:T(8,128)S(1)}, u32[]{:S(2)}, u32[]{:S(2)}) %collective-permute-start.29) | collective-permute-done | bytes 49184 | tf_op jit(solution)/shard_map/ppermute | solution.py:645
  144.5 2.5 %collective-permute-start.32 = (f32[128,384]{1,0:T(8,128)S(1)}, f32[128,384]{1,0:T(8,128)S(1)}, u32[]{:S(2)}, u32[]{:S(2)}) collective-permute-start(f32[128,384]{1,0:T(8,128)S(1)} %get-tuple-element.90.l0), channel_id=1, source_target_pairs={{2,0},{3,1},{0,2},{1,3},{6,4},{7,5},{4,6},{5,7},{10,8},{11,9},{8,1... | collective-permute-start | bytes 589832 | tf_op jit(solution)/shard_map/ppermute | solution.py:645
  151.7 2.6 %collective-permute-start.34 = (f32[128,384]{1,0:T(8,128)S(1)}, f32[128,384]{1,0:T(8,128)S(1)}, u32[]{:S(2)}, u32[]{:S(2)}) collective-permute-start(f32[128,384]{1,0:T(8,128)S(1)} %get-tuple-element.91.r0), channel_id=1, source_target_pairs={{4,0},{8,4},{12,8},{0,12},{5,1},{9,5},{13,9},{1,13},{6,2},{10,6},{... | collective-permute-start | bytes 589832 | tf_op jit(solution)/shard_map/ppermute | solution.py:645
  154.6 3.7 %collective-permute-done.36.r3 = f32[128,384]{1,0:T(8,128)S(1)} collective-permute-done((f32[128,384]{1,0:T(8,128)S(1)}, f32[128,384]{1,0:T(8,128)S(1)}, u32[]{:S(2)}, u32[]{:S(2)}) %collective-permute-start.36) | collective-permute-done | bytes 196640 | tf_op jit(solution)/shard_map/ppermute | solution.py:645
  (134 shorter events, 44.2 us)
Async XLA Ops:
  3.1 14.6 %collective-permute-start.2 = (bf16[192,512]{1,0:T(8,128)(2,1)}, bf16[192,512]{1,0:T(8,128)(2,1)S(1)}, u32[]{:S(2)}, u32[]{:S(2)}) collective-permute-start(bf16[192,512]{1,0:T(8,128)(2,1)} %get-tuple-element.61), channel_id=1, source_target_pairs={{96,0},{0,32},{32,64},{64,96},{97,1},{1,33},{33,65},{65,97},{98,2}... | collective-permute-start | bytes 589832 | tf_op jit(solution)/shard_map/ppermute | solution.py:645
  4.8 13.0 %collective-permute-start.1 = (bf16[192,512]{1,0:T(8,128)(2,1)}, bf16[192,512]{1,0:T(8,128)(2,1)S(1)}, u32[]{:S(2)}, u32[]{:S(2)}) collective-permute-start(bf16[192,512]{1,0:T(8,128)(2,1)} %get-tuple-element.61), channel_id=1, source_target_pairs={{64,0},{96,32},{0,64},{32,96},{65,1},{97,33},{1,65},{33,97},{66,2}... | collective-permute-start | bytes 589832 | tf_op jit(solution)/shard_map/ppermute | solution.py:645
  7.7 10.2 %collective-permute-start = (bf16[192,512]{1,0:T(8,128)(2,1)}, bf16[192,512]{1,0:T(8,128)(2,1)S(1)}, u32[]{:S(2)}, u32[]{:S(2)}) collective-permute-start(bf16[192,512]{1,0:T(8,128)(2,1)} %get-tuple-element.61), channel_id=1, source_target_pairs={{32,0},{64,32},{96,64},{0,96},{33,1},{65,33},{97,65},{1,97},{34,2}... | collective-permute-start | bytes 589832 | tf_op jit(solution)/shard_map/ppermute | solution.py:645
  9.0 17.0 %all-to-all-start = ((s32[128,1,16]{2,1,0:T(1,128)}), s32[128,1,16]{2,1,0:T(1,128)S(1)}, u32[]{:S(2)}, u32[]{:S(2)}) async-start(s32[128,1,16]{2,1,0:T(1,128)} %bitcast.36), calls=%async_computation | async-start | bytes 131072 | tf_op jit(solution)/shard_map/all_to_all | solution.py:681
  17.9 16.3 %collective-permute-start.5 = (bf16[3,96,512]{2,1,0:T(8,128)(2,1)S(1)}, bf16[3,96,512]{2,1,0:T(8,128)(2,1)S(1)}, u32[]{:S(2)}, u32[]{:S(2)}) collective-permute-start(bf16[3,96,512]{2,1,0:T(8,128)(2,1)S(1)} %pad_maximum_fusion.refs_1_), channel_id=1, source_target_pairs={{3,0},{0,1},{1,2},{2,3},{7,4},{4,5},{5,6},{6,7},{11,8},{8,9},{9,10... | collective-permute-start | bytes 884744 | tf_op jit(solution)/shard_map/ppermute | solution.py:645
  26.1 21.6 %collective-permute-start.4 = (bf16[3,96,512]{2,1,0:T(8,128)(2,1)S(1)}, bf16[3,96,512]{2,1,0:T(8,128)(2,1)}, u32[]{:S(2)}, u32[]{:S(2)}) collective-permute-start(bf16[3,96,512]{2,1,0:T(8,128)(2,1)S(1)} %pad_maximum_fusion.refs_1_), channel_id=1, source_target_pairs={{2,0},{3,1},{0,2},{1,3},{6,4},{7,5},{4,6},{5,7},{10,8},{11,9},{8,1... | collective-permute-start | bytes 884744 | tf_op jit(solution)/shard_map/ppermute | solution.py:645
  27.7 19.9 %collective-permute-start.3 = (bf16[3,96,512]{2,1,0:T(8,128)(2,1)S(1)}, bf16[3,96,512]{2,1,0:T(8,128)(2,1)}, u32[]{:S(2)}, u32[]{:S(2)}) collective-permute-start(bf16[3,96,512]{2,1,0:T(8,128)(2,1)S(1)} %pad_maximum_fusion.refs_1_), channel_id=1, source_target_pairs={{1,0},{2,1},{3,2},{0,3},{5,4},{6,5},{7,6},{4,7},{9,8},{10,9},{11,1... | collective-permute-start | bytes 884744 | tf_op jit(solution)/shard_map/ppermute | solution.py:645
  29.3 18.3 %collective-permute-start.8 = (bf16[3,96,512]{2,1,0:T(8,128)(2,1)S(1)}, bf16[3,96,512]{2,1,0:T(8,128)(2,1)}, u32[]{:S(2)}, u32[]{:S(2)}) collective-permute-start(bf16[3,96,512]{2,1,0:T(8,128)(2,1)S(1)} %pad_maximum_fusion.1.refs_5_), channel_id=1, source_target_pairs={{12,0},{0,4},{4,8},{8,12},{13,1},{1,5},{5,9},{9,13},{14,2},{2,6},{... | collective-permute-start | bytes 884744 | tf_op jit(solution)/shard_map/ppermute | solution.py:645
  31.0 16.6 %collective-permute-start.7 = (bf16[3,96,512]{2,1,0:T(8,128)(2,1)S(1)}, bf16[3,96,512]{2,1,0:T(8,128)(2,1)}, u32[]{:S(2)}, u32[]{:S(2)}) collective-permute-start(bf16[3,96,512]{2,1,0:T(8,128)(2,1)S(1)} %pad_maximum_fusion.1.refs_5_), channel_id=1, source_target_pairs={{8,0},{12,4},{0,8},{4,12},{9,1},{13,5},{1,9},{5,13},{10,2},{14,6},... | collective-permute-start | bytes 884744 | tf_op jit(solution)/shard_map/ppermute | solution.py:645
  34.3 13.4 %collective-permute-start.6 = (bf16[3,96,512]{2,1,0:T(8,128)(2,1)S(1)}, bf16[3,96,512]{2,1,0:T(8,128)(2,1)}, u32[]{:S(2)}, u32[]{:S(2)}) collective-permute-start(bf16[3,96,512]{2,1,0:T(8,128)(2,1)S(1)} %pad_maximum_fusion.1.refs_5_), channel_id=1, source_target_pairs={{4,0},{8,4},{12,8},{0,12},{5,1},{9,5},{13,9},{1,13},{6,2},{10,6},{... | collective-permute-start | bytes 884744 | tf_op jit(solution)/shard_map/ppermute | solution.py:645
  40.7 24.7 %all-to-all-start.1 = ((bf16[128,16,256]{2,1,0:T(8,128)(2,1)}), bf16[128,16,256]{2,1,0:T(8,128)(2,1)}, u32[]{:S(2)}, u32[]{:S(2)}) async-start(bf16[128,16,256]{2,1,0:T(8,128)(2,1)} %bitcast.32), calls=%async_computation.1 | async-start | bytes 2097152 | tf_op jit(solution)/shard_map/all_to_all | solution.py:695
  74.2 13.7 %collective-permute-start.20 = (bf16[128,896]{1,0:T(8,128)(2,1)}, bf16[128,896]{1,0:T(8,128)(2,1)}, u32[]{:S(2)}, u32[]{:S(2)}) collective-permute-start(bf16[128,896]{1,0:T(8,128)(2,1)} %get-tuple-element.76.refs_0_), channel_id=1, source_target_pairs={{96,0},{0,32},{32,64},{64,96},{97,1},{1,33},{33,65},{65,97},{98,2}... | collective-permute-start | bytes 688136 | tf_op jit(solution)/shard_map/ppermute | solution.py:645
  74.9 13.1 %collective-permute-start.19 = (bf16[128,896]{1,0:T(8,128)(2,1)}, bf16[128,896]{1,0:T(8,128)(2,1)}, u32[]{:S(2)}, u32[]{:S(2)}) collective-permute-start(bf16[128,896]{1,0:T(8,128)(2,1)} %get-tuple-element.76.refs_0_), channel_id=1, source_target_pairs={{64,0},{96,32},{0,64},{32,96},{65,1},{97,33},{1,65},{33,97},{66,2}... | collective-permute-start | bytes 688136 | tf_op jit(solution)/shard_map/ppermute | solution.py:645
  76.8 11.8 %collective-permute-start.18 = (bf16[128,896]{1,0:T(8,128)(2,1)}, bf16[128,896]{1,0:T(8,128)(2,1)}, u32[]{:S(2)}, u32[]{:S(2)}) collective-permute-start(bf16[128,896]{1,0:T(8,128)(2,1)} %get-tuple-element.76.refs_0_), channel_id=1, source_target_pairs={{32,0},{64,32},{96,64},{0,96},{33,1},{65,33},{97,65},{1,97},{34,2}... | collective-permute-start | bytes 688136 | tf_op jit(solution)/shard_map/ppermute | solution.py:645
  88.6 24.5 %all-to-all-start.2 = ((bf16[128,16,256]{2,1,0:T(8,128)(2,1)}), bf16[128,16,256]{2,1,0:T(8,128)(2,1)S(1)}, u32[]{:S(2)}, u32[]{:S(2)}) async-start(bf16[128,16,256]{2,1,0:T(8,128)(2,1)} %bitcast.33), calls=%async_computation.2 | async-start | bytes 2097152 | tf_op jit(solution)/shard_map/all_to_all | solution.py:713
  113.1 17.5 %all-to-all-start.3 = ((bf16[16,32,768]{2,1,0:T(8,128)(2,1)}), bf16[16,32,768]{2,1,0:T(8,128)(2,1)}, u32[]{:S(2)}, u32[]{:S(2)}) async-start(bf16[16,32,768]{2,1,0:T(8,128)(2,1)} %bitcast.31), calls=%async_computation.3 | async-start | bytes 1572864 | tf_op jit(solution)/shard_map/all_to_all | solution.py:722
  131.8 8.4 %collective-permute-start.27 = (f32[32,384]{1,0:T(8,128)S(1)}, f32[32,384]{1,0:T(8,128)S(1)}, u32[]{:S(2)}, u32[]{:S(2)}) collective-permute-start(f32[32,384]{1,0:T(8,128)S(1)} %get-tuple-element.86.refs_0_), channel_id=1, source_target_pairs={{12,0},{0,4},{4,8},{8,12},{13,1},{1,5},{5,9},{9,13},{14,2},{2,6},{... | collective-permute-start | bytes 147464 | tf_op jit(solution)/shard_map/ppermute | solution.py:645
  132.4 8.2 %collective-permute-start.26 = (f32[32,384]{1,0:T(8,128)S(1)}, f32[32,384]{1,0:T(8,128)S(1)}, u32[]{:S(2)}, u32[]{:S(2)}) collective-permute-start(f32[32,384]{1,0:T(8,128)S(1)} %get-tuple-element.86.refs_0_), channel_id=1, source_target_pairs={{8,0},{12,4},{0,8},{4,12},{9,1},{13,5},{1,9},{5,13},{10,2},{14,6},... | collective-permute-start | bytes 147464 | tf_op jit(solution)/shard_map/ppermute | solution.py:645
  144.3 7.3 %collective-permute-start.33 = (f32[128,384]{1,0:T(8,128)S(1)}, f32[128,384]{1,0:T(8,128)S(1)}, u32[]{:S(2)}, u32[]{:S(2)}) collective-permute-start(f32[128,384]{1,0:T(8,128)S(1)} %get-tuple-element.90.l0), channel_id=1, source_target_pairs={{3,0},{0,1},{1,2},{2,3},{7,4},{4,5},{5,6},{6,7},{11,8},{8,9},{9,10... | collective-permute-start | bytes 589832 | tf_op jit(solution)/shard_map/ppermute | solution.py:645
  144.5 10.1 %collective-permute-start.32 = (f32[128,384]{1,0:T(8,128)S(1)}, f32[128,384]{1,0:T(8,128)S(1)}, u32[]{:S(2)}, u32[]{:S(2)}) collective-permute-start(f32[128,384]{1,0:T(8,128)S(1)} %get-tuple-element.90.l0), channel_id=1, source_target_pairs={{2,0},{3,1},{0,2},{1,3},{6,4},{7,5},{4,6},{5,7},{10,8},{11,9},{8,1... | collective-permute-start | bytes 589832 | tf_op jit(solution)/shard_map/ppermute | solution.py:645
  147.0 7.6 %collective-permute-start.31 = (f32[128,384]{1,0:T(8,128)S(1)}, f32[128,384]{1,0:T(8,128)S(1)}, u32[]{:S(2)}, u32[]{:S(2)}) collective-permute-start(f32[128,384]{1,0:T(8,128)S(1)} %get-tuple-element.90.l0), channel_id=1, source_target_pairs={{1,0},{2,1},{3,2},{0,3},{5,4},{6,5},{7,6},{4,7},{9,8},{10,9},{11,1... | collective-permute-start | bytes 589832 | tf_op jit(solution)/shard_map/ppermute | solution.py:645
  149.3 9.0 %collective-permute-start.36 = (f32[128,384]{1,0:T(8,128)S(1)}, f32[128,384]{1,0:T(8,128)S(1)}, u32[]{:S(2)}, u32[]{:S(2)}) collective-permute-start(f32[128,384]{1,0:T(8,128)S(1)} %get-tuple-element.91.r0), channel_id=1, source_target_pairs={{12,0},{0,4},{4,8},{8,12},{13,1},{1,5},{5,9},{9,13},{14,2},{2,6},{... | collective-permute-start | bytes 589832 | tf_op jit(solution)/shard_map/ppermute | solution.py:645
  149.6 8.7 %collective-permute-start.35 = (f32[128,384]{1,0:T(8,128)S(1)}, f32[128,384]{1,0:T(8,128)S(1)}, u32[]{:S(2)}, u32[]{:S(2)}) collective-permute-start(f32[128,384]{1,0:T(8,128)S(1)} %get-tuple-element.91.r0), channel_id=1, source_target_pairs={{8,0},{12,4},{0,8},{4,12},{9,1},{13,5},{1,9},{5,13},{10,2},{14,6},... | collective-permute-start | bytes 589832 | tf_op jit(solution)/shard_map/ppermute | solution.py:645
  151.7 7.5 %collective-permute-start.34 = (f32[128,384]{1,0:T(8,128)S(1)}, f32[128,384]{1,0:T(8,128)S(1)}, u32[]{:S(2)}, u32[]{:S(2)}) collective-permute-start(f32[128,384]{1,0:T(8,128)S(1)} %get-tuple-element.91.r0), channel_id=1, source_target_pairs={{4,0},{8,4},{12,8},{0,12},{5,1},{9,5},{13,9},{1,13},{6,2},{10,6},{... | collective-permute-start | bytes 589832 | tf_op jit(solution)/shard_map/ppermute | solution.py:645
  (41 other events, 310.9 us)

commit v4 on v3

--- a/solution.py
+++ b/solution.py
@@ -161,12 +161,15 @@
     )(place, scale)
 
 
-def lookup_kernel(asked_ref, table_hbm, out_hbm, table_ref, out_ref, sem, sems):
+def lookup_kernel(asked_hbm, table_hbm, out_hbm, asked_ref, table_ref, out_ref, two, sems):
     devices, capacity = asked_ref.shape
     slots, width = out_ref.shape
     rows = table_ref.shape[0]
-    load = pltpu.make_async_copy(table_hbm, table_ref, sem)
+    first = pltpu.make_async_copy(asked_hbm, asked_ref, two.at[0])
+    load = pltpu.make_async_copy(table_hbm, table_ref, two.at[1])
+    first.start()
     load.start()
+    first.wait()
     full = (devices, capacity, capacity)
     wide = jnp.broadcast_to(asked_ref[...].astype(f32)[:, None, :], full)
     kept = jnp.where(iota(full, 1) == iota(full, 2), wide, 0.0).reshape(slots, capacity)
@@ -195,12 +198,13 @@
     return pl.pallas_call(
         lookup_kernel,
         out_shape=jax.ShapeDtypeStruct(shape, bf16),
-        in_specs=[VM, HBM],
+        in_specs=[HBM, HBM],
         out_specs=HBM,
         scratch_shapes=[
+            pltpu.VMEM(asked.shape, i32),
             pltpu.VMEM(table.shape, bf16),
             pltpu.VMEM(shape, bf16),
-            pltpu.SemaphoreType.DMA,
+            pltpu.SemaphoreType.DMA((2,)),
             pltpu.SemaphoreType.DMA((shape[0] // 256,)),
         ],
         compiler_params=ALONE,
@@ -235,11 +239,11 @@
                 copies.append(pltpu.make_async_copy(src, dst, sems.at[n]))
                 n += 1
         lists.append(copies)
+    for n, copies in enumerate(lists):
+        copies[0].start(priority=n)
     for copies in lists:
-        copies[0].start()
-    for copies in lists:
-        for copy in copies[1:]:
-            copy.start()
+        for n, copy in enumerate(copies[1:]):
+            copy.start(priority=n % 2)
     return lists
 
 
@@ -319,17 +323,22 @@
     )(counts, *pieces)
 
 
-def tower_kernel(hot_ref, head_ref, label_ref, ids_ref, returned_ref, spread_hbm, *refs):
-    pieces, refs = refs[:-9], refs[-9:]
-    out_hbm, load_ref, pre_ref, sig_ref, spread_ref, w_ref, out_ref, two, sems = refs
+def tower_kernel(*refs):
+    smalls, pieces, refs = refs[:6], refs[6:-14], refs[-14:]
+    out_hbm, load_ref, pre_ref, sig_ref, *held, w_ref, out_ref, two, sems = refs
+    small_copies = [
+        pltpu.make_async_copy(a, b, two.at[n]) for n, (a, b) in enumerate(zip(smalls, held))
+    ]
+    for copy in small_copies:
+        copy.start()
+    hot_ref, returned_ref, spread_ref, head_ref, label_ref, ids_ref = held
     batch, width = hot_ref.shape
     _, _, din, part = w_ref.shape
     parts = 8
     keys = ids_ref.shape[1]
-    early = pltpu.make_async_copy(spread_hbm, spread_ref, two.at[0])
-    early.start()
     lists = gather_copies(pieces, 0, w_ref, sems)
-    early.wait()
+    for copy in small_copies:
+        copy.wait()
     cold = contract_rows(spread_ref[...], returned_ref[...]).astype(bf16)
     feat = jnp.concatenate([hot_ref[...], cold], axis=1)
     logit = jnp.zeros((batch, 1), f32)
@@ -356,7 +365,7 @@
     dhot = dfeat[:, :width]
     dcold = dfeat[:, width:].astype(bf16)
     out_ref[...] = jnp.dot(spread_ref[...], dcold, preferred_element_type=f32).astype(bf16)
-    last = pltpu.make_async_copy(out_ref, out_hbm, two.at[1])
+    last = pltpu.make_async_copy(out_ref, out_hbm, two.at[6])
     last.start()
     load_ref[:, :din] = feat
     load_ref[:, din : din + width] = dhot.astype(bf16)
@@ -382,27 +391,30 @@
 def tower(hot, returned, spread_mat, head, label, ids, pieces):
     batch, width = hot.shape
     hidden = head.shape[1]
+    smalls = (hot, returned, spread_mat, head, label, ids)
     return pl.pallas_call(
         tower_kernel,
         out_shape=(
             jax.ShapeDtypeStruct(returned.shape, bf16),
             jax.ShapeDtypeStruct((batch, 3 * width + 128), bf16),
         ),
-        in_specs=[VM] * 5 + [HBM] * (1 + len(pieces)),
+        in_specs=[HBM] * (6 + len(pieces)),
         out_specs=(HBM, VM),
         scratch_shapes=[
             pltpu.VMEM((batch, hidden), f32),
             pltpu.VMEM((batch, hidden), f32),
-            pltpu.VMEM(spread_mat.shape, bf16),
+        ]
+        + [pltpu.VMEM(value.shape, value.dtype) for value in smalls]
+        + [
             pltpu.VMEM((2, 4, 2 * width, hidden // 8), bf16),
             pltpu.VMEM(returned.shape, bf16),
-            pltpu.SemaphoreType.DMA((2,)),
+            pltpu.SemaphoreType.DMA((7,)),
             pltpu.SemaphoreType.DMA((COPIES,)),
         ],
         compiler_params=MOST,
         cost_estimate=cost(6),
         name="tower",
-    )(hot, head, label, ids, returned, spread_mat, *pieces)
+    )(*smalls, *pieces)
 
 
 def hold_kernel(in_ref, out_ref):

time: 162 us -> 161 us (level)
  transfers between devices with their start and end apart: 41 -> 41, of which waited for: 17 -> 17; matrix products, arithmetic and copies ran while one was open for 2% -> 3% of each run, Pallas kernels for 19% -> 18%
where the time goes in v4:
time: 161 us; the launch traced here: 160 us
  starting transfers between devices  67.2 us (42%)
  Pallas kernels  43.3 us (27%)
  waiting for transfers between devices  41.8 us (26%)
  local copies, waits for them, and re-layouts  4.99 us (3%)
  other arithmetic  1.76 us (1%)
    ppermute x24, starting transfers between devices, along(): return lax.ppermute(value, axis, [((i + by) % 4, i) for i in range(4)])  39.1 us
    ppermute x24, waiting for transfers between devices, along(): return lax.ppermute(value, axis, [((i + by) % 4, i) for i in range(4)])  19.2 us
    pallas_call x2, Pallas kernels, columns(): pl.pallas_call(functools.partial(columns_kernel, keys, last), out_shape=j...  10.2 us
    pallas_call x1, Pallas kernels, tower(): pl.pallas_call(tower_kernel, out_shape=(jax.ShapeDtypeStruct(returned.sha...  8.14 us
    all_to_all x1, starting transfers between devices, on_device(): asked = lax.all_to_all(asks, ALL, split_axis=0, concat_axis=0, tiled=True)  8.01 us
    all_to_all x1, waiting for transfers between devices, on_device(): lax.all_to_all(looked.reshape(devices, capacity, width), ALL, split_axis=...  7.23 us
    all_to_all x1, waiting for transfers between devices, on_device(): lax.all_to_all(outgoing.reshape(devices, capacity, width), ALL, split_axi...  6.76 us
    all_to_all x1, starting transfers between devices, on_device(): lax.all_to_all(looked.reshape(devices, capacity, width), ALL, split_axis=...  6.16 us
  transfers between devices with their start and end apart: 41, of which 17 were waited for; matrix products, arithmetic and copies ran while one was open for 3% of the time, Pallas kernels for 18%

profile of v4, /device:TPU:2, one launch (start us, length us, event | category | flops | bytes accessed | tf_op | source)
XLA Modules:
  0.0 160.1 jit_solution(430260241502401762)
XLA Ops:
  0.6 2.5 %route.1 = (s32[128,16]{1,0:T(8,128)}, f32[128,128]{1,0:T(8,128)}, f32[128,128]{1,0:T(8,128)}, bf16[768,512]{1,0:T(8,128)(2,1)}, bf16[192,512]{1,0:T(8,128)(2,1)}) custom-call(s32[8,128]{1,0:T(8,128)} %bitcast.42, s32[8,128]{1,0:T(8,128)} %bitcast.43, s32[8,128]{1,0:T(8,128)} %bitcast.44, f32[512,256]{1,0:T(8,128)} %refs_2_, f32[512,512]{1,0:T(8,128)} %refs_0_), custom_call_target="tpu_custom_call" | custom-call | flops 2000000000 | bytes 6000000 | tf_op jit(solution)/shard_map/route/pallas_call | solution.py:110
  4.8 2.9 %collective-permute-start.1 = (bf16[192,512]{1,0:T(8,128)(2,1)}, bf16[192,512]{1,0:T(8,128)(2,1)S(1)}, u32[]{:S(2)}, u32[]{:S(2)}) collective-permute-start(bf16[192,512]{1,0:T(8,128)(2,1)} %get-tuple-element.61), channel_id=1, source_target_pairs={{64,0},{96,32},{0,64},{32,96},{65,1},{97,33},{1,65},{33,97},{66,2}... | collective-permute-start | bytes 589832 | tf_op jit(solution)/shard_map/ppermute | solution.py:657
  9.0 8.0 %all-to-all-start = ((s32[128,1,16]{2,1,0:T(1,128)}), s32[128,1,16]{2,1,0:T(1,128)S(1)}, u32[]{:S(2)}, u32[]{:S(2)}) async-start(s32[128,1,16]{2,1,0:T(1,128)} %bitcast.36), calls=%async_computation | async-start | bytes 131072 | tf_op jit(solution)/shard_map/all_to_all | solution.py:693
  19.4 3.5 %count.1.counts_hbm = bf16[128,4096]{1,0:T(8,128)(2,1)} custom-call(s32[128,8]{1,0:T(8,128)} %copy.25.ids_ref.refs_5_), custom_call_target="tpu_custom_call" | custom-call | flops 3000000000 | bytes 9000000 | tf_op jit(solution)/shard_map/count/pallas_call | solution.py:273
  31.0 3.2 %collective-permute-start.7 = (bf16[3,96,512]{2,1,0:T(8,128)(2,1)S(1)}, bf16[3,96,512]{2,1,0:T(8,128)(2,1)}, u32[]{:S(2)}, u32[]{:S(2)}) collective-permute-start(bf16[3,96,512]{2,1,0:T(8,128)(2,1)S(1)} %pad_maximum_fusion.1.refs_5_.refs_11_), channel_id=1, source_target_pairs={{8,0},{12,4},{0,8},{4,12},{9,1},{13,5},{1,9},{5,13},{10,2},{14,6},... | collective-permute-start | bytes 884744 | tf_op jit(solution)/shard_map/ppermute | solution.py:657
  35.5 4.4 %lookup.1 = bf16[2048,256]{1,0:T(8,128)(2,1)} custom-call(s32[128,16]{1,0:T(8,128)} %bitcast.34, bf16[2048,256]{1,0:T(8,128)(2,1)} %convert_element_type.3.table_hbm), custom_call_target="tpu_custom_call" | custom-call | flops 3000000000 | bytes 9000000 | tf_op jit(solution)/shard_map/lookup/pallas_call | solution.py:198
  39.9 6.2 %all-to-all-start.1 = ((bf16[128,16,256]{2,1,0:T(8,128)(2,1)}), bf16[128,16,256]{2,1,0:T(8,128)(2,1)}, u32[]{:S(2)}, u32[]{:S(2)}) async-start(bf16[128,16,256]{2,1,0:T(8,128)(2,1)} %bitcast.32), calls=%async_computation.1 | async-start | bytes 2097152 | tf_op jit(solution)/shard_map/all_to_all | solution.py:707
  53.9 3.5 %hot_pool.1.refs_0_ = bf16[128,256]{1,0:T(8,128)(2,1)} custom-call(bf16[128,4096]{1,0:T(8,128)(2,1)} %count.1.counts_hbm, bf16[768,512]{1,0:T(8,128)(2,1)} %get-tuple-element.62.refs_0_.refs_6_.half_hbm, bf16[3,96,512]{2,1,0:T(8,128)(2,1)} %copy-done.7, bf16[3,96,512]{2,1,0:T(8,128)(2,1)} %collective-permute-done.3.refs_2_.refs_8_, ...), custom_call_target="tpu_custom_call" | custom-call | flops 100000000 | bytes 300000 | tf_op jit(solution)/shard_map/hot_pool/pallas_call | solution.py:309
  57.4 7.2 %all-to-all-done.1 = bf16[128,16,256]{2,1,0:T(8,128)(2,1)} async-done(((bf16[128,16,256]{2,1,0:T(8,128)(2,1)}), bf16[128,16,256]{2,1,0:T(8,128)(2,1)}, u32[]{:S(2)}, u32[]{:S(2)}) %all-to-all-start.1) | async-done | bytes 1048608 | tf_op jit(solution)/shard_map/all_to_all | solution.py:707
  64.6 8.1 %tower.1 = (bf16[2048,256]{1,0:T(8,128)(2,1)}, bf16[128,896]{1,0:T(8,128)(2,1)}) custom-call(bf16[128,256]{1,0:T(8,128)(2,1)} %hot_pool.1.refs_0_, bf16[2048,256]{1,0:T(8,128)(2,1)} %bitcast.14.refs_1_, bf16[2048,128]{1,0:T(8,128)(2,1)} %spread.1.refs_2_, f32[1,4096]{1,0:T(1,128)} %pad_maximum_fusion.2.refs_3_, f32[128,1]{1,0:T(8,128)} %copy.26.refs_4_, ...), custom_call_target="tpu_custom_call" | custom-call | flops 6000000000 | bytes 18000000 | tf_op jit(solution)/shard_map/tower/pallas_call | solution.py:395
  76.2 10.3 %collective-permute-done.20.refs_3_ = bf16[128,896]{1,0:T(8,128)(2,1)} collective-permute-done((bf16[128,896]{1,0:T(8,128)(2,1)}, bf16[128,896]{1,0:T(8,128)(2,1)}, u32[]{:S(2)}, u32[]{:S(2)}) %collective-permute-start.20) | collective-permute-done | bytes 229408 | tf_op jit(solution)/shard_map/ppermute | solution.py:657
  87.1 5.7 %all-to-all-start.2 = ((bf16[128,16,256]{2,1,0:T(8,128)(2,1)}), bf16[128,16,256]{2,1,0:T(8,128)(2,1)S(1)}, u32[]{:S(2)}, u32[]{:S(2)}) async-start(bf16[128,16,256]{2,1,0:T(8,128)(2,1)} %bitcast.33), calls=%async_computation.2 | async-start | bytes 2097152 | tf_op jit(solution)/shard_map/all_to_all | solution.py:725
  94.6 5.2 %columns.2.refs_0_ = f32[512,768]{1,0:T(8,128)} custom-call(f32[1,512]{1,0:T(1,128)} %bitcast.39, bf16[768,512]{1,0:T(8,128)(2,1)} %get-tuple-element.62.refs_0_.refs_6_.half_hbm, bf16[128,896]{1,0:T(8,128)(2,1)} %get-tuple-element.76.refs_0_, bf16[128,896]{1,0:T(8,128)(2,1)} %collective-permute-done.21.refs_1_, ...), custom_call_target="tpu_custom_call" | custom-call | flops 200000000 | bytes 600000 | tf_op jit(solution)/shard_map/columns/pallas_call | solution.py:493
  99.8 5.1 %columns.3 = bf16[512,768]{1,0:T(8,128)(2,1)} custom-call(f32[1,512]{1,0:T(1,128)} %bitcast.40, bf16[768,512]{1,0:T(8,128)(2,1)} %get-tuple-element.62.refs_0_.refs_6_.half_hbm, f32[512,768]{1,0:T(8,128)} %columns.2.refs_0_, bf16[128,896]{1,0:T(8,128)(2,1)} %collective-permute-done.19.refs_1_, bf16[128,896]{1,0:T(8,128)(2,1)} %collective-permute-done.22.refs_2_, ...), custom_call_target="tpu_custom_call" | custom-call | flops 200000000 | bytes 600000 | tf_op jit(solution)/shard_map/columns/pallas_call | solution.py:493
  104.8 6.8 %all-to-all-done.2 = bf16[128,16,256]{2,1,0:T(8,128)(2,1)S(1)} async-done(((bf16[128,16,256]{2,1,0:T(8,128)(2,1)}), bf16[128,16,256]{2,1,0:T(8,128)(2,1)S(1)}, u32[]{:S(2)}, u32[]{:S(2)}) %all-to-all-start.2) | async-done | bytes 1048608 | tf_op jit(solution)/shard_map/all_to_all | solution.py:725
  111.6 5.3 %all-to-all-start.3 = ((bf16[16,32,768]{2,1,0:T(8,128)(2,1)}), bf16[16,32,768]{2,1,0:T(8,128)(2,1)}, u32[]{:S(2)}, u32[]{:S(2)}) async-start(bf16[16,32,768]{2,1,0:T(8,128)(2,1)} %bitcast.31), calls=%async_computation.3 | async-start | bytes 1572864 | tf_op jit(solution)/shard_map/all_to_all | solution.py:734
  118.6 5.4 %cold_update.1 = (f32[2048,256]{1,0:T(8,128)}, f32[2048,256]{1,0:T(8,128)}) custom-call(s32[1,2048]{1,0:T(1,128)S(1)} %reshape.50.asked_ref, bf16[2048,256]{1,0:T(8,128)(2,1)S(1)} %bitcast.30, f32[2048,256]{1,0:T(8,128)S(1)} %copy-done, f32[2048,256]{1,0:T(8,128)S(1)} %copy-done.1), custom_call_target="tpu_custom_call" | custom-call | flops 5000000000 | bytes 15000000 | tf_op jit(solution)/shard_map/cold_update/pallas_call | solution.py:639
  124.0 5.1 %all-to-all-done.3 = bf16[16,32,768]{2,1,0:T(8,128)(2,1)} async-done(((bf16[16,32,768]{2,1,0:T(8,128)(2,1)}), bf16[16,32,768]{2,1,0:T(8,128)(2,1)}, u32[]{:S(2)}, u32[]{:S(2)}) %all-to-all-start.3) | async-done | bytes 786464 | tf_op jit(solution)/shard_map/all_to_all | solution.py:734
  131.2 2.4 %collective-permute-start.26 = (f32[32,384]{1,0:T(8,128)S(1)}, f32[32,384]{1,0:T(8,128)S(1)}, u32[]{:S(2)}, u32[]{:S(2)}) collective-permute-start(f32[32,384]{1,0:T(8,128)S(1)} %get-tuple-element.86.refs_0_), channel_id=1, source_target_pairs={{8,0},{12,4},{0,8},{4,12},{9,1},{13,5},{1,9},{5,13},{10,2},{14,6},... | collective-permute-start | bytes 147464 | tf_op jit(solution)/shard_map/ppermute | solution.py:657
  136.5 2.5 %collective-permute-start.29 = (f32[32,384]{1,0:T(8,128)S(1)}, f32[32,384]{1,0:T(8,128)S(1)}, u32[]{:S(2)}, u32[]{:S(2)}) collective-permute-start(f32[32,384]{1,0:T(8,128)S(1)} %get-tuple-element.87.refs_4_), channel_id=1, source_target_pairs={{2,0},{3,1},{0,2},{1,3},{6,4},{7,5},{4,6},{5,7},{10,8},{11,9},{8,1... | collective-permute-start | bytes 147464 | tf_op jit(solution)/shard_map/ppermute | solution.py:657
  139.4 2.6 %collective-permute-done.29.refs_6_ = f32[32,384]{1,0:T(8,128)S(1)} collective-permute-done((f32[32,384]{1,0:T(8,128)S(1)}, f32[32,384]{1,0:T(8,128)S(1)}, u32[]{:S(2)}, u32[]{:S(2)}) %collective-permute-start.29) | collective-permute-done | bytes 49184 | tf_op jit(solution)/shard_map/ppermute | solution.py:657
  143.3 2.5 %collective-permute-start.32 = (f32[128,384]{1,0:T(8,128)S(1)}, f32[128,384]{1,0:T(8,128)S(1)}, u32[]{:S(2)}, u32[]{:S(2)}) collective-permute-start(f32[128,384]{1,0:T(8,128)S(1)} %get-tuple-element.90.l0), channel_id=1, source_target_pairs={{2,0},{3,1},{0,2},{1,3},{6,4},{7,5},{4,6},{5,7},{10,8},{11,9},{8,1... | collective-permute-start | bytes 589832 | tf_op jit(solution)/shard_map/ppermute | solution.py:657
  150.5 2.6 %collective-permute-start.34 = (f32[128,384]{1,0:T(8,128)S(1)}, f32[128,384]{1,0:T(8,128)S(1)}, u32[]{:S(2)}, u32[]{:S(2)}) collective-permute-start(f32[128,384]{1,0:T(8,128)S(1)} %get-tuple-element.91.r0), channel_id=1, source_target_pairs={{4,0},{8,4},{12,8},{0,12},{5,1},{9,5},{13,9},{1,13},{6,2},{10,6},{... | collective-permute-start | bytes 589832 | tf_op jit(solution)/shard_map/ppermute | solution.py:657
  153.4 3.7 %collective-permute-done.36.r3 = f32[128,384]{1,0:T(8,128)S(1)} collective-permute-done((f32[128,384]{1,0:T(8,128)S(1)}, f32[128,384]{1,0:T(8,128)S(1)}, u32[]{:S(2)}, u32[]{:S(2)}) %collective-permute-start.36) | collective-permute-done | bytes 196640 | tf_op jit(solution)/shard_map/ppermute | solution.py:657
  (134 shorter events, 44.5 us)
Async XLA Ops:
  3.1 14.6 %collective-permute-start.2 = (bf16[192,512]{1,0:T(8,128)(2,1)}, bf16[192,512]{1,0:T(8,128)(2,1)S(1)}, u32[]{:S(2)}, u32[]{:S(2)}) collective-permute-start(bf16[192,512]{1,0:T(8,128)(2,1)} %get-tuple-element.61), channel_id=1, source_target_pairs={{96,0},{0,32},{32,64},{64,96},{97,1},{1,33},{33,65},{65,97},{98,2}... | collective-permute-start | bytes 589832 | tf_op jit(solution)/shard_map/ppermute | solution.py:657
  4.8 13.0 %collective-permute-start.1 = (bf16[192,512]{1,0:T(8,128)(2,1)}, bf16[192,512]{1,0:T(8,128)(2,1)S(1)}, u32[]{:S(2)}, u32[]{:S(2)}) collective-permute-start(bf16[192,512]{1,0:T(8,128)(2,1)} %get-tuple-element.61), channel_id=1, source_target_pairs={{64,0},{96,32},{0,64},{32,96},{65,1},{97,33},{1,65},{33,97},{66,2}... | collective-permute-start | bytes 589832 | tf_op jit(solution)/shard_map/ppermute | solution.py:657
  7.7 10.2 %collective-permute-start = (bf16[192,512]{1,0:T(8,128)(2,1)}, bf16[192,512]{1,0:T(8,128)(2,1)S(1)}, u32[]{:S(2)}, u32[]{:S(2)}) collective-permute-start(bf16[192,512]{1,0:T(8,128)(2,1)} %get-tuple-element.61), channel_id=1, source_target_pairs={{32,0},{64,32},{96,64},{0,96},{33,1},{65,33},{97,65},{1,97},{34,2}... | collective-permute-start | bytes 589832 | tf_op jit(solution)/shard_map/ppermute | solution.py:657
  9.0 17.0 %all-to-all-start = ((s32[128,1,16]{2,1,0:T(1,128)}), s32[128,1,16]{2,1,0:T(1,128)S(1)}, u32[]{:S(2)}, u32[]{:S(2)}) async-start(s32[128,1,16]{2,1,0:T(1,128)} %bitcast.36), calls=%async_computation | async-start | bytes 131072 | tf_op jit(solution)/shard_map/all_to_all | solution.py:693
  17.9 16.3 %collective-permute-start.5 = (bf16[3,96,512]{2,1,0:T(8,128)(2,1)S(1)}, bf16[3,96,512]{2,1,0:T(8,128)(2,1)S(1)}, u32[]{:S(2)}, u32[]{:S(2)}) collective-permute-start(bf16[3,96,512]{2,1,0:T(8,128)(2,1)S(1)} %pad_maximum_fusion.refs_1_.refs_7_), channel_id=1, source_target_pairs={{3,0},{0,1},{1,2},{2,3},{7,4},{4,5},{5,6},{6,7},{11,8},{8,9},{9,10... | collective-permute-start | bytes 884744 | tf_op jit(solution)/shard_map/ppermute | solution.py:657
  26.1 20.8 %collective-permute-start.4 = (bf16[3,96,512]{2,1,0:T(8,128)(2,1)S(1)}, bf16[3,96,512]{2,1,0:T(8,128)(2,1)}, u32[]{:S(2)}, u32[]{:S(2)}) collective-permute-start(bf16[3,96,512]{2,1,0:T(8,128)(2,1)S(1)} %pad_maximum_fusion.refs_1_.refs_7_), channel_id=1, source_target_pairs={{2,0},{3,1},{0,2},{1,3},{6,4},{7,5},{4,6},{5,7},{10,8},{11,9},{8,1... | collective-permute-start | bytes 884744 | tf_op jit(solution)/shard_map/ppermute | solution.py:657
  27.7 19.2 %collective-permute-start.3 = (bf16[3,96,512]{2,1,0:T(8,128)(2,1)S(1)}, bf16[3,96,512]{2,1,0:T(8,128)(2,1)}, u32[]{:S(2)}, u32[]{:S(2)}) collective-permute-start(bf16[3,96,512]{2,1,0:T(8,128)(2,1)S(1)} %pad_maximum_fusion.refs_1_.refs_7_), channel_id=1, source_target_pairs={{1,0},{2,1},{3,2},{0,3},{5,4},{6,5},{7,6},{4,7},{9,8},{10,9},{11,1... | collective-permute-start | bytes 884744 | tf_op jit(solution)/shard_map/ppermute | solution.py:657
  29.3 17.5 %collective-permute-start.8 = (bf16[3,96,512]{2,1,0:T(8,128)(2,1)S(1)}, bf16[3,96,512]{2,1,0:T(8,128)(2,1)}, u32[]{:S(2)}, u32[]{:S(2)}) collective-permute-start(bf16[3,96,512]{2,1,0:T(8,128)(2,1)S(1)} %pad_maximum_fusion.1.refs_5_.refs_11_), channel_id=1, source_target_pairs={{12,0},{0,4},{4,8},{8,12},{13,1},{1,5},{5,9},{9,13},{14,2},{2,6},{... | collective-permute-start | bytes 884744 | tf_op jit(solution)/shard_map/ppermute | solution.py:657
  31.0 15.8 %collective-permute-start.7 = (bf16[3,96,512]{2,1,0:T(8,128)(2,1)S(1)}, bf16[3,96,512]{2,1,0:T(8,128)(2,1)}, u32[]{:S(2)}, u32[]{:S(2)}) collective-permute-start(bf16[3,96,512]{2,1,0:T(8,128)(2,1)S(1)} %pad_maximum_fusion.1.refs_5_.refs_11_), channel_id=1, source_target_pairs={{8,0},{12,4},{0,8},{4,12},{9,1},{13,5},{1,9},{5,13},{10,2},{14,6},... | collective-permute-start | bytes 884744 | tf_op jit(solution)/shard_map/ppermute | solution.py:657
  34.3 12.6 %collective-permute-start.6 = (bf16[3,96,512]{2,1,0:T(8,128)(2,1)S(1)}, bf16[3,96,512]{2,1,0:T(8,128)(2,1)}, u32[]{:S(2)}, u32[]{:S(2)}) collective-permute-start(bf16[3,96,512]{2,1,0:T(8,128)(2,1)S(1)} %pad_maximum_fusion.1.refs_5_.refs_11_), channel_id=1, source_target_pairs={{4,0},{8,4},{12,8},{0,12},{5,1},{9,5},{13,9},{1,13},{6,2},{10,6},{... | collective-permute-start | bytes 884744 | tf_op jit(solution)/shard_map/ppermute | solution.py:657
  39.9 24.7 %all-to-all-start.1 = ((bf16[128,16,256]{2,1,0:T(8,128)(2,1)}), bf16[128,16,256]{2,1,0:T(8,128)(2,1)}, u32[]{:S(2)}, u32[]{:S(2)}) async-start(bf16[128,16,256]{2,1,0:T(8,128)(2,1)} %bitcast.32), calls=%async_computation.1 | async-start | bytes 2097152 | tf_op jit(solution)/shard_map/all_to_all | solution.py:707
  72.8 13.7 %collective-permute-start.20 = (bf16[128,896]{1,0:T(8,128)(2,1)}, bf16[128,896]{1,0:T(8,128)(2,1)}, u32[]{:S(2)}, u32[]{:S(2)}) collective-permute-start(bf16[128,896]{1,0:T(8,128)(2,1)} %get-tuple-element.76.refs_0_), channel_id=1, source_target_pairs={{96,0},{0,32},{32,64},{64,96},{97,1},{1,33},{33,65},{65,97},{98,2}... | collective-permute-start | bytes 688136 | tf_op jit(solution)/shard_map/ppermute | solution.py:657
  73.4 13.1 %collective-permute-start.19 = (bf16[128,896]{1,0:T(8,128)(2,1)}, bf16[128,896]{1,0:T(8,128)(2,1)}, u32[]{:S(2)}, u32[]{:S(2)}) collective-permute-start(bf16[128,896]{1,0:T(8,128)(2,1)} %get-tuple-element.76.refs_0_), channel_id=1, source_target_pairs={{64,0},{96,32},{0,64},{32,96},{65,1},{97,33},{1,65},{33,97},{66,2}... | collective-permute-start | bytes 688136 | tf_op jit(solution)/shard_map/ppermute | solution.py:657
  75.3 11.8 %collective-permute-start.18 = (bf16[128,896]{1,0:T(8,128)(2,1)}, bf16[128,896]{1,0:T(8,128)(2,1)}, u32[]{:S(2)}, u32[]{:S(2)}) collective-permute-start(bf16[128,896]{1,0:T(8,128)(2,1)} %get-tuple-element.76.refs_0_), channel_id=1, source_target_pairs={{32,0},{64,32},{96,64},{0,96},{33,1},{65,33},{97,65},{1,97},{34,2}... | collective-permute-start | bytes 688136 | tf_op jit(solution)/shard_map/ppermute | solution.py:657
  87.1 24.5 %all-to-all-start.2 = ((bf16[128,16,256]{2,1,0:T(8,128)(2,1)}), bf16[128,16,256]{2,1,0:T(8,128)(2,1)S(1)}, u32[]{:S(2)}, u32[]{:S(2)}) async-start(bf16[128,16,256]{2,1,0:T(8,128)(2,1)} %bitcast.33), calls=%async_computation.2 | async-start | bytes 2097152 | tf_op jit(solution)/shard_map/all_to_all | solution.py:725
  111.6 17.5 %all-to-all-start.3 = ((bf16[16,32,768]{2,1,0:T(8,128)(2,1)}), bf16[16,32,768]{2,1,0:T(8,128)(2,1)}, u32[]{:S(2)}, u32[]{:S(2)}) async-start(bf16[16,32,768]{2,1,0:T(8,128)(2,1)} %bitcast.31), calls=%async_computation.3 | async-start | bytes 1572864 | tf_op jit(solution)/shard_map/all_to_all | solution.py:734
  130.4 8.6 %collective-permute-start.27 = (f32[32,384]{1,0:T(8,128)S(1)}, f32[32,384]{1,0:T(8,128)S(1)}, u32[]{:S(2)}, u32[]{:S(2)}) collective-permute-start(f32[32,384]{1,0:T(8,128)S(1)} %get-tuple-element.86.refs_0_), channel_id=1, source_target_pairs={{12,0},{0,4},{4,8},{8,12},{13,1},{1,5},{5,9},{9,13},{14,2},{2,6},{... | collective-permute-start | bytes 147464 | tf_op jit(solution)/shard_map/ppermute | solution.py:657
  131.2 8.2 %collective-permute-start.26 = (f32[32,384]{1,0:T(8,128)S(1)}, f32[32,384]{1,0:T(8,128)S(1)}, u32[]{:S(2)}, u32[]{:S(2)}) collective-permute-start(f32[32,384]{1,0:T(8,128)S(1)} %get-tuple-element.86.refs_0_), channel_id=1, source_target_pairs={{8,0},{12,4},{0,8},{4,12},{9,1},{13,5},{1,9},{5,13},{10,2},{14,6},... | collective-permute-start | bytes 147464 | tf_op jit(solution)/shard_map/ppermute | solution.py:657
  143.1 7.3 %collective-permute-start.33 = (f32[128,384]{1,0:T(8,128)S(1)}, f32[128,384]{1,0:T(8,128)S(1)}, u32[]{:S(2)}, u32[]{:S(2)}) collective-permute-start(f32[128,384]{1,0:T(8,128)S(1)} %get-tuple-element.90.l0), channel_id=1, source_target_pairs={{3,0},{0,1},{1,2},{2,3},{7,4},{4,5},{5,6},{6,7},{11,8},{8,9},{9,10... | collective-permute-start | bytes 589832 | tf_op jit(solution)/shard_map/ppermute | solution.py:657
  143.3 10.1 %collective-permute-start.32 = (f32[128,384]{1,0:T(8,128)S(1)}, f32[128,384]{1,0:T(8,128)S(1)}, u32[]{:S(2)}, u32[]{:S(2)}) collective-permute-start(f32[128,384]{1,0:T(8,128)S(1)} %get-tuple-element.90.l0), channel_id=1, source_target_pairs={{2,0},{3,1},{0,2},{1,3},{6,4},{7,5},{4,6},{5,7},{10,8},{11,9},{8,1... | collective-permute-start | bytes 589832 | tf_op jit(solution)/shard_map/ppermute | solution.py:657
  145.8 7.6 %collective-permute-start.31 = (f32[128,384]{1,0:T(8,128)S(1)}, f32[128,384]{1,0:T(8,128)S(1)}, u32[]{:S(2)}, u32[]{:S(2)}) collective-permute-start(f32[128,384]{1,0:T(8,128)S(1)} %get-tuple-element.90.l0), channel_id=1, source_target_pairs={{1,0},{2,1},{3,2},{0,3},{5,4},{6,5},{7,6},{4,7},{9,8},{10,9},{11,1... | collective-permute-start | bytes 589832 | tf_op jit(solution)/shard_map/ppermute | solution.py:657
  148.1 9.0 %collective-permute-start.36 = (f32[128,384]{1,0:T(8,128)S(1)}, f32[128,384]{1,0:T(8,128)S(1)}, u32[]{:S(2)}, u32[]{:S(2)}) collective-permute-start(f32[128,384]{1,0:T(8,128)S(1)} %get-tuple-element.91.r0), channel_id=1, source_target_pairs={{12,0},{0,4},{4,8},{8,12},{13,1},{1,5},{5,9},{9,13},{14,2},{2,6},{... | collective-permute-start | bytes 589832 | tf_op jit(solution)/shard_map/ppermute | solution.py:657
  148.4 8.7 %collective-permute-start.35 = (f32[128,384]{1,0:T(8,128)S(1)}, f32[128,384]{1,0:T(8,128)S(1)}, u32[]{:S(2)}, u32[]{:S(2)}) collective-permute-start(f32[128,384]{1,0:T(8,128)S(1)} %get-tuple-element.91.r0), channel_id=1, source_target_pairs={{8,0},{12,4},{0,8},{4,12},{9,1},{13,5},{1,9},{5,13},{10,2},{14,6},... | collective-permute-start | bytes 589832 | tf_op jit(solution)/shard_map/ppermute | solution.py:657
  150.5 7.5 %collective-permute-start.34 = (f32[128,384]{1,0:T(8,128)S(1)}, f32[128,384]{1,0:T(8,128)S(1)}, u32[]{:S(2)}, u32[]{:S(2)}) collective-permute-start(f32[128,384]{1,0:T(8,128)S(1)} %get-tuple-element.91.r0), channel_id=1, source_target_pairs={{4,0},{8,4},{12,8},{0,12},{5,1},{9,5},{13,9},{1,13},{6,2},{10,6},{... | collective-permute-start | bytes 589832 | tf_op jit(solution)/shard_map/ppermute | solution.py:657
  (41 other events, 310.2 us)

commit v5 on v4

--- a/solution.py
+++ b/solution.py
@@ -695,9 +695,7 @@
     quarters = tuple(along(quarter, "y", by) for by in (1, 2, 3))
     counts = count_of(hot_ids, hot_rows)
     cold_half = cold_table.astype(bf16)
-    asked, counts, cold_half, spread_mat = lax.optimization_barrier(
-        (asked, counts, cold_half, spread_mat)
-    )
+    asked, counts, cold_half = lax.optimization_barrier((asked, counts, cold_half))
     count = quarter.shape[0] // 2
     by_x = jnp.stack([value[:count] for value in quarters])
     by_z = jnp.stack([value[count:] for value in quarters])

time: 161 us -> 159 us (0.988)
    ppermute x24, starting transfers between devices: 39.1 us -> 37.1 us  [along(): return lax.ppermute(value, axis, [((i + by) % 4, i) for i in range(4)])]
    all_to_all x1, waiting for transfers between devices: 0.03 us -> 2.04 us  [on_device(): asked = lax.all_to_all(asks, ALL, split_axis=0, concat_axis=0, tiled=True)]
    ppermute x13, waiting for transfers between devices: 3.44 us -> 1.44 us  [swap(): return lax.ppermute(value, 'core', [(0, 1), (1, 0)])]
    unnamed x50 -> x38, local copies, waits for them, and re-layouts: 3.43 us -> 2.39 us
  transfers between devices with their start and end apart: 41 -> 41, of which waited for: 17 -> 16; matrix products, arithmetic and copies ran while one was open for 3% -> 3% of each run, Pallas kernels for 18% -> 18%
where the time goes in v5:
time: 159 us; the launch traced here: 158 us
  starting transfers between devices  65.8 us (41%)
  Pallas kernels  43.2 us (27%)
  waiting for transfers between devices  42.3 us (27%)
  local copies, waits for them, and re-layouts  3.95 us (2%)
  other arithmetic  1.76 us (1%)
    ppermute x24, starting transfers between devices, along(): return lax.ppermute(value, axis, [((i + by) % 4, i) for i in range(4)])  37.1 us
    ppermute x24, waiting for transfers between devices, along(): return lax.ppermute(value, axis, [((i + by) % 4, i) for i in range(4)])  20.2 us
    pallas_call x2, Pallas kernels, columns(): pl.pallas_call(functools.partial(columns_kernel, keys, last), out_shape=j...  10.2 us
    pallas_call x1, Pallas kernels, tower(): pl.pallas_call(tower_kernel, out_shape=(jax.ShapeDtypeStruct(returned.sha...  8.15 us
    all_to_all x1, starting transfers between devices, on_device(): asked = lax.all_to_all(asks, ALL, split_axis=0, concat_axis=0, tiled=True)  8.01 us
    all_to_all x1, waiting for transfers between devices, on_device(): lax.all_to_all(looked.reshape(devices, capacity, width), ALL, split_axis=...  6.8 us
    all_to_all x1, waiting for transfers between devices, on_device(): lax.all_to_all(outgoing.reshape(devices, capacity, width), ALL, split_axi...  6.76 us
    all_to_all x1, starting transfers between devices, on_device(): lax.all_to_all(looked.reshape(devices, capacity, width), ALL, split_axis=...  6.26 us
  transfers between devices with their start and end apart: 41, of which 16 were waited for; matrix products, arithmetic and copies ran while one was open for 3% of the time, Pallas kernels for 18%

profile of v5, /device:TPU:2, one launch (start us, length us, event | category | flops | bytes accessed | tf_op | source)
XLA Modules:
  0.0 158.2 jit_solution(10679723391774816708)
XLA Ops:
  0.6 2.5 %route.1 = (s32[128,16]{1,0:T(8,128)}, f32[128,128]{1,0:T(8,128)}, f32[128,128]{1,0:T(8,128)}, bf16[768,512]{1,0:T(8,128)(2,1)}, bf16[192,512]{1,0:T(8,128)(2,1)}) custom-call(s32[8,128]{1,0:T(8,128)} %bitcast.42, s32[8,128]{1,0:T(8,128)} %bitcast.43, s32[8,128]{1,0:T(8,128)} %bitcast.44, f32[512,256]{1,0:T(8,128)} %refs_2_, f32[512,512]{1,0:T(8,128)} %refs_0_), custom_call_target="tpu_custom_call" | custom-call | flops 2000000000 | bytes 6000000 | tf_op jit(solution)/shard_map/route/pallas_call | solution.py:110
  4.8 2.9 %collective-permute-start.1 = (bf16[192,512]{1,0:T(8,128)(2,1)}, bf16[192,512]{1,0:T(8,128)(2,1)S(1)}, u32[]{:S(2)}, u32[]{:S(2)}) collective-permute-start(bf16[192,512]{1,0:T(8,128)(2,1)} %get-tuple-element.58), channel_id=1, source_target_pairs={{64,0},{96,32},{0,64},{32,96},{65,1},{97,33},{1,65},{33,97},{66,2}... | collective-permute-start | bytes 589832 | tf_op jit(solution)/shard_map/ppermute | solution.py:657
  9.0 8.0 %all-to-all-start = ((s32[128,1,16]{2,1,0:T(1,128)}), s32[128,1,16]{2,1,0:T(1,128)S(1)}, u32[]{:S(2)}, u32[]{:S(2)}) async-start(s32[128,1,16]{2,1,0:T(1,128)} %bitcast.36), calls=%async_computation | async-start | bytes 131072 | tf_op jit(solution)/shard_map/all_to_all | solution.py:693
  19.5 3.5 %count.1.counts_hbm = bf16[128,4096]{1,0:T(8,128)(2,1)} custom-call(s32[128,8]{1,0:T(8,128)} %copy.25.ids_ref.refs_5_), custom_call_target="tpu_custom_call" | custom-call | flops 3000000000 | bytes 9000000 | tf_op jit(solution)/shard_map/count/pallas_call | solution.py:273
  29.0 3.2 %collective-permute-start.7 = (bf16[3,96,512]{2,1,0:T(8,128)(2,1)S(1)}, bf16[3,96,512]{2,1,0:T(8,128)(2,1)}, u32[]{:S(2)}, u32[]{:S(2)}) collective-permute-start(bf16[3,96,512]{2,1,0:T(8,128)(2,1)S(1)} %pad_maximum_fusion.1.refs_5_.refs_11_), channel_id=1, source_target_pairs={{8,0},{12,4},{0,8},{4,12},{9,1},{13,5},{1,9},{5,13},{10,2},{14,6},... | collective-permute-start | bytes 884744 | tf_op jit(solution)/shard_map/ppermute | solution.py:657
  33.4 4.4 %lookup.1 = bf16[2048,256]{1,0:T(8,128)(2,1)} custom-call(s32[128,16]{1,0:T(8,128)} %bitcast.34, bf16[2048,256]{1,0:T(8,128)(2,1)} %convert_element_type.3.table_hbm), custom_call_target="tpu_custom_call" | custom-call | flops 3000000000 | bytes 9000000 | tf_op jit(solution)/shard_map/lookup/pallas_call | solution.py:198
  37.9 6.3 %all-to-all-start.1 = ((bf16[128,16,256]{2,1,0:T(8,128)(2,1)}), bf16[128,16,256]{2,1,0:T(8,128)(2,1)}, u32[]{:S(2)}, u32[]{:S(2)}) async-start(bf16[128,16,256]{2,1,0:T(8,128)(2,1)} %bitcast.32), calls=%async_computation.1 | async-start | bytes 2097152 | tf_op jit(solution)/shard_map/all_to_all | solution.py:705
  52.4 3.4 %hot_pool.1.refs_0_ = bf16[128,256]{1,0:T(8,128)(2,1)} custom-call(bf16[128,4096]{1,0:T(8,128)(2,1)} %count.1.counts_hbm, bf16[768,512]{1,0:T(8,128)(2,1)} %get-tuple-element.59.refs_0_.refs_6_.half_hbm, bf16[3,96,512]{2,1,0:T(8,128)(2,1)} %copy-done.7, bf16[3,96,512]{2,1,0:T(8,128)(2,1)} %collective-permute-done.3.refs_2_.refs_8_, ...), custom_call_target="tpu_custom_call" | custom-call | flops 100000000 | bytes 300000 | tf_op jit(solution)/shard_map/hot_pool/pallas_call | solution.py:309
  55.8 6.8 %all-to-all-done.1 = bf16[128,16,256]{2,1,0:T(8,128)(2,1)} async-done(((bf16[128,16,256]{2,1,0:T(8,128)(2,1)}), bf16[128,16,256]{2,1,0:T(8,128)(2,1)}, u32[]{:S(2)}, u32[]{:S(2)}) %all-to-all-start.1) | async-done | bytes 1048608 | tf_op jit(solution)/shard_map/all_to_all | solution.py:705
  62.6 8.2 %tower.1 = (bf16[2048,256]{1,0:T(8,128)(2,1)}, bf16[128,896]{1,0:T(8,128)(2,1)}) custom-call(bf16[128,256]{1,0:T(8,128)(2,1)} %hot_pool.1.refs_0_, bf16[2048,256]{1,0:T(8,128)(2,1)} %bitcast.14.refs_1_, bf16[2048,128]{1,0:T(8,128)(2,1)} %spread.1.refs_2_, f32[1,4096]{1,0:T(1,128)} %pad_maximum_fusion.2.refs_3_, f32[128,1]{1,0:T(8,128)} %copy.26.refs_4_, ...), custom_call_target="tpu_custom_call" | custom-call | flops 6000000000 | bytes 18000000 | tf_op jit(solution)/shard_map/tower/pallas_call | solution.py:395
  74.2 10.3 %collective-permute-done.20.refs_3_ = bf16[128,896]{1,0:T(8,128)(2,1)} collective-permute-done((bf16[128,896]{1,0:T(8,128)(2,1)}, bf16[128,896]{1,0:T(8,128)(2,1)}, u32[]{:S(2)}, u32[]{:S(2)}) %collective-permute-start.20) | collective-permute-done | bytes 229408 | tf_op jit(solution)/shard_map/ppermute | solution.py:657
  85.2 5.7 %all-to-all-start.2 = ((bf16[128,16,256]{2,1,0:T(8,128)(2,1)}), bf16[128,16,256]{2,1,0:T(8,128)(2,1)S(1)}, u32[]{:S(2)}, u32[]{:S(2)}) async-start(bf16[128,16,256]{2,1,0:T(8,128)(2,1)} %bitcast.33), calls=%async_computation.2 | async-start | bytes 2097152 | tf_op jit(solution)/shard_map/all_to_all | solution.py:723
  92.6 5.2 %columns.2.refs_0_ = f32[512,768]{1,0:T(8,128)} custom-call(f32[1,512]{1,0:T(1,128)} %bitcast.39, bf16[768,512]{1,0:T(8,128)(2,1)} %get-tuple-element.59.refs_0_.refs_6_.half_hbm, bf16[128,896]{1,0:T(8,128)(2,1)} %get-tuple-element.74.refs_0_, bf16[128,896]{1,0:T(8,128)(2,1)} %collective-permute-done.21.refs_1_, ...), custom_call_target="tpu_custom_call" | custom-call | flops 200000000 | bytes 600000 | tf_op jit(solution)/shard_map/columns/pallas_call | solution.py:493
  97.8 5.1 %columns.3 = bf16[512,768]{1,0:T(8,128)(2,1)} custom-call(f32[1,512]{1,0:T(1,128)} %bitcast.40, bf16[768,512]{1,0:T(8,128)(2,1)} %get-tuple-element.59.refs_0_.refs_6_.half_hbm, f32[512,768]{1,0:T(8,128)} %columns.2.refs_0_, bf16[128,896]{1,0:T(8,128)(2,1)} %collective-permute-done.19.refs_1_, bf16[128,896]{1,0:T(8,128)(2,1)} %collective-permute-done.22.refs_2_, ...), custom_call_target="tpu_custom_call" | custom-call | flops 200000000 | bytes 600000 | tf_op jit(solution)/shard_map/columns/pallas_call | solution.py:493
  102.9 6.8 %all-to-all-done.2 = bf16[128,16,256]{2,1,0:T(8,128)(2,1)S(1)} async-done(((bf16[128,16,256]{2,1,0:T(8,128)(2,1)}), bf16[128,16,256]{2,1,0:T(8,128)(2,1)S(1)}, u32[]{:S(2)}, u32[]{:S(2)}) %all-to-all-start.2) | async-done | bytes 1048608 | tf_op jit(solution)/shard_map/all_to_all | solution.py:723
  109.6 5.4 %all-to-all-start.3 = ((bf16[16,32,768]{2,1,0:T(8,128)(2,1)}), bf16[16,32,768]{2,1,0:T(8,128)(2,1)}, u32[]{:S(2)}, u32[]{:S(2)}) async-start(bf16[16,32,768]{2,1,0:T(8,128)(2,1)} %bitcast.31), calls=%async_computation.3 | async-start | bytes 1572864 | tf_op jit(solution)/shard_map/all_to_all | solution.py:732
  116.7 5.4 %cold_update.1 = (f32[2048,256]{1,0:T(8,128)}, f32[2048,256]{1,0:T(8,128)}) custom-call(s32[1,2048]{1,0:T(1,128)S(1)} %reshape.50.asked_ref, bf16[2048,256]{1,0:T(8,128)(2,1)S(1)} %bitcast.30, f32[2048,256]{1,0:T(8,128)S(1)} %copy-done, f32[2048,256]{1,0:T(8,128)S(1)} %copy-done.1), custom_call_target="tpu_custom_call" | custom-call | flops 5000000000 | bytes 15000000 | tf_op jit(solution)/shard_map/cold_update/pallas_call | solution.py:639
  122.1 5.1 %all-to-all-done.3 = bf16[16,32,768]{2,1,0:T(8,128)(2,1)} async-done(((bf16[16,32,768]{2,1,0:T(8,128)(2,1)}), bf16[16,32,768]{2,1,0:T(8,128)(2,1)}, u32[]{:S(2)}, u32[]{:S(2)}) %all-to-all-start.3) | async-done | bytes 786464 | tf_op jit(solution)/shard_map/all_to_all | solution.py:732
  129.2 2.4 %collective-permute-start.26 = (f32[32,384]{1,0:T(8,128)S(1)}, f32[32,384]{1,0:T(8,128)S(1)}, u32[]{:S(2)}, u32[]{:S(2)}) collective-permute-start(f32[32,384]{1,0:T(8,128)S(1)} %get-tuple-element.84.refs_0_), channel_id=1, source_target_pairs={{8,0},{12,4},{0,8},{4,12},{9,1},{13,5},{1,9},{5,13},{10,2},{14,6},... | collective-permute-start | bytes 147464 | tf_op jit(solution)/shard_map/ppermute | solution.py:657
  134.5 2.5 %collective-permute-start.29 = (f32[32,384]{1,0:T(8,128)S(1)}, f32[32,384]{1,0:T(8,128)S(1)}, u32[]{:S(2)}, u32[]{:S(2)}) collective-permute-start(f32[32,384]{1,0:T(8,128)S(1)} %get-tuple-element.85.refs_4_), channel_id=1, source_target_pairs={{2,0},{3,1},{0,2},{1,3},{6,4},{7,5},{4,6},{5,7},{10,8},{11,9},{8,1... | collective-permute-start | bytes 147464 | tf_op jit(solution)/shard_map/ppermute | solution.py:657
  137.5 2.6 %collective-permute-done.29.refs_6_ = f32[32,384]{1,0:T(8,128)S(1)} collective-permute-done((f32[32,384]{1,0:T(8,128)S(1)}, f32[32,384]{1,0:T(8,128)S(1)}, u32[]{:S(2)}, u32[]{:S(2)}) %collective-permute-start.29) | collective-permute-done | bytes 49184 | tf_op jit(solution)/shard_map/ppermute | solution.py:657
  141.3 2.5 %collective-permute-start.32 = (f32[128,384]{1,0:T(8,128)S(1)}, f32[128,384]{1,0:T(8,128)S(1)}, u32[]{:S(2)}, u32[]{:S(2)}) collective-permute-start(f32[128,384]{1,0:T(8,128)S(1)} %get-tuple-element.88.l0), channel_id=1, source_target_pairs={{2,0},{3,1},{0,2},{1,3},{6,4},{7,5},{4,6},{5,7},{10,8},{11,9},{8,1... | collective-permute-start | bytes 589832 | tf_op jit(solution)/shard_map/ppermute | solution.py:657
  148.5 2.6 %collective-permute-start.34 = (f32[128,384]{1,0:T(8,128)S(1)}, f32[128,384]{1,0:T(8,128)S(1)}, u32[]{:S(2)}, u32[]{:S(2)}) collective-permute-start(f32[128,384]{1,0:T(8,128)S(1)} %get-tuple-element.89.r0), channel_id=1, source_target_pairs={{4,0},{8,4},{12,8},{0,12},{5,1},{9,5},{13,9},{1,13},{6,2},{10,6},{... | collective-permute-start | bytes 589832 | tf_op jit(solution)/shard_map/ppermute | solution.py:657
  151.4 3.7 %collective-permute-done.36.r3 = f32[128,384]{1,0:T(8,128)S(1)} collective-permute-done((f32[128,384]{1,0:T(8,128)S(1)}, f32[128,384]{1,0:T(8,128)S(1)}, u32[]{:S(2)}, u32[]{:S(2)}) %collective-permute-start.36) | collective-permute-done | bytes 196640 | tf_op jit(solution)/shard_map/ppermute | solution.py:657
  (122 shorter events, 42.8 us)
Async XLA Ops:
  3.1 14.6 %collective-permute-start.2 = (bf16[192,512]{1,0:T(8,128)(2,1)}, bf16[192,512]{1,0:T(8,128)(2,1)S(1)}, u32[]{:S(2)}, u32[]{:S(2)}) collective-permute-start(bf16[192,512]{1,0:T(8,128)(2,1)} %get-tuple-element.58), channel_id=1, source_target_pairs={{96,0},{0,32},{32,64},{64,96},{97,1},{1,33},{33,65},{65,97},{98,2}... | collective-permute-start | bytes 589832 | tf_op jit(solution)/shard_map/ppermute | solution.py:657
  4.8 13.0 %collective-permute-start.1 = (bf16[192,512]{1,0:T(8,128)(2,1)}, bf16[192,512]{1,0:T(8,128)(2,1)S(1)}, u32[]{:S(2)}, u32[]{:S(2)}) collective-permute-start(bf16[192,512]{1,0:T(8,128)(2,1)} %get-tuple-element.58), channel_id=1, source_target_pairs={{64,0},{96,32},{0,64},{32,96},{65,1},{97,33},{1,65},{33,97},{66,2}... | collective-permute-start | bytes 589832 | tf_op jit(solution)/shard_map/ppermute | solution.py:657
  7.7 10.2 %collective-permute-start = (bf16[192,512]{1,0:T(8,128)(2,1)}, bf16[192,512]{1,0:T(8,128)(2,1)S(1)}, u32[]{:S(2)}, u32[]{:S(2)}) collective-permute-start(bf16[192,512]{1,0:T(8,128)(2,1)} %get-tuple-element.58), channel_id=1, source_target_pairs={{32,0},{64,32},{96,64},{0,96},{33,1},{65,33},{97,65},{1,97},{34,2}... | collective-permute-start | bytes 589832 | tf_op jit(solution)/shard_map/ppermute | solution.py:657
  9.0 17.0 %all-to-all-start = ((s32[128,1,16]{2,1,0:T(1,128)}), s32[128,1,16]{2,1,0:T(1,128)S(1)}, u32[]{:S(2)}, u32[]{:S(2)}) async-start(s32[128,1,16]{2,1,0:T(1,128)} %bitcast.36), calls=%async_computation | async-start | bytes 131072 | tf_op jit(solution)/shard_map/all_to_all | solution.py:693
  17.9 14.3 %collective-permute-start.5 = (bf16[3,96,512]{2,1,0:T(8,128)(2,1)S(1)}, bf16[3,96,512]{2,1,0:T(8,128)(2,1)S(1)}, u32[]{:S(2)}, u32[]{:S(2)}) collective-permute-start(bf16[3,96,512]{2,1,0:T(8,128)(2,1)S(1)} %pad_maximum_fusion.refs_1_.refs_7_), channel_id=1, source_target_pairs={{3,0},{0,1},{1,2},{2,3},{7,4},{4,5},{5,6},{6,7},{11,8},{8,9},{9,10... | collective-permute-start | bytes 884744 | tf_op jit(solution)/shard_map/ppermute | solution.py:657
  26.1 18.1 %collective-permute-start.4 = (bf16[3,96,512]{2,1,0:T(8,128)(2,1)S(1)}, bf16[3,96,512]{2,1,0:T(8,128)(2,1)}, u32[]{:S(2)}, u32[]{:S(2)}) collective-permute-start(bf16[3,96,512]{2,1,0:T(8,128)(2,1)S(1)} %pad_maximum_fusion.refs_1_.refs_7_), channel_id=1, source_target_pairs={{2,0},{3,1},{0,2},{1,3},{6,4},{7,5},{4,6},{5,7},{10,8},{11,9},{8,1... | collective-permute-start | bytes 884744 | tf_op jit(solution)/shard_map/ppermute | solution.py:657
  27.5 16.7 %collective-permute-start.3 = (bf16[3,96,512]{2,1,0:T(8,128)(2,1)S(1)}, bf16[3,96,512]{2,1,0:T(8,128)(2,1)}, u32[]{:S(2)}, u32[]{:S(2)}) collective-permute-start(bf16[3,96,512]{2,1,0:T(8,128)(2,1)S(1)} %pad_maximum_fusion.refs_1_.refs_7_), channel_id=1, source_target_pairs={{1,0},{2,1},{3,2},{0,3},{5,4},{6,5},{7,6},{4,7},{9,8},{10,9},{11,1... | collective-permute-start | bytes 884744 | tf_op jit(solution)/shard_map/ppermute | solution.py:657
  28.5 15.7 %collective-permute-start.8 = (bf16[3,96,512]{2,1,0:T(8,128)(2,1)S(1)}, bf16[3,96,512]{2,1,0:T(8,128)(2,1)}, u32[]{:S(2)}, u32[]{:S(2)}) collective-permute-start(bf16[3,96,512]{2,1,0:T(8,128)(2,1)S(1)} %pad_maximum_fusion.1.refs_5_.refs_11_), channel_id=1, source_target_pairs={{12,0},{0,4},{4,8},{8,12},{13,1},{1,5},{5,9},{9,13},{14,2},{2,6},{... | collective-permute-start | bytes 884744 | tf_op jit(solution)/shard_map/ppermute | solution.py:657
  29.0 15.8 %collective-permute-start.7 = (bf16[3,96,512]{2,1,0:T(8,128)(2,1)S(1)}, bf16[3,96,512]{2,1,0:T(8,128)(2,1)}, u32[]{:S(2)}, u32[]{:S(2)}) collective-permute-start(bf16[3,96,512]{2,1,0:T(8,128)(2,1)S(1)} %pad_maximum_fusion.1.refs_5_.refs_11_), channel_id=1, source_target_pairs={{8,0},{12,4},{0,8},{4,12},{9,1},{13,5},{1,9},{5,13},{10,2},{14,6},... | collective-permute-start | bytes 884744 | tf_op jit(solution)/shard_map/ppermute | solution.py:657
  32.2 13.0 %collective-permute-start.6 = (bf16[3,96,512]{2,1,0:T(8,128)(2,1)S(1)}, bf16[3,96,512]{2,1,0:T(8,128)(2,1)}, u32[]{:S(2)}, u32[]{:S(2)}) collective-permute-start(bf16[3,96,512]{2,1,0:T(8,128)(2,1)S(1)} %pad_maximum_fusion.1.refs_5_.refs_11_), channel_id=1, source_target_pairs={{4,0},{8,4},{12,8},{0,12},{5,1},{9,5},{13,9},{1,13},{6,2},{10,6},{... | collective-permute-start | bytes 884744 | tf_op jit(solution)/shard_map/ppermute | solution.py:657
  37.9 24.7 %all-to-all-start.1 = ((bf16[128,16,256]{2,1,0:T(8,128)(2,1)}), bf16[128,16,256]{2,1,0:T(8,128)(2,1)}, u32[]{:S(2)}, u32[]{:S(2)}) async-start(bf16[128,16,256]{2,1,0:T(8,128)(2,1)} %bitcast.32), calls=%async_computation.1 | async-start | bytes 2097152 | tf_op jit(solution)/shard_map/all_to_all | solution.py:705
  70.8 13.7 %collective-permute-start.20 = (bf16[128,896]{1,0:T(8,128)(2,1)}, bf16[128,896]{1,0:T(8,128)(2,1)}, u32[]{:S(2)}, u32[]{:S(2)}) collective-permute-start(bf16[128,896]{1,0:T(8,128)(2,1)} %get-tuple-element.74.refs_0_), channel_id=1, source_target_pairs={{96,0},{0,32},{32,64},{64,96},{97,1},{1,33},{33,65},{65,97},{98,2}... | collective-permute-start | bytes 688136 | tf_op jit(solution)/shard_map/ppermute | solution.py:657
  71.4 13.1 %collective-permute-start.19 = (bf16[128,896]{1,0:T(8,128)(2,1)}, bf16[128,896]{1,0:T(8,128)(2,1)}, u32[]{:S(2)}, u32[]{:S(2)}) collective-permute-start(bf16[128,896]{1,0:T(8,128)(2,1)} %get-tuple-element.74.refs_0_), channel_id=1, source_target_pairs={{64,0},{96,32},{0,64},{32,96},{65,1},{97,33},{1,65},{33,97},{66,2}... | collective-permute-start | bytes 688136 | tf_op jit(solution)/shard_map/ppermute | solution.py:657
  73.4 11.8 %collective-permute-start.18 = (bf16[128,896]{1,0:T(8,128)(2,1)}, bf16[128,896]{1,0:T(8,128)(2,1)}, u32[]{:S(2)}, u32[]{:S(2)}) collective-permute-start(bf16[128,896]{1,0:T(8,128)(2,1)} %get-tuple-element.74.refs_0_), channel_id=1, source_target_pairs={{32,0},{64,32},{96,64},{0,96},{33,1},{65,33},{97,65},{1,97},{34,2}... | collective-permute-start | bytes 688136 | tf_op jit(solution)/shard_map/ppermute | solution.py:657
  85.2 24.5 %all-to-all-start.2 = ((bf16[128,16,256]{2,1,0:T(8,128)(2,1)}), bf16[128,16,256]{2,1,0:T(8,128)(2,1)S(1)}, u32[]{:S(2)}, u32[]{:S(2)}) async-start(bf16[128,16,256]{2,1,0:T(8,128)(2,1)} %bitcast.33), calls=%async_computation.2 | async-start | bytes 2097152 | tf_op jit(solution)/shard_map/all_to_all | solution.py:723
  109.6 17.5 %all-to-all-start.3 = ((bf16[16,32,768]{2,1,0:T(8,128)(2,1)}), bf16[16,32,768]{2,1,0:T(8,128)(2,1)}, u32[]{:S(2)}, u32[]{:S(2)}) async-start(bf16[16,32,768]{2,1,0:T(8,128)(2,1)} %bitcast.31), calls=%async_computation.3 | async-start | bytes 1572864 | tf_op jit(solution)/shard_map/all_to_all | solution.py:732
  128.4 8.6 %collective-permute-start.27 = (f32[32,384]{1,0:T(8,128)S(1)}, f32[32,384]{1,0:T(8,128)S(1)}, u32[]{:S(2)}, u32[]{:S(2)}) collective-permute-start(f32[32,384]{1,0:T(8,128)S(1)} %get-tuple-element.84.refs_0_), channel_id=1, source_target_pairs={{12,0},{0,4},{4,8},{8,12},{13,1},{1,5},{5,9},{9,13},{14,2},{2,6},{... | collective-permute-start | bytes 147464 | tf_op jit(solution)/shard_map/ppermute | solution.py:657
  129.2 8.2 %collective-permute-start.26 = (f32[32,384]{1,0:T(8,128)S(1)}, f32[32,384]{1,0:T(8,128)S(1)}, u32[]{:S(2)}, u32[]{:S(2)}) collective-permute-start(f32[32,384]{1,0:T(8,128)S(1)} %get-tuple-element.84.refs_0_), channel_id=1, source_target_pairs={{8,0},{12,4},{0,8},{4,12},{9,1},{13,5},{1,9},{5,13},{10,2},{14,6},... | collective-permute-start | bytes 147464 | tf_op jit(solution)/shard_map/ppermute | solution.py:657
  141.2 7.3 %collective-permute-start.33 = (f32[128,384]{1,0:T(8,128)S(1)}, f32[128,384]{1,0:T(8,128)S(1)}, u32[]{:S(2)}, u32[]{:S(2)}) collective-permute-start(f32[128,384]{1,0:T(8,128)S(1)} %get-tuple-element.88.l0), channel_id=1, source_target_pairs={{3,0},{0,1},{1,2},{2,3},{7,4},{4,5},{5,6},{6,7},{11,8},{8,9},{9,10... | collective-permute-start | bytes 589832 | tf_op jit(solution)/shard_map/ppermute | solution.py:657
  141.3 10.1 %collective-permute-start.32 = (f32[128,384]{1,0:T(8,128)S(1)}, f32[128,384]{1,0:T(8,128)S(1)}, u32[]{:S(2)}, u32[]{:S(2)}) collective-permute-start(f32[128,384]{1,0:T(8,128)S(1)} %get-tuple-element.88.l0), channel_id=1, source_target_pairs={{2,0},{3,1},{0,2},{1,3},{6,4},{7,5},{4,6},{5,7},{10,8},{11,9},{8,1... | collective-permute-start | bytes 589832 | tf_op jit(solution)/shard_map/ppermute | solution.py:657
  143.8 7.6 %collective-permute-start.31 = (f32[128,384]{1,0:T(8,128)S(1)}, f32[128,384]{1,0:T(8,128)S(1)}, u32[]{:S(2)}, u32[]{:S(2)}) collective-permute-start(f32[128,384]{1,0:T(8,128)S(1)} %get-tuple-element.88.l0), channel_id=1, source_target_pairs={{1,0},{2,1},{3,2},{0,3},{5,4},{6,5},{7,6},{4,7},{9,8},{10,9},{11,1... | collective-permute-start | bytes 589832 | tf_op jit(solution)/shard_map/ppermute | solution.py:657
  146.1 9.0 %collective-permute-start.36 = (f32[128,384]{1,0:T(8,128)S(1)}, f32[128,384]{1,0:T(8,128)S(1)}, u32[]{:S(2)}, u32[]{:S(2)}) collective-permute-start(f32[128,384]{1,0:T(8,128)S(1)} %get-tuple-element.89.r0), channel_id=1, source_target_pairs={{12,0},{0,4},{4,8},{8,12},{13,1},{1,5},{5,9},{9,13},{14,2},{2,6},{... | collective-permute-start | bytes 589832 | tf_op jit(solution)/shard_map/ppermute | solution.py:657
  146.4 8.7 %collective-permute-start.35 = (f32[128,384]{1,0:T(8,128)S(1)}, f32[128,384]{1,0:T(8,128)S(1)}, u32[]{:S(2)}, u32[]{:S(2)}) collective-permute-start(f32[128,384]{1,0:T(8,128)S(1)} %get-tuple-element.89.r0), channel_id=1, source_target_pairs={{8,0},{12,4},{0,8},{4,12},{9,1},{13,5},{1,9},{5,13},{10,2},{14,6},... | collective-permute-start | bytes 589832 | tf_op jit(solution)/shard_map/ppermute | solution.py:657
  148.5 7.5 %collective-permute-start.34 = (f32[128,384]{1,0:T(8,128)S(1)}, f32[128,384]{1,0:T(8,128)S(1)}, u32[]{:S(2)}, u32[]{:S(2)}) collective-permute-start(f32[128,384]{1,0:T(8,128)S(1)} %get-tuple-element.89.r0), channel_id=1, source_target_pairs={{4,0},{8,4},{12,8},{0,12},{5,1},{9,5},{13,9},{1,13},{6,2},{10,6},{... | collective-permute-start | bytes 589832 | tf_op jit(solution)/shard_map/ppermute | solution.py:657
  (35 other events, 302.7 us)

commit v6 on v5

--- a/solution.py
+++ b/solution.py
@@ -364,9 +364,14 @@
         )
     dhot = dfeat[:, :width]
     dcold = dfeat[:, width:].astype(bf16)
-    out_ref[...] = jnp.dot(spread_ref[...], dcold, preferred_element_type=f32).astype(bf16)
-    last = pltpu.make_async_copy(out_ref, out_hbm, two.at[6])
-    last.start()
+    stores = []
+    step = out_ref.shape[0] // 4
+    for n in range(4):
+        at = slice(n * step, (n + 1) * step)
+        out = jnp.dot(spread_ref[at, :], dcold, preferred_element_type=f32)
+        out_ref[at, :] = out.astype(bf16)
+        stores.append(pltpu.make_async_copy(out_ref.at[at], out_hbm.at[at], two.at[6 + n]))
+        stores[n].start(priority=n % 2)
     load_ref[:, :din] = feat
     load_ref[:, din : din + width] = dhot.astype(bf16)
     first = dlogit.astype(bf16).astype(f32)
@@ -385,7 +390,8 @@
         extra = jnp.where(lanes == 8 + k, high[:, k : k + 1], extra)
         extra = jnp.where(lanes == 8 + keys + k, low[:, k : k + 1], extra)
     load_ref[:, din + width :] = extra.astype(bf16)
-    last.wait()
+    for store in stores:
+        store.wait()
 
 
 def tower(hot, returned, spread_mat, head, label, ids, pieces):
@@ -408,7 +414,7 @@
         + [
             pltpu.VMEM((2, 4, 2 * width, hidden // 8), bf16),
             pltpu.VMEM(returned.shape, bf16),
-            pltpu.SemaphoreType.DMA((7,)),
+            pltpu.SemaphoreType.DMA((10,)),
             pltpu.SemaphoreType.DMA((COPIES,)),
         ],
         compiler_params=MOST,

time: 159 us -> 159 us (level)
  no operation moved by 1% of the time
where the time goes in v6:
time: 159 us; the launch traced here: 158 us
  starting transfers between devices  65.8 us (41%)
  Pallas kernels  43.1 us (27%)
  waiting for transfers between devices  42.3 us (27%)
  local copies, waits for them, and re-layouts  3.95 us (2%)
  other arithmetic  1.76 us (1%)
    ppermute x24, starting transfers between devices, along(): return lax.ppermute(value, axis, [((i + by) % 4, i) for i in range(4)])  37.1 us
    ppermute x24, waiting for transfers between devices, along(): return lax.ppermute(value, axis, [((i + by) % 4, i) for i in range(4)])  20.2 us
    pallas_call x2, Pallas kernels, columns(): pl.pallas_call(functools.partial(columns_kernel, keys, last), out_shape=j...  10.2 us
    pallas_call x1, Pallas kernels, tower(): pl.pallas_call(tower_kernel, out_shape=(jax.ShapeDtypeStruct(returned.sha...  8.04 us
    all_to_all x1, starting transfers between devices, on_device(): asked = lax.all_to_all(asks, ALL, split_axis=0, concat_axis=0, tiled=True)  8.01 us
    all_to_all x1, waiting for transfers between devices, on_device(): lax.all_to_all(looked.reshape(devices, capacity, width), ALL, split_axis=...  6.8 us
    all_to_all x1, waiting for transfers between devices, on_device(): lax.all_to_all(outgoing.reshape(devices, capacity, width), ALL, split_axi...  6.75 us
    all_to_all x1, starting transfers between devices, on_device(): lax.all_to_all(looked.reshape(devices, capacity, width), ALL, split_axis=...  6.26 us
  transfers between devices with their start and end apart: 41, of which 16 were waited for; matrix products, arithmetic and copies ran while one was open for 3% of the time, Pallas kernels for 18%

profile of v6, /device:TPU:2, one launch (start us, length us, event | category | flops | bytes accessed | tf_op | source)
XLA Modules:
  0.0 158.1 jit_solution(4587749506641105182)
XLA Ops:
  0.6 2.5 %route.1 = (s32[128,16]{1,0:T(8,128)}, f32[128,128]{1,0:T(8,128)}, f32[128,128]{1,0:T(8,128)}, bf16[768,512]{1,0:T(8,128)(2,1)}, bf16[192,512]{1,0:T(8,128)(2,1)}) custom-call(s32[8,128]{1,0:T(8,128)} %bitcast.42, s32[8,128]{1,0:T(8,128)} %bitcast.43, s32[8,128]{1,0:T(8,128)} %bitcast.44, f32[512,256]{1,0:T(8,128)} %refs_2_, f32[512,512]{1,0:T(8,128)} %refs_0_), custom_call_target="tpu_custom_call" | custom-call | flops 2000000000 | bytes 6000000 | tf_op jit(solution)/shard_map/route/pallas_call | solution.py:110
  4.8 2.9 %collective-permute-start.1 = (bf16[192,512]{1,0:T(8,128)(2,1)}, bf16[192,512]{1,0:T(8,128)(2,1)S(1)}, u32[]{:S(2)}, u32[]{:S(2)}) collective-permute-start(bf16[192,512]{1,0:T(8,128)(2,1)} %get-tuple-element.58), channel_id=1, source_target_pairs={{64,0},{96,32},{0,64},{32,96},{65,1},{97,33},{1,65},{33,97},{66,2}... | collective-permute-start | bytes 589832 | tf_op jit(solution)/shard_map/ppermute | solution.py:663
  9.0 8.0 %all-to-all-start = ((s32[128,1,16]{2,1,0:T(1,128)}), s32[128,1,16]{2,1,0:T(1,128)S(1)}, u32[]{:S(2)}, u32[]{:S(2)}) async-start(s32[128,1,16]{2,1,0:T(1,128)} %bitcast.36), calls=%async_computation | async-start | bytes 131072 | tf_op jit(solution)/shard_map/all_to_all | solution.py:699
  19.5 3.5 %count.1.counts_hbm = bf16[128,4096]{1,0:T(8,128)(2,1)} custom-call(s32[128,8]{1,0:T(8,128)} %copy.25.ids_ref.refs_5_), custom_call_target="tpu_custom_call" | custom-call | flops 3000000000 | bytes 9000000 | tf_op jit(solution)/shard_map/count/pallas_call | solution.py:273
  29.0 3.2 %collective-permute-start.7 = (bf16[3,96,512]{2,1,0:T(8,128)(2,1)S(1)}, bf16[3,96,512]{2,1,0:T(8,128)(2,1)}, u32[]{:S(2)}, u32[]{:S(2)}) collective-permute-start(bf16[3,96,512]{2,1,0:T(8,128)(2,1)S(1)} %pad_maximum_fusion.1.refs_5_.refs_11_), channel_id=1, source_target_pairs={{8,0},{12,4},{0,8},{4,12},{9,1},{13,5},{1,9},{5,13},{10,2},{14,6},... | collective-permute-start | bytes 884744 | tf_op jit(solution)/shard_map/ppermute | solution.py:663
  33.4 4.4 %lookup.1 = bf16[2048,256]{1,0:T(8,128)(2,1)} custom-call(s32[128,16]{1,0:T(8,128)} %bitcast.34, bf16[2048,256]{1,0:T(8,128)(2,1)} %convert_element_type.3.table_hbm), custom_call_target="tpu_custom_call" | custom-call | flops 3000000000 | bytes 9000000 | tf_op jit(solution)/shard_map/lookup/pallas_call | solution.py:198
  37.9 6.3 %all-to-all-start.1 = ((bf16[128,16,256]{2,1,0:T(8,128)(2,1)}), bf16[128,16,256]{2,1,0:T(8,128)(2,1)}, u32[]{:S(2)}, u32[]{:S(2)}) async-start(bf16[128,16,256]{2,1,0:T(8,128)(2,1)} %bitcast.32), calls=%async_computation.1 | async-start | bytes 2097152 | tf_op jit(solution)/shard_map/all_to_all | solution.py:711
  52.4 3.4 %hot_pool.1.refs_0_ = bf16[128,256]{1,0:T(8,128)(2,1)} custom-call(bf16[128,4096]{1,0:T(8,128)(2,1)} %count.1.counts_hbm, bf16[768,512]{1,0:T(8,128)(2,1)} %get-tuple-element.59.refs_0_.refs_6_.half_hbm, bf16[3,96,512]{2,1,0:T(8,128)(2,1)} %copy-done.7, bf16[3,96,512]{2,1,0:T(8,128)(2,1)} %collective-permute-done.3.refs_2_.refs_8_, ...), custom_call_target="tpu_custom_call" | custom-call | flops 100000000 | bytes 300000 | tf_op jit(solution)/shard_map/hot_pool/pallas_call | solution.py:309
  55.8 6.8 %all-to-all-done.1 = bf16[128,16,256]{2,1,0:T(8,128)(2,1)} async-done(((bf16[128,16,256]{2,1,0:T(8,128)(2,1)}), bf16[128,16,256]{2,1,0:T(8,128)(2,1)}, u32[]{:S(2)}, u32[]{:S(2)}) %all-to-all-start.1) | async-done | bytes 1048608 | tf_op jit(solution)/shard_map/all_to_all | solution.py:711
  62.6 8.0 %tower.1 = (bf16[2048,256]{1,0:T(8,128)(2,1)}, bf16[128,896]{1,0:T(8,128)(2,1)}) custom-call(bf16[128,256]{1,0:T(8,128)(2,1)} %hot_pool.1.refs_0_, bf16[2048,256]{1,0:T(8,128)(2,1)} %bitcast.14.refs_1_, bf16[2048,128]{1,0:T(8,128)(2,1)} %spread.1.refs_2_, f32[1,4096]{1,0:T(1,128)} %pad_maximum_fusion.2.refs_3_, f32[128,1]{1,0:T(8,128)} %copy.26.refs_4_, ...), custom_call_target="tpu_custom_call" | custom-call | flops 6000000000 | bytes 18000000 | tf_op jit(solution)/shard_map/tower/pallas_call | solution.py:401
  74.1 10.3 %collective-permute-done.20.refs_3_ = bf16[128,896]{1,0:T(8,128)(2,1)} collective-permute-done((bf16[128,896]{1,0:T(8,128)(2,1)}, bf16[128,896]{1,0:T(8,128)(2,1)}, u32[]{:S(2)}, u32[]{:S(2)}) %collective-permute-start.20) | collective-permute-done | bytes 229408 | tf_op jit(solution)/shard_map/ppermute | solution.py:663
  85.0 5.7 %all-to-all-start.2 = ((bf16[128,16,256]{2,1,0:T(8,128)(2,1)}), bf16[128,16,256]{2,1,0:T(8,128)(2,1)S(1)}, u32[]{:S(2)}, u32[]{:S(2)}) async-start(bf16[128,16,256]{2,1,0:T(8,128)(2,1)} %bitcast.33), calls=%async_computation.2 | async-start | bytes 2097152 | tf_op jit(solution)/shard_map/all_to_all | solution.py:729
  92.5 5.2 %columns.2.refs_0_ = f32[512,768]{1,0:T(8,128)} custom-call(f32[1,512]{1,0:T(1,128)} %bitcast.39, bf16[768,512]{1,0:T(8,128)(2,1)} %get-tuple-element.59.refs_0_.refs_6_.half_hbm, bf16[128,896]{1,0:T(8,128)(2,1)} %get-tuple-element.74.refs_0_, bf16[128,896]{1,0:T(8,128)(2,1)} %collective-permute-done.21.refs_1_, ...), custom_call_target="tpu_custom_call" | custom-call | flops 200000000 | bytes 600000 | tf_op jit(solution)/shard_map/columns/pallas_call | solution.py:499
  97.7 5.1 %columns.3 = bf16[512,768]{1,0:T(8,128)(2,1)} custom-call(f32[1,512]{1,0:T(1,128)} %bitcast.40, bf16[768,512]{1,0:T(8,128)(2,1)} %get-tuple-element.59.refs_0_.refs_6_.half_hbm, f32[512,768]{1,0:T(8,128)} %columns.2.refs_0_, bf16[128,896]{1,0:T(8,128)(2,1)} %collective-permute-done.19.refs_1_, bf16[128,896]{1,0:T(8,128)(2,1)} %collective-permute-done.22.refs_2_, ...), custom_call_target="tpu_custom_call" | custom-call | flops 200000000 | bytes 600000 | tf_op jit(solution)/shard_map/columns/pallas_call | solution.py:499
  102.8 6.8 %all-to-all-done.2 = bf16[128,16,256]{2,1,0:T(8,128)(2,1)S(1)} async-done(((bf16[128,16,256]{2,1,0:T(8,128)(2,1)}), bf16[128,16,256]{2,1,0:T(8,128)(2,1)S(1)}, u32[]{:S(2)}, u32[]{:S(2)}) %all-to-all-start.2) | async-done | bytes 1048608 | tf_op jit(solution)/shard_map/all_to_all | solution.py:729
  109.5 5.4 %all-to-all-start.3 = ((bf16[16,32,768]{2,1,0:T(8,128)(2,1)}), bf16[16,32,768]{2,1,0:T(8,128)(2,1)}, u32[]{:S(2)}, u32[]{:S(2)}) async-start(bf16[16,32,768]{2,1,0:T(8,128)(2,1)} %bitcast.31), calls=%async_computation.3 | async-start | bytes 1572864 | tf_op jit(solution)/shard_map/all_to_all | solution.py:738
  116.6 5.4 %cold_update.1 = (f32[2048,256]{1,0:T(8,128)}, f32[2048,256]{1,0:T(8,128)}) custom-call(s32[1,2048]{1,0:T(1,128)S(1)} %reshape.50.asked_ref, bf16[2048,256]{1,0:T(8,128)(2,1)S(1)} %bitcast.30, f32[2048,256]{1,0:T(8,128)S(1)} %copy-done, f32[2048,256]{1,0:T(8,128)S(1)} %copy-done.1), custom_call_target="tpu_custom_call" | custom-call | flops 5000000000 | bytes 15000000 | tf_op jit(solution)/shard_map/cold_update/pallas_call | solution.py:645
  122.0 5.1 %all-to-all-done.3 = bf16[16,32,768]{2,1,0:T(8,128)(2,1)} async-done(((bf16[16,32,768]{2,1,0:T(8,128)(2,1)}), bf16[16,32,768]{2,1,0:T(8,128)(2,1)}, u32[]{:S(2)}, u32[]{:S(2)}) %all-to-all-start.3) | async-done | bytes 786464 | tf_op jit(solution)/shard_map/all_to_all | solution.py:738
  129.1 2.4 %collective-permute-start.26 = (f32[32,384]{1,0:T(8,128)S(1)}, f32[32,384]{1,0:T(8,128)S(1)}, u32[]{:S(2)}, u32[]{:S(2)}) collective-permute-start(f32[32,384]{1,0:T(8,128)S(1)} %get-tuple-element.84.refs_0_), channel_id=1, source_target_pairs={{8,0},{12,4},{0,8},{4,12},{9,1},{13,5},{1,9},{5,13},{10,2},{14,6},... | collective-permute-start | bytes 147464 | tf_op jit(solution)/shard_map/ppermute | solution.py:663
  134.4 2.5 %collective-permute-start.29 = (f32[32,384]{1,0:T(8,128)S(1)}, f32[32,384]{1,0:T(8,128)S(1)}, u32[]{:S(2)}, u32[]{:S(2)}) collective-permute-start(f32[32,384]{1,0:T(8,128)S(1)} %get-tuple-element.85.refs_4_), channel_id=1, source_target_pairs={{2,0},{3,1},{0,2},{1,3},{6,4},{7,5},{4,6},{5,7},{10,8},{11,9},{8,1... | collective-permute-start | bytes 147464 | tf_op jit(solution)/shard_map/ppermute | solution.py:663
  137.4 2.6 %collective-permute-done.29.refs_6_ = f32[32,384]{1,0:T(8,128)S(1)} collective-permute-done((f32[32,384]{1,0:T(8,128)S(1)}, f32[32,384]{1,0:T(8,128)S(1)}, u32[]{:S(2)}, u32[]{:S(2)}) %collective-permute-start.29) | collective-permute-done | bytes 49184 | tf_op jit(solution)/shard_map/ppermute | solution.py:663
  141.2 2.5 %collective-permute-start.32 = (f32[128,384]{1,0:T(8,128)S(1)}, f32[128,384]{1,0:T(8,128)S(1)}, u32[]{:S(2)}, u32[]{:S(2)}) collective-permute-start(f32[128,384]{1,0:T(8,128)S(1)} %get-tuple-element.88.l0), channel_id=1, source_target_pairs={{2,0},{3,1},{0,2},{1,3},{6,4},{7,5},{4,6},{5,7},{10,8},{11,9},{8,1... | collective-permute-start | bytes 589832 | tf_op jit(solution)/shard_map/ppermute | solution.py:663
  148.4 2.6 %collective-permute-start.34 = (f32[128,384]{1,0:T(8,128)S(1)}, f32[128,384]{1,0:T(8,128)S(1)}, u32[]{:S(2)}, u32[]{:S(2)}) collective-permute-start(f32[128,384]{1,0:T(8,128)S(1)} %get-tuple-element.89.r0), channel_id=1, source_target_pairs={{4,0},{8,4},{12,8},{0,12},{5,1},{9,5},{13,9},{1,13},{6,2},{10,6},{... | collective-permute-start | bytes 589832 | tf_op jit(solution)/shard_map/ppermute | solution.py:663
  151.3 3.7 %collective-permute-done.36.r3 = f32[128,384]{1,0:T(8,128)S(1)} collective-permute-done((f32[128,384]{1,0:T(8,128)S(1)}, f32[128,384]{1,0:T(8,128)S(1)}, u32[]{:S(2)}, u32[]{:S(2)}) %collective-permute-start.36) | collective-permute-done | bytes 196640 | tf_op jit(solution)/shard_map/ppermute | solution.py:663
  (122 shorter events, 42.8 us)
Async XLA Ops:
  3.1 14.6 %collective-permute-start.2 = (bf16[192,512]{1,0:T(8,128)(2,1)}, bf16[192,512]{1,0:T(8,128)(2,1)S(1)}, u32[]{:S(2)}, u32[]{:S(2)}) collective-permute-start(bf16[192,512]{1,0:T(8,128)(2,1)} %get-tuple-element.58), channel_id=1, source_target_pairs={{96,0},{0,32},{32,64},{64,96},{97,1},{1,33},{33,65},{65,97},{98,2}... | collective-permute-start | bytes 589832 | tf_op jit(solution)/shard_map/ppermute | solution.py:663
  4.8 13.0 %collective-permute-start.1 = (bf16[192,512]{1,0:T(8,128)(2,1)}, bf16[192,512]{1,0:T(8,128)(2,1)S(1)}, u32[]{:S(2)}, u32[]{:S(2)}) collective-permute-start(bf16[192,512]{1,0:T(8,128)(2,1)} %get-tuple-element.58), channel_id=1, source_target_pairs={{64,0},{96,32},{0,64},{32,96},{65,1},{97,33},{1,65},{33,97},{66,2}... | collective-permute-start | bytes 589832 | tf_op jit(solution)/shard_map/ppermute | solution.py:663
  7.7 10.2 %collective-permute-start = (bf16[192,512]{1,0:T(8,128)(2,1)}, bf16[192,512]{1,0:T(8,128)(2,1)S(1)}, u32[]{:S(2)}, u32[]{:S(2)}) collective-permute-start(bf16[192,512]{1,0:T(8,128)(2,1)} %get-tuple-element.58), channel_id=1, source_target_pairs={{32,0},{64,32},{96,64},{0,96},{33,1},{65,33},{97,65},{1,97},{34,2}... | collective-permute-start | bytes 589832 | tf_op jit(solution)/shard_map/ppermute | solution.py:663
  9.0 17.0 %all-to-all-start = ((s32[128,1,16]{2,1,0:T(1,128)}), s32[128,1,16]{2,1,0:T(1,128)S(1)}, u32[]{:S(2)}, u32[]{:S(2)}) async-start(s32[128,1,16]{2,1,0:T(1,128)} %bitcast.36), calls=%async_computation | async-start | bytes 131072 | tf_op jit(solution)/shard_map/all_to_all | solution.py:699
  17.9 14.3 %collective-permute-start.5 = (bf16[3,96,512]{2,1,0:T(8,128)(2,1)S(1)}, bf16[3,96,512]{2,1,0:T(8,128)(2,1)S(1)}, u32[]{:S(2)}, u32[]{:S(2)}) collective-permute-start(bf16[3,96,512]{2,1,0:T(8,128)(2,1)S(1)} %pad_maximum_fusion.refs_1_.refs_7_), channel_id=1, source_target_pairs={{3,0},{0,1},{1,2},{2,3},{7,4},{4,5},{5,6},{6,7},{11,8},{8,9},{9,10... | collective-permute-start | bytes 884744 | tf_op jit(solution)/shard_map/ppermute | solution.py:663
  26.1 18.1 %collective-permute-start.4 = (bf16[3,96,512]{2,1,0:T(8,128)(2,1)S(1)}, bf16[3,96,512]{2,1,0:T(8,128)(2,1)}, u32[]{:S(2)}, u32[]{:S(2)}) collective-permute-start(bf16[3,96,512]{2,1,0:T(8,128)(2,1)S(1)} %pad_maximum_fusion.refs_1_.refs_7_), channel_id=1, source_target_pairs={{2,0},{3,1},{0,2},{1,3},{6,4},{7,5},{4,6},{5,7},{10,8},{11,9},{8,1... | collective-permute-start | bytes 884744 | tf_op jit(solution)/shard_map/ppermute | solution.py:663
  27.5 16.7 %collective-permute-start.3 = (bf16[3,96,512]{2,1,0:T(8,128)(2,1)S(1)}, bf16[3,96,512]{2,1,0:T(8,128)(2,1)}, u32[]{:S(2)}, u32[]{:S(2)}) collective-permute-start(bf16[3,96,512]{2,1,0:T(8,128)(2,1)S(1)} %pad_maximum_fusion.refs_1_.refs_7_), channel_id=1, source_target_pairs={{1,0},{2,1},{3,2},{0,3},{5,4},{6,5},{7,6},{4,7},{9,8},{10,9},{11,1... | collective-permute-start | bytes 884744 | tf_op jit(solution)/shard_map/ppermute | solution.py:663
  28.5 15.7 %collective-permute-start.8 = (bf16[3,96,512]{2,1,0:T(8,128)(2,1)S(1)}, bf16[3,96,512]{2,1,0:T(8,128)(2,1)}, u32[]{:S(2)}, u32[]{:S(2)}) collective-permute-start(bf16[3,96,512]{2,1,0:T(8,128)(2,1)S(1)} %pad_maximum_fusion.1.refs_5_.refs_11_), channel_id=1, source_target_pairs={{12,0},{0,4},{4,8},{8,12},{13,1},{1,5},{5,9},{9,13},{14,2},{2,6},{... | collective-permute-start | bytes 884744 | tf_op jit(solution)/shard_map/ppermute | solution.py:663
  29.0 15.8 %collective-permute-start.7 = (bf16[3,96,512]{2,1,0:T(8,128)(2,1)S(1)}, bf16[3,96,512]{2,1,0:T(8,128)(2,1)}, u32[]{:S(2)}, u32[]{:S(2)}) collective-permute-start(bf16[3,96,512]{2,1,0:T(8,128)(2,1)S(1)} %pad_maximum_fusion.1.refs_5_.refs_11_), channel_id=1, source_target_pairs={{8,0},{12,4},{0,8},{4,12},{9,1},{13,5},{1,9},{5,13},{10,2},{14,6},... | collective-permute-start | bytes 884744 | tf_op jit(solution)/shard_map/ppermute | solution.py:663
  32.2 13.0 %collective-permute-start.6 = (bf16[3,96,512]{2,1,0:T(8,128)(2,1)S(1)}, bf16[3,96,512]{2,1,0:T(8,128)(2,1)}, u32[]{:S(2)}, u32[]{:S(2)}) collective-permute-start(bf16[3,96,512]{2,1,0:T(8,128)(2,1)S(1)} %pad_maximum_fusion.1.refs_5_.refs_11_), channel_id=1, source_target_pairs={{4,0},{8,4},{12,8},{0,12},{5,1},{9,5},{13,9},{1,13},{6,2},{10,6},{... | collective-permute-start | bytes 884744 | tf_op jit(solution)/shard_map/ppermute | solution.py:663
  37.9 24.7 %all-to-all-start.1 = ((bf16[128,16,256]{2,1,0:T(8,128)(2,1)}), bf16[128,16,256]{2,1,0:T(8,128)(2,1)}, u32[]{:S(2)}, u32[]{:S(2)}) async-start(bf16[128,16,256]{2,1,0:T(8,128)(2,1)} %bitcast.32), calls=%async_computation.1 | async-start | bytes 2097152 | tf_op jit(solution)/shard_map/all_to_all | solution.py:711
  70.7 13.7 %collective-permute-start.20 = (bf16[128,896]{1,0:T(8,128)(2,1)}, bf16[128,896]{1,0:T(8,128)(2,1)}, u32[]{:S(2)}, u32[]{:S(2)}) collective-permute-start(bf16[128,896]{1,0:T(8,128)(2,1)} %get-tuple-element.74.refs_0_), channel_id=1, source_target_pairs={{96,0},{0,32},{32,64},{64,96},{97,1},{1,33},{33,65},{65,97},{98,2}... | collective-permute-start | bytes 688136 | tf_op jit(solution)/shard_map/ppermute | solution.py:663
  71.3 13.1 %collective-permute-start.19 = (bf16[128,896]{1,0:T(8,128)(2,1)}, bf16[128,896]{1,0:T(8,128)(2,1)}, u32[]{:S(2)}, u32[]{:S(2)}) collective-permute-start(bf16[128,896]{1,0:T(8,128)(2,1)} %get-tuple-element.74.refs_0_), channel_id=1, source_target_pairs={{64,0},{96,32},{0,64},{32,96},{65,1},{97,33},{1,65},{33,97},{66,2}... | collective-permute-start | bytes 688136 | tf_op jit(solution)/shard_map/ppermute | solution.py:663
  73.3 11.8 %collective-permute-start.18 = (bf16[128,896]{1,0:T(8,128)(2,1)}, bf16[128,896]{1,0:T(8,128)(2,1)}, u32[]{:S(2)}, u32[]{:S(2)}) collective-permute-start(bf16[128,896]{1,0:T(8,128)(2,1)} %get-tuple-element.74.refs_0_), channel_id=1, source_target_pairs={{32,0},{64,32},{96,64},{0,96},{33,1},{65,33},{97,65},{1,97},{34,2}... | collective-permute-start | bytes 688136 | tf_op jit(solution)/shard_map/ppermute | solution.py:663
  85.0 24.5 %all-to-all-start.2 = ((bf16[128,16,256]{2,1,0:T(8,128)(2,1)}), bf16[128,16,256]{2,1,0:T(8,128)(2,1)S(1)}, u32[]{:S(2)}, u32[]{:S(2)}) async-start(bf16[128,16,256]{2,1,0:T(8,128)(2,1)} %bitcast.33), calls=%async_computation.2 | async-start | bytes 2097152 | tf_op jit(solution)/shard_map/all_to_all | solution.py:729
  109.5 17.5 %all-to-all-start.3 = ((bf16[16,32,768]{2,1,0:T(8,128)(2,1)}), bf16[16,32,768]{2,1,0:T(8,128)(2,1)}, u32[]{:S(2)}, u32[]{:S(2)}) async-start(bf16[16,32,768]{2,1,0:T(8,128)(2,1)} %bitcast.31), calls=%async_computation.3 | async-start | bytes 1572864 | tf_op jit(solution)/shard_map/all_to_all | solution.py:738
  128.3 8.6 %collective-permute-start.27 = (f32[32,384]{1,0:T(8,128)S(1)}, f32[32,384]{1,0:T(8,128)S(1)}, u32[]{:S(2)}, u32[]{:S(2)}) collective-permute-start(f32[32,384]{1,0:T(8,128)S(1)} %get-tuple-element.84.refs_0_), channel_id=1, source_target_pairs={{12,0},{0,4},{4,8},{8,12},{13,1},{1,5},{5,9},{9,13},{14,2},{2,6},{... | collective-permute-start | bytes 147464 | tf_op jit(solution)/shard_map/ppermute | solution.py:663
  129.1 8.2 %collective-permute-start.26 = (f32[32,384]{1,0:T(8,128)S(1)}, f32[32,384]{1,0:T(8,128)S(1)}, u32[]{:S(2)}, u32[]{:S(2)}) collective-permute-start(f32[32,384]{1,0:T(8,128)S(1)} %get-tuple-element.84.refs_0_), channel_id=1, source_target_pairs={{8,0},{12,4},{0,8},{4,12},{9,1},{13,5},{1,9},{5,13},{10,2},{14,6},... | collective-permute-start | bytes 147464 | tf_op jit(solution)/shard_map/ppermute | solution.py:663
  141.0 7.3 %collective-permute-start.33 = (f32[128,384]{1,0:T(8,128)S(1)}, f32[128,384]{1,0:T(8,128)S(1)}, u32[]{:S(2)}, u32[]{:S(2)}) collective-permute-start(f32[128,384]{1,0:T(8,128)S(1)} %get-tuple-element.88.l0), channel_id=1, source_target_pairs={{3,0},{0,1},{1,2},{2,3},{7,4},{4,5},{5,6},{6,7},{11,8},{8,9},{9,10... | collective-permute-start | bytes 589832 | tf_op jit(solution)/shard_map/ppermute | solution.py:663
  141.2 10.1 %collective-permute-start.32 = (f32[128,384]{1,0:T(8,128)S(1)}, f32[128,384]{1,0:T(8,128)S(1)}, u32[]{:S(2)}, u32[]{:S(2)}) collective-permute-start(f32[128,384]{1,0:T(8,128)S(1)} %get-tuple-element.88.l0), channel_id=1, source_target_pairs={{2,0},{3,1},{0,2},{1,3},{6,4},{7,5},{4,6},{5,7},{10,8},{11,9},{8,1... | collective-permute-start | bytes 589832 | tf_op jit(solution)/shard_map/ppermute | solution.py:663
  143.7 7.6 %collective-permute-start.31 = (f32[128,384]{1,0:T(8,128)S(1)}, f32[128,384]{1,0:T(8,128)S(1)}, u32[]{:S(2)}, u32[]{:S(2)}) collective-permute-start(f32[128,384]{1,0:T(8,128)S(1)} %get-tuple-element.88.l0), channel_id=1, source_target_pairs={{1,0},{2,1},{3,2},{0,3},{5,4},{6,5},{7,6},{4,7},{9,8},{10,9},{11,1... | collective-permute-start | bytes 589832 | tf_op jit(solution)/shard_map/ppermute | solution.py:663
  146.0 9.0 %collective-permute-start.36 = (f32[128,384]{1,0:T(8,128)S(1)}, f32[128,384]{1,0:T(8,128)S(1)}, u32[]{:S(2)}, u32[]{:S(2)}) collective-permute-start(f32[128,384]{1,0:T(8,128)S(1)} %get-tuple-element.89.r0), channel_id=1, source_target_pairs={{12,0},{0,4},{4,8},{8,12},{13,1},{1,5},{5,9},{9,13},{14,2},{2,6},{... | collective-permute-start | bytes 589832 | tf_op jit(solution)/shard_map/ppermute | solution.py:663
  146.3 8.7 %collective-permute-start.35 = (f32[128,384]{1,0:T(8,128)S(1)}, f32[128,384]{1,0:T(8,128)S(1)}, u32[]{:S(2)}, u32[]{:S(2)}) collective-permute-start(f32[128,384]{1,0:T(8,128)S(1)} %get-tuple-element.89.r0), channel_id=1, source_target_pairs={{8,0},{12,4},{0,8},{4,12},{9,1},{13,5},{1,9},{5,13},{10,2},{14,6},... | collective-permute-start | bytes 589832 | tf_op jit(solution)/shard_map/ppermute | solution.py:663
  148.4 7.5 %collective-permute-start.34 = (f32[128,384]{1,0:T(8,128)S(1)}, f32[128,384]{1,0:T(8,128)S(1)}, u32[]{:S(2)}, u32[]{:S(2)}) collective-permute-start(f32[128,384]{1,0:T(8,128)S(1)} %get-tuple-element.89.r0), channel_id=1, source_target_pairs={{4,0},{8,4},{12,8},{0,12},{5,1},{9,5},{13,9},{1,13},{6,2},{10,6},{... | collective-permute-start | bytes 589832 | tf_op jit(solution)/shard_map/ppermute | solution.py:663
  (35 other events, 302.7 us)
